TPU v7x, 32 devices: a whole 2x2x4 slice. The times are simulated.
32 devices in a mesh: dp: 16 (over z, y, x), tensor: 2 (over core).
Axes of the slice: x: 2, y: 2, z: 4, core: 2. Of those that a mesh axis runs over, the one named last changes fastest.
Arguments:
- inputs: bfloat16 [40960, 512], P(('dp', 'tensor')), may hold values from -6 to 6
- cotangent: bfloat16 [40960, 512], P(('dp', 'tensor')), may hold values from -6 to 6
- timesteps: int32 [160], P('dp'), may hold values from 0 to 999
- item_scale: float32 [160], P('dp'), may hold values from 0.5 to 2
- qkv_weight: float32 [2, 512, 3, 512], P(None, 'dp', None, 'tensor'), may hold values from -0.25 to 0.25
- qkv_first: float32 [2, 512, 3, 512], P(None, 'dp', None, 'tensor'), may hold values from -256 to 256
- qkv_second: float32 [2, 512, 3, 512], P(None, 'dp', None, 'tensor'), may hold values from 819.2 to 13107.2
- out_weight: float32 [2, 512, 512], P(None, 'tensor', 'dp'), may hold values from -1 to 1
- out_first: float32 [2, 512, 512], P(None, 'tensor', 'dp'), may hold values from -256 to 256
- out_second: float32 [2, 512, 512], P(None, 'tensor', 'dp'), may hold values from 819.2 to 13107.2
- up_weight: float32 [2, 512, 2048], P(None, 'dp', 'tensor'), may hold values from -0.25 to 0.25
- up_first: float32 [2, 512, 2048], P(None, 'dp', 'tensor'), may hold values from -384 to 384
- up_second: float32 [2, 512, 2048], P(None, 'dp', 'tensor'), may hold values from 1843.2 to 29491.2
- up_bias: float32 [2, 16, 128], P(None, 'tensor', 'dp'), may hold values from -3 to 3
- bias_first: float32 [2, 16, 128], P(None, 'tensor', 'dp'), may hold values from -384 to 384
- bias_second: float32 [2, 16, 128], P(None, 'tensor', 'dp'), may hold values from 1843.2 to 29491.2
- down_weight: float32 [2, 2048, 512], P(None, 'tensor', 'dp'), may hold values from -0.125 to 0.125
- down_first: float32 [2, 2048, 512], P(None, 'tensor', 'dp'), may hold values from -512 to 512
- down_second: float32 [2, 2048, 512], P(None, 'tensor', 'dp'), may hold values from 3276.8 to 52428.8
- norm_params: float32 [2, 5, 512], P(None, None, ('dp', 'tensor')), may hold values from -1.2 to 1.4, as said below
- norm_first: float32 [2, 5, 512], P(None, None, ('dp', 'tensor')), may hold values from -1280 to 1280
- norm_second: float32 [2, 5, 512], P(None, None, ('dp', 'tensor')), may hold values from 20480 to 327680
- time_weight: float32 [2, 512, 512], P(None, ('dp', 'tensor')), may hold values from -0.25 to 0.25
- time_first: float32 [2, 512, 512], P(None, ('dp', 'tensor')), may hold values from -896 to 896
- time_second: float32 [2, 512, 512], P(None, ('dp', 'tensor')), may hold values from 10035.2 to 160563.2
Outputs:
- activations: bfloat16 [40960, 512], P(('dp', 'tensor'))
- input_grad: bfloat16 [40960, 512], P(('dp', 'tensor'))
- new_qkv_weight: float32 [2, 512, 3, 512], P(None, 'dp', None, 'tensor')
- new_qkv_first: float32 [2, 512, 3, 512], P(None, 'dp', None, 'tensor')
- new_qkv_second: float32 [2, 512, 2, 512], P(None, 'dp', None, 'tensor')
- new_value_second: float32 [2, 512, 512], P(None, 'dp', 'tensor')
- new_out_weight: float32 [2, 512, 512], P(None, 'tensor', 'dp')
- new_out_first: float32 [2, 512, 512], P(None, 'tensor', 'dp')
- new_out_second: float32 [2, 512, 512], P(None, 'tensor', 'dp')
- new_up_weight: float32 [2, 512, 2048], P(None, 'dp', 'tensor')
- new_up_first: float32 [2, 512, 2048], P(None, 'dp', 'tensor')
- new_up_second: float32 [2, 512, 2048], P(None, 'dp', 'tensor')
- new_up_bias: float32 [2, 16, 128], P(None, 'tensor', 'dp')
- new_bias_first: float32 [2, 16, 128], P(None, 'tensor', 'dp')
- new_bias_second: float32 [2, 16, 128], P(None, 'tensor', 'dp')
- new_down_weight: float32 [2, 2048, 512], P(None, 'tensor', 'dp')
- new_down_first: float32 [2, 2048, 512], P(None, 'tensor', 'dp')
- new_down_second: float32 [2, 2048, 512], P(None, 'tensor', 'dp')
- new_norm_params: float32 [2, 5, 512], P(None, None, ('dp', 'tensor'))
- new_norm_first: float32 [2, 5, 512], P(None, None, ('dp', 'tensor'))
- new_norm_second: float32 [2, 5, 512], P(None, None, ('dp', 'tensor'))
- new_time_weight: float32 [2, 512, 512], P(None, ('dp', 'tensor'))
- new_time_first: float32 [2, 512, 512], P(None, ('dp', 'tensor'))
- new_time_second: float32 [2, 512, 512], P(None, ('dp', 'tensor'))
Inputs may be any that keep to these rules, and one draw needn't show every extreme that they name: `norm_params`: rows 0 and 2 of each layer are gains, rows 1, 3 and 4 shifts and a bias.
All inputs are finite; a program needn't handle non-finite values.
Results may differ from a plain program's by a relative error of at most 0.018.
Values may be sent and summed in bfloat16 or wider, within the bound.
A program may use at most 256 MiB of HBM per device.

v0:
```python
import math

import jax
import jax.numpy as jnp
from jax import lax
from jax.sharding import PartitionSpec as P

HEAD_DIM = 64
TE = 512
LENGTH = 256
LAYERS = 2
STEP = 8
BIAS_ROW = 128


highest = lax.Precision.HIGHEST
beta_first = 0.5
beta_second = 0.5
learn_rate = 0.1
norm_rate = 0.4
weight_decay = 0.01
adam_eps = 1e-08
norm_eps = 1e-05


def layer_norm(values, gain, shift):
    center = values - jnp.mean(values, -1, keepdims=True)
    spread = jnp.mean(center * center, -1, keepdims=True)
    return center * lax.rsqrt(spread + norm_eps) * gain + shift


def time_features(steps_in):
    half_width = TE // 2
    frequency = jnp.exp(
        -math.log(10000.0) / half_width * jnp.arange(half_width).astype(jnp.float32)
    )
    angles = steps_in.astype(jnp.float32)[:, None] * frequency[None, :]
    return jnp.concatenate([jnp.sin(angles), jnp.cos(angles)], 1)


def gelu_exact(values):
    return jax.nn.gelu(values, approximate=False)


def adamw(weight, gradient, first_moment, second_moment, rate):
    first_new = beta_first * first_moment + (1.0 - beta_first) * gradient
    second_new = beta_second * second_moment + (1.0 - beta_second) * gradient * gradient
    first_corr = first_new / (1.0 - beta_first**STEP)
    second_corr = second_new / (1.0 - beta_second**STEP)
    weight_new = weight - rate * (
        first_corr / (jnp.sqrt(second_corr) + adam_eps) + weight_decay * weight
    )
    return (weight_new, first_new, second_new)


def own_slice(whole, master, dim):
    count = master.shape[dim]
    return lax.dynamic_slice_in_dim(whole, lax.axis_index("dp") * count, count, dim)


def attend(query_mat, key_mat, value_mat):
    score_scale = HEAD_DIM ** (-0.5)
    scores = (
        jnp.einsum("snhd,smhd->shnm", query_mat, key_mat, preferred_element_type=jnp.float32)
        * score_scale
    )
    row_max = jnp.max(scores, -1, keepdims=True)
    exponent = jnp.exp(scores - row_max)
    row_total = jnp.sum(exponent, -1, keepdims=True)
    attn_probs = (exponent / row_total).astype(jnp.bfloat16)
    mixed = jnp.einsum("shnm,smhd->snhd", attn_probs, value_mat, preferred_element_type=jnp.float32)
    return (mixed.astype(jnp.bfloat16), row_max + jnp.log(row_total))


def attend_back(query_mat, key_mat, value_mat, log_total, grad_mixed):
    score_scale = HEAD_DIM ** (-0.5)
    scores = (
        jnp.einsum("snhd,smhd->shnm", query_mat, key_mat, preferred_element_type=jnp.float32)
        * score_scale
    )
    attn_probs = jnp.exp(scores - log_total)
    grad_probs = jnp.einsum(
        "snhd,smhd->shnm", grad_mixed, value_mat, preferred_element_type=jnp.float32
    )
    inner_sum = jnp.sum(grad_probs * attn_probs, -1, keepdims=True)
    grad_scores = (attn_probs * (grad_probs - inner_sum)).astype(jnp.bfloat16)
    grad_query = (
        jnp.einsum("shnm,smhd->snhd", grad_scores, key_mat, preferred_element_type=jnp.float32)
        * score_scale
    )
    grad_key = (
        jnp.einsum("shnm,snhd->smhd", grad_scores, query_mat, preferred_element_type=jnp.float32)
        * score_scale
    )
    grad_value = jnp.einsum(
        "shnm,snhd->smhd",
        attn_probs.astype(jnp.bfloat16),
        grad_mixed,
        preferred_element_type=jnp.float32,
    )
    return (
        grad_query.astype(jnp.bfloat16),
        grad_key.astype(jnp.bfloat16),
        grad_value.astype(jnp.bfloat16),
    )


def per_device(
    inputs,
    cotangent,
    timesteps,
    item_scale,
    qkv_weight,
    qkv_first,
    qkv_second,
    out_weight,
    out_first,
    out_second,
    up_weight,
    up_first,
    up_second,
    up_bias,
    bias_first,
    bias_second,
    down_weight,
    down_first,
    down_second,
    norm_params,
    norm_first,
    norm_second,
    time_weight,
    time_first,
    time_second,
):
    qkv_full, out_full, up_full, bias_full, down_full = (
        lax.all_gather(qkv_weight.astype(jnp.bfloat16), "dp", axis=1, tiled=True),
        lax.all_gather(out_weight.astype(jnp.bfloat16), "dp", axis=2, tiled=True),
        lax.all_gather(up_weight.astype(jnp.bfloat16), "dp", axis=1, tiled=True),
        lax.all_gather(up_bias.astype(jnp.bfloat16), "dp", axis=2, tiled=True),
        lax.all_gather(down_weight.astype(jnp.bfloat16), "dp", axis=2, tiled=True),
    )
    norm_full, time_full = (
        lax.all_gather(norm_params, ("dp", "tensor"), axis=2, tiled=True),
        lax.all_gather(time_weight, ("dp", "tensor"), axis=1, tiled=True),
    )
    model_width = inputs.shape[1]
    shard_rows = inputs.shape[0]
    local_items = shard_rows // LENGTH
    first_item = lax.axis_index("tensor") * local_items
    my_steps = lax.dynamic_slice_in_dim(timesteps, first_item, local_items)
    my_scale = lax.dynamic_slice_in_dim(item_scale, first_item, local_items)
    time_feats = time_features(my_steps)
    stream = inputs.astype(jnp.float32)
    kept_layers = []
    for layer_index in range(LAYERS):
        shift_rows = jnp.dot(
            time_feats,
            time_full[layer_index],
            precision=highest,
            preferred_element_type=jnp.float32,
        )
        stream = (
            stream.reshape(local_items, LENGTH, model_width) + shift_rows[:, None, :]
        ).reshape(shard_rows, model_width)
        entry_rows = stream
        normed = layer_norm(stream, norm_full[layer_index, 0], norm_full[layer_index, 1]).astype(
            jnp.bfloat16
        )
        normed_all = lax.all_gather(normed, "tensor", axis=0, tiled=True)
        local_width = qkv_full.shape[3]
        proj_flat = qkv_full[layer_index].reshape(model_width, 3 * local_width)
        projected = jnp.dot(normed_all, proj_flat, preferred_element_type=jnp.float32).astype(
            jnp.bfloat16
        )
        group_rows = normed_all.shape[0]
        seq_count = group_rows // LENGTH
        heads_here = local_width // HEAD_DIM
        shaped = projected.reshape(seq_count, LENGTH, 3, heads_here, HEAD_DIM)
        query_mat = shaped[:, :, 0]
        key_mat = shaped[:, :, 1]
        value_mat = shaped[:, :, 2]
        mixed, log_total = attend(query_mat, key_mat, value_mat)
        mixed_rows = mixed.reshape(group_rows, local_width)

        def out_term(start, count, rows_in=mixed_rows, weight_in=out_full[layer_index]):
            return jnp.dot(rows_in, weight_in, preferred_element_type=jnp.float32)

        stream = stream + lax.psum_scatter(
            out_term(jnp.int32(0), shard_rows * lax.axis_size("tensor")).astype(jnp.bfloat16),
            "tensor",
            scatter_dimension=0,
            tiled=True,
        ).astype(jnp.float32)
        middle = stream
        normed_ffn = layer_norm(
            stream, norm_full[layer_index, 2], norm_full[layer_index, 3]
        ).astype(jnp.bfloat16)
        ffn_all = lax.all_gather(normed_ffn, "tensor", axis=0, tiled=True)
        pre_act = jnp.dot(
            ffn_all, up_full[layer_index], preferred_element_type=jnp.float32
        ) + bias_full[layer_index].reshape(-1).astype(jnp.float32)
        hidden = gelu_exact(pre_act).astype(jnp.bfloat16)

        def down_term(start, count, rows_in=hidden, weight_in=down_full[layer_index]):
            return jnp.dot(rows_in, weight_in, preferred_element_type=jnp.float32)

        stream = (
            stream
            + lax.psum_scatter(
                down_term(jnp.int32(0), shard_rows * lax.axis_size("tensor")).astype(jnp.bfloat16),
                "tensor",
                scatter_dimension=0,
                tiled=True,
            ).astype(jnp.float32)
            + norm_full[layer_index, 4]
        )
        kept_layers.append(
            (
                entry_rows,
                normed_all,
                query_mat,
                key_mat,
                value_mat,
                log_total,
                mixed_rows,
                middle,
                ffn_all,
                pre_act,
                hidden,
            )
        )
    activations = stream.astype(jnp.bfloat16)
    gradient = (
        cotangent.astype(jnp.float32).reshape(local_items, LENGTH, model_width)
        * my_scale[:, None, None]
    ).reshape(shard_rows, model_width)
    layer_grads = [None] * LAYERS
    for layer_index in reversed(range(LAYERS)):
        (
            entry_rows,
            normed_all,
            query_mat,
            key_mat,
            value_mat,
            log_total,
            mixed_rows,
            middle,
            ffn_all,
            pre_act,
            hidden,
        ) = kept_layers[layer_index]
        group_rows = normed_all.shape[0]
        seq_count = group_rows // LENGTH
        local_width = mixed_rows.shape[1]
        heads_here = local_width // HEAD_DIM
        bias_down_grad = jnp.sum(gradient, 0)
        grad_low = gradient.astype(jnp.bfloat16)
        grad_all = lax.all_gather(grad_low, "tensor", axis=0, tiled=True)
        down_grad = jnp.einsum("gf,gd->fd", hidden, grad_all, preferred_element_type=jnp.float32)
        hidden_grad = jnp.einsum(
            "gd,fd->gf", grad_all, down_full[layer_index], preferred_element_type=jnp.float32
        )
        gelu_pull = jax.vjp(gelu_exact, pre_act)[1]
        pre_grad = gelu_pull(hidden_grad)[0].astype(jnp.bfloat16)
        bias_up_grad = jnp.sum(pre_grad.astype(jnp.float32), 0)
        up_grad = jnp.einsum("gd,gf->df", ffn_all, pre_grad, preferred_element_type=jnp.float32)

        def up_term(start, count, rows_in=pre_grad, weight_in=up_full[layer_index]):
            return jnp.einsum("gf,df->gd", rows_in, weight_in, preferred_element_type=jnp.float32)

        normed_grad = lax.psum_scatter(
            up_term(jnp.int32(0), shard_rows * lax.axis_size("tensor")).astype(jnp.bfloat16),
            "tensor",
            scatter_dimension=0,
            tiled=True,
        ).astype(jnp.float32)
        middle_pull = jax.vjp(
            layer_norm, middle, norm_full[layer_index, 2], norm_full[layer_index, 3]
        )[1]
        middle_part, gain_two, shift_two = middle_pull(normed_grad)
        middle_grad = gradient + middle_part
        middle_low = middle_grad.astype(jnp.bfloat16)
        attn_all = lax.all_gather(middle_low, "tensor", axis=0, tiled=True)
        out_grad = jnp.einsum("gk,gd->kd", mixed_rows, attn_all, preferred_element_type=jnp.float32)
        mixed_grad = jnp.einsum(
            "gd,kd->gk", attn_all, out_full[layer_index], preferred_element_type=jnp.float32
        ).astype(jnp.bfloat16)
        grad_query, grad_key, grad_value = attend_back(
            query_mat,
            key_mat,
            value_mat,
            log_total,
            mixed_grad.reshape(seq_count, LENGTH, heads_here, HEAD_DIM),
        )
        stacked = jnp.stack([grad_query, grad_key, grad_value], 2).reshape(
            group_rows, 3 * local_width
        )
        qkv_grad = jnp.einsum(
            "gd,gk->dk", normed_all, stacked, preferred_element_type=jnp.float32
        ).reshape(model_width, 3, local_width)

        def qkv_term(
            start,
            count,
            rows_in=stacked,
            weight_in=qkv_full[layer_index].reshape(model_width, 3 * local_width),
        ):
            return jnp.einsum("gk,dk->gd", rows_in, weight_in, preferred_element_type=jnp.float32)

        entry_part = lax.psum_scatter(
            qkv_term(jnp.int32(0), shard_rows * lax.axis_size("tensor")).astype(jnp.bfloat16),
            "tensor",
            scatter_dimension=0,
            tiled=True,
        ).astype(jnp.float32)
        entry_pull = jax.vjp(
            layer_norm, entry_rows, norm_full[layer_index, 0], norm_full[layer_index, 1]
        )[1]
        entry_grad, gain_one, shift_one = entry_pull(entry_part)
        entry_grad = middle_grad + entry_grad
        item_grad = jnp.sum(entry_grad.reshape(local_items, LENGTH, model_width), 1)
        time_grad = jnp.dot(
            time_feats.T, item_grad, precision=highest, preferred_element_type=jnp.float32
        )
        norm_grad = jnp.stack([gain_one, shift_one, gain_two, shift_two, bias_down_grad])
        layer_grads[layer_index] = (
            qkv_grad,
            out_grad,
            up_grad,
            bias_up_grad.reshape(-1, BIAS_ROW),
            down_grad,
            norm_grad,
            time_grad,
        )
        gradient = entry_grad
    input_grad = gradient.astype(jnp.bfloat16)
    qkv_total = jnp.stack([entry_set[0] for entry_set in layer_grads])
    out_total = jnp.stack([entry_set[1] for entry_set in layer_grads])
    up_total = jnp.stack([entry_set[2] for entry_set in layer_grads])
    bias_total = jnp.stack([entry_set[3] for entry_set in layer_grads])
    down_total = jnp.stack([entry_set[4] for entry_set in layer_grads])
    norm_total = jnp.stack([entry_set[5] for entry_set in layer_grads])
    time_total = jnp.stack([entry_set[6] for entry_set in layer_grads])
    summed = lax.psum((qkv_total, out_total, up_total, bias_total, down_total), "dp")
    qkv_own = own_slice(summed[0], qkv_weight, 1)
    out_own = own_slice(summed[1], out_weight, 2)
    up_own = own_slice(summed[2], up_weight, 1)
    bias_own = own_slice(summed[3], up_bias, 2)
    down_own = own_slice(summed[4], down_weight, 2)
    norm_own, time_own = (
        lax.psum_scatter(norm_total, ("dp", "tensor"), scatter_dimension=2, tiled=True),
        lax.psum_scatter(time_total, ("dp", "tensor"), scatter_dimension=1, tiled=True),
    )
    new_qkv = adamw(qkv_weight, qkv_own, qkv_first, qkv_second, learn_rate)
    new_out = adamw(out_weight, out_own, out_first, out_second, learn_rate)
    new_up = adamw(up_weight, up_own, up_first, up_second, learn_rate)
    new_bias = adamw(up_bias, bias_own, bias_first, bias_second, learn_rate)
    new_down = adamw(down_weight, down_own, down_first, down_second, learn_rate)
    new_norm = adamw(norm_params, norm_own, norm_first, norm_second, norm_rate)
    new_time = adamw(time_weight, time_own, time_first, time_second, learn_rate)
    return (
        activations,
        input_grad,
        new_qkv[0],
        new_qkv[1],
        new_qkv[2][:, :, :2],
        new_qkv[2][:, :, 2],
        new_out[0],
        new_out[1],
        new_out[2],
        new_up[0],
        new_up[1],
        new_up[2],
        new_bias[0],
        new_bias[1],
        new_bias[2],
        new_down[0],
        new_down[1],
        new_down[2],
        new_norm[0],
        new_norm[1],
        new_norm[2],
        new_time[0],
        new_time[1],
        new_time[2],
    )


def solution(mesh):
    return jax.shard_map(
        per_device,
        mesh=mesh,
        in_specs=(
            P(("dp", "tensor"), None),
            P(("dp", "tensor"), None),
            P("dp"),
            P("dp"),
            P(None, "dp", None, "tensor"),
            P(None, "dp", None, "tensor"),
            P(None, "dp", None, "tensor"),
            P(None, "tensor", "dp"),
            P(None, "tensor", "dp"),
            P(None, "tensor", "dp"),
            P(None, "dp", "tensor"),
            P(None, "dp", "tensor"),
            P(None, "dp", "tensor"),
            P(None, "tensor", "dp"),
            P(None, "tensor", "dp"),
            P(None, "tensor", "dp"),
            P(None, "tensor", "dp"),
            P(None, "tensor", "dp"),
            P(None, "tensor", "dp"),
            P(None, None, ("dp", "tensor")),
            P(None, None, ("dp", "tensor")),
            P(None, None, ("dp", "tensor")),
            P(None, ("dp", "tensor"), None),
            P(None, ("dp", "tensor"), None),
            P(None, ("dp", "tensor"), None),
        ),
        out_specs=(
            P(("dp", "tensor"), None),
            P(("dp", "tensor"), None),
            P(None, "dp", None, "tensor"),
            P(None, "dp", None, "tensor"),
            P(None, "dp", None, "tensor"),
            P(None, "dp", "tensor"),
            P(None, "tensor", "dp"),
            P(None, "tensor", "dp"),
            P(None, "tensor", "dp"),
            P(None, "dp", "tensor"),
            P(None, "dp", "tensor"),
            P(None, "dp", "tensor"),
            P(None, "tensor", "dp"),
            P(None, "tensor", "dp"),
            P(None, "tensor", "dp"),
            P(None, "tensor", "dp"),
            P(None, "tensor", "dp"),
            P(None, "tensor", "dp"),
            P(None, None, ("dp", "tensor")),
            P(None, None, ("dp", "tensor")),
            P(None, None, ("dp", "tensor")),
            P(None, ("dp", "tensor"), None),
            P(None, ("dp", "tensor"), None),
            P(None, ("dp", "tensor"), None),
        ),
        check_vma=False,
    )
```

profile of v0, /device:TPU:0, one launch (start us, length us, event | category | flops | bytes accessed | tf_op | source)
XLA Modules:
  0.0 1410.1 jit_solution(7055341840546088544)
XLA Ops:
  10.6 44.7 %all_gather.46 = f32[2,5,512]{1,0,2:T(2,128)S(1)} all-gather(f32[2,5,16]{1,0,2:T(2,128)S(1)} %copy.247), channel_id=1, replica_groups=mesh['dp'=16,'tensor'=2] {'dp','tensor'}, dimensions={2}, use_global_device_ids=true | all-gather | bytes 21120 | tf_op jit(solution)/shard_map/all_gather | solution.py:143
  56.1 18.2 %slice_reduce_fusion = (f32[512]{0:T(512)}, f32[512]{0:T(512)}, f32[512]{0:T(512)}, f32[512]{0:T(512)S(1)}, f32[512]{0:T(512)S(1)}, /*index=5*/f32[512]{0:T(512)...) fusion(f32[2,5,512]{1,0,2:T(2,128)S(1)} %all_gather.46), kind=kLoop, calls=%fused_computation.203 | loop fusion | bytes 40960 | tf_op jit(solution)/shard_map/slice | solution.py:215
  79.1 39.4 %all_gather.49 = bf16[2,256,512]{1,2,0:T(8,128)(2,1)S(1)} all-gather(bf16[2,256,32]{1,2,0:T(8,128)(2,1)S(1)} %convert_element_type.234), channel_id=1, replica_groups=mesh['dp'=16,'tensor'=2] {'dp'}, dimensions={2}, use_global_device_ids=true | all-gather | bytes 557056 | tf_op jit(solution)/shard_map/all_gather | solution.py:137
  118.4 13.5 all-gather.17.cloned.1.call-done
  132.0 5.3 fusion.141
  137.3 3.2 copy.320
  140.5 3.7 all-gather.15.cloned.1.call-done
  144.2 6.1 convolution_convert_fusion.1
  150.3 12.3 reshape.313
  162.6 8.6 fusion.140
  171.2 4.7 copy.321
  175.9 4.7 copy.322
  180.6 3.8 copy.323
  184.4 3.4 multiply_reduce_fusion.3
  201.0 9.8 reduce-scatter.13.cloned.1.call-done
  216.9 41.4 %all_gather.52 = bf16[2,8,128]{1,0,2:T(2,128)(2,1)S(1)} all-gather(bf16[2,8,8]{1,0,2:T(2,128)(2,1)S(1)} %copy.256), channel_id=1, replica_groups=mesh['dp'=16,'tensor'=2] {'dp'}, dimensions={2}, use_global_device_ids=true | all-gather | bytes 4352 | tf_op jit(solution)/shard_map/all_gather | solution.py:139
  258.5 18.2 %all-gather.21.cloned.1.call-done = bf16[2,512,1024]{2,1,0:T(8,128)(2,1)} async-done(((bf16[2,32,1024]{2,1,0:T(8,128)(2,1)}), bf16[2,512,1024]{2,1,0:T(8,128)(2,1)}) %all-gather.21.cloned.1.call-update) | async-done | bytes 2097168 | tf_op jit(solution)/shard_map/all_gather | solution.py:138
  276.6 12.0 all-gather.19.cloned.1.call-done
  288.6 37.1 %multiply_convert_fusion.3 = (bf16[2560,1024]{1,0:T(8,128)(2,1)}, f32[2560,1024]{1,0:T(8,128)}, f32[2560,1024]{1,0:T(8,128)}) fusion(f32[1024]{0:T(1024)S(1)} %bitcast_convert_fusion.1, bf16[2560,512]{1,0:T(8,128)(2,1)} %all-gather.19.cloned.1.call-done, bf16[2,512,1024]{2,1,0:T(8,128)(2,1)} %all-gather.21.cloned.1.call-done), kind=kOutput, calls=%fused_computation.29 | convolution fusion | flops 2857369600 | bytes 29888512 | tf_op jit(solution)/shard_map/dot_general | solution.py:199
  325.7 28.5 %all-gather.23.cloned.1.call-done = bf16[2,1024,512]{1,2,0:T(8,128)(2,1)} async-done(((bf16[2,1024,32]{1,2,0:T(8,128)(2,1)}), bf16[2,1024,512]{1,2,0:T(8,128)(2,1)}) %all-gather.23.cloned.1.call-update) | async-done | bytes 2097168 | tf_op jit(solution)/shard_map/all_gather | solution.py:140
  354.2 7.2 convolution_convert_fusion.5
  363.3 7.0 reduce-scatter.15.cloned.1.call-done
  378.0 10.3 all-gather.25.cloned.1.call-done
  388.3 5.9 convolution_convert_fusion
  394.2 12.3 reshape.314
  406.5 7.7 fusion.139
  417.0 3.8 copy.327
  420.8 4.2 copy.328
  438.2 11.3 reduce-scatter.17.cloned.1.call-done
  456.0 11.0 all-gather.27.cloned.1.call-done
  466.9 28.8 %multiply_convert_fusion.2 = (bf16[2560,1024]{1,0:T(8,128)(2,1)}, f32[2560,1024]{1,0:T(8,128)}, f32[2560,1024]{1,0:T(8,128)}) fusion(f32[1024]{0:T(1024)S(1)} %bitcast_convert_fusion, bf16[2560,512]{1,0:T(8,128)(2,1)} %all-gather.27.cloned.1.call-done, bf16[2,512,1024]{2,1,0:T(8,128)(2,1)} %all-gather.21.cloned.1.call-done), kind=kOutput, calls=%fused_computation.14 | convolution fusion | flops 2857369600 | bytes 29888512 | tf_op jit(solution)/shard_map/dot_general | solution.py:199
  495.7 12.4 convert_reduce_fusion
  510.6 4.3 convolution_convert_fusion.3
  515.1 6.7 convolution_convert_fusion.4
  521.9 4.4 reduce-scatter.21.cloned.1.call-done
  528.7 11.2 reduce-scatter.19.cloned.1.call-done
  539.9 3.6 fusion.134
  546.7 12.7 all-gather.31.cloned.1.call-done
  564.1 3.8 copy.267
  567.9 7.1 fusion.74
  575.1 5.6 multiply_reduce_fusion.1
  587.3 3.0 copy.272
  594.9 3.8 convolution_convert_fusion.7
  598.8 11.4 reduce-scatter.23.cloned.1.call-done
  619.5 12.7 all-gather.33.cloned.1.call-done
  632.3 12.0 convert_reduce_fusion.1
  646.5 4.2 convolution_convert_fusion.2
  650.9 11.4 reduce-scatter.25.cloned.1.call-done
  669.1 12.7 all-gather.35.cloned.1.call-done
  681.8 3.7 convolution_convert_fusion.10
  685.5 5.1 reshape.316
  690.6 4.7 copy.274
  695.4 7.5 fusion.71
  702.9 7.5 multiply_reduce_fusion
  724.6 3.9 convolution_convert_fusion.6
  728.8 7.7 convolution_bitcast_fusion
  736.5 6.9 convolution_bitcast_fusion.2
  753.0 4.1 fusion.133
  763.5 3.0 convolution_bitcast_fusion.6
  766.5 4.1 fusion.66
  791.3 42.7 %psum.38 = f32[2,8,128]{2,1,0:T(8,128)S(1)} all-reduce(f32[2,8,128]{2,1,0:T(8,128)S(1)} %pad_maximum_fusion.9), channel_id=1, replica_groups=mesh['dp'=16,'tensor'=2] {'dp'}, use_global_device_ids=true, to_apply=%region_35.0 | all-reduce | flops 2048 | bytes 16384 | tf_op jit(solution)/shard_map/psum | solution.py:344
  834.7 60.6 %reduce-scatter.31.cloned.1.call-done = f32[16,10]{1,0:T(8,128)} async-done(((f32[512,10]{1,0:T(8,128)}), f32[16,10]{1,0:T(8,128)}) %reduce-scatter.31.cloned.1.call-update) | async-done | bytes 656
  898.0 132.2 %reduce-scatter.29.cloned.1.call-done = f32[2,16,512]{2,1,0:T(8,128)} async-done(((f32[2,512,512]{2,1,0:T(8,128)}), f32[2,16,512]{2,1,0:T(8,128)}) %reduce-scatter.29.cloned.1.call-update) | async-done | bytes 65552 | tf_op jit(solution)/shard_map/reduce_scatter | solution.py:352
  1031.8 362.8 %all-reduce.3.cloned.1.call-done = (f32[2,512,3,256]{3,1,2,0:T(8,128)}, f32[2,256,512]{1,2,0:T(8,128)}, f32[2,512,1024]{2,1,0:T(8,128)}, f32[2,1024,512]{1,2,0:T(8,128)}) async-done(((f32[2,512,3,256]{3,1,2,0:T(8,128)}, f32[2,256,512]{1,2,0:T(8,128)}, f32[2,512,1024]{2,1,0:T(8,128)}, f32[2,1024,512]{1,2,0:T(8,128)}), (f32[2,512,3,256]{3,1,2,0:T(8,128)}, f32[2,256,512]{1,2,0:T(8,128)}, ...) | async-done | bytes 12582928 | tf_op jit(solution)/shard_map/psum | solution.py:344
  (448 shorter events, 166.3 us)
Async XLA Ops:
  7.2 69.0 %copy-start.2 = (bf16[1280,512]{1,0:T(8,128)(2,1)S(1)}, bf16[1280,512]{1,0:T(8,128)(2,1)}, u32[]{:S(2)}) copy-start(bf16[1280,512]{1,0:T(8,128)(2,1)} %param.25) | copy-start | bytes 3932164
  7.2 67.2 %all-gather.13.cloned.1.call-start = ((), (), s32[]{:S(2)}) async-start(), calls=%async_computation.10 | async-start | bytes 2162688 | tf_op jit(solution)/shard_map/all_gather | solution.py:144
  7.9 124.0 %all-gather.17.cloned.1.call-start = ((), (), s32[]{:S(2)}) async-start(), calls=%async_computation.12 | async-start | bytes 1671168 | tf_op jit(solution)/shard_map/all_gather | solution.py:136
  9.7 134.5 %all-gather.15.cloned.1.call-start = ((), (), s32[]{:S(2)}) async-start(), calls=%async_computation.11 | async-start | bytes 3932160 | tf_op jit(solution)/shard_map/all_gather | solution.py:169
  56.1 305.4 %copy-start.72 = (f32[5,256]{1,0:T(8,128)}, f32[5,256]{1,0:T(8,128)S(1)}, u32[]{:S(2)}) copy-start(f32[5,256]{1,0:T(8,128)S(1)} %get-tuple-element.220) | copy-start | bytes 15364
  56.1 305.4 %copy-start.74 = (f32[5,256]{1,0:T(8,128)}, f32[5,256]{1,0:T(8,128)S(1)}, u32[]{:S(2)}) copy-start(f32[5,256]{1,0:T(8,128)S(1)} %get-tuple-element.221) | copy-start | bytes 15364
  74.4 139.7 %copy-start.92 = (f32[512]{0:T(512)}, f32[512]{0:T(512)S(1)}, u32[]{:S(2)}) copy-start(f32[512]{0:T(512)S(1)} %get-tuple-element.166) | copy-start | bytes 6148
  74.4 298.7 %copy-start.98 = (f32[512]{0:T(512)}, f32[512]{0:T(512)S(1)}, u32[]{:S(2)}) copy-start(f32[512]{0:T(512)S(1)} %get-tuple-element.163) | copy-start | bytes 6148
  76.2 294.1 %copy-start.45 = (f32[5,512]{1,0:T(8,128)}, f32[5,512]{1,0:T(8,128)S(1)}, u32[]{:S(2)}) copy-start(f32[5,512]{1,0:T(8,128)S(1)} %fusion.98) | copy-start | bytes 30724
  79.0 131.9 %reduce-scatter.13.cloned.1.call-start = ((), (), s32[]{:S(2)}) async-start(), calls=%async_computation.13 | async-start | bytes 3932160 | tf_op jit(solution)/shard_map/reduce_scatter | solution.py:188
  199.3 77.3 %all-gather.21.cloned.1.call-start = ((), (), s32[]{:S(2)}) async-start(), calls=%async_computation.15 | async-start | bytes 2228224 | tf_op jit(solution)/shard_map/all_gather | solution.py:138
  200.9 87.7 %all-gather.19.cloned.1.call-start = ((), (), s32[]{:S(2)}) async-start(), calls=%async_computation.14 | async-start | bytes 3932160 | tf_op jit(solution)/shard_map/all_gather | solution.py:198
  216.0 138.2 %all-gather.23.cloned.1.call-start = ((), (), s32[]{:S(2)}) async-start(), calls=%async_computation.16 | async-start | bytes 2228224 | tf_op jit(solution)/shard_map/all_gather | solution.py:140
  216.7 153.6 %reduce-scatter.15.cloned.1.call-start = ((), (), s32[]{:S(2)}) async-start(), calls=%async_computation.17 | async-start | bytes 3932160 | tf_op jit(solution)/shard_map/reduce_scatter | solution.py:209
  258.5 67.2 %copy-start.112 = (f32[1024]{0:T(1024)}, f32[1024]{0:T(1024)S(1)}, u32[]{:S(2)}) copy-start(f32[1024]{0:T(1024)S(1)} %bitcast_convert_fusion.1) | copy-start | bytes 12292
  361.4 26.9 %all-gather.25.cloned.1.call-start = ((), (), s32[]{:S(2)}) async-start(), calls=%async_computation.18 | async-start | bytes 3932160 | tf_op jit(solution)/shard_map/all_gather | solution.py:169
  375.6 73.9 %reduce-scatter.17.cloned.1.call-start = ((), (), s32[]{:S(2)}) async-start(), calls=%async_computation.19 | async-start | bytes 3932160 | tf_op jit(solution)/shard_map/reduce_scatter | solution.py:188
  378.0 16.2 %copy-start.55 = (bf16[1,512,3,256]{1,3,2,0:T(8,128)(2,1)}, bf16[1,512,3,256]{1,3,2,0:T(8,128)(2,1)S(1)}, u32[]{:S(2)}) copy-start(bf16[1,512,3,256]{1,3,2,0:T(8,128)(2,1)S(1)} %copy.325) | copy-start | bytes 2359300
  437.9 29.0 %all-gather.27.cloned.1.call-start = ((), (), s32[]{:S(2)}) async-start(), calls=%async_computation.20 | async-start | bytes 3932160 | tf_op jit(solution)/shard_map/all_gather | solution.py:198
  454.2 41.6 %all-gather.29.cloned.1.call-start = ((), (), s32[]{:S(2)}) async-start(), calls=%async_computation.22 | async-start | bytes 3932160 | tf_op jit(solution)/shard_map/all_gather | solution.py:258
  455.8 70.5 %reduce-scatter.21.cloned.1.call-start = ((), (), s32[]{:S(2)}) async-start(), calls=%async_computation.23 | async-start | bytes 3932160 | tf_op jit(solution)/shard_map/reduce_scatter | solution.py:271
  456.0 39.8 %copy-start.122 = (bf16[2,1024,512]{1,2,0:T(8,128)(2,1)S(1)}, bf16[2,1024,512]{1,2,0:T(8,128)(2,1)}, u32[]{:S(2)}) copy-start(bf16[2,1024,512]{1,2,0:T(8,128)(2,1)} %all-gather.23.cloned.1.call-done) | copy-start | bytes 6291460
  495.7 14.8 %copy-start.120 = (bf16[2,512,1024]{2,1,0:T(8,128)(2,1)S(1)}, bf16[2,512,1024]{2,1,0:T(8,128)(2,1)}, u32[]{:S(2)}) copy-start(bf16[2,512,1024]{2,1,0:T(8,128)(2,1)} %all-gather.21.cloned.1.call-done) | copy-start | bytes 6291460
  514.9 25.1 %reduce-scatter.19.cloned.1.call-start = ((), (), s32[]{:S(2)}) async-start(), calls=%async_computation.21 | async-start | bytes 3932160 | tf_op jit(solution)/shard_map/reduce_scatter | solution.py:209
  521.9 18.1 %copy-start.109 = (f32[512]{0:T(512)S(1)}, f32[512]{0:T(512)}, u32[]{:S(2)}) copy-start(f32[512]{0:T(512)} %get-tuple-element.159) | copy-start | bytes 6148
  521.9 37.6 %all-gather.31.cloned.1.call-start = ((), (), s32[]{:S(2)}) async-start(), calls=%async_computation.24 | async-start | bytes 3932160 | tf_op jit(solution)/shard_map/all_gather | solution.py:283
  546.7 63.6 %reduce-scatter.23.cloned.1.call-start = ((), (), s32[]{:S(2)}) async-start(), calls=%async_computation.25 | async-start | bytes 3932160 | tf_op jit(solution)/shard_map/reduce_scatter | solution.py:310
  594.9 15.3 %copy-start.64 = (f32[1280]{0:T(1024)S(1)}, f32[1280]{0:T(1024)}, u32[]{:S(2)}) copy-start(f32[1280]{0:T(1024)} %copy-done.63) | copy-start | bytes 15364
  598.8 33.5 %all-gather.33.cloned.1.call-start = ((), (), s32[]{:S(2)}) async-start(), calls=%async_computation.26 | async-start | bytes 3932160 | tf_op jit(solution)/shard_map/all_gather | solution.py:258
  618.2 14.1 copy-start.123
  619.5 42.8 %reduce-scatter.25.cloned.1.call-start = ((), (), s32[]{:S(2)}) async-start(), calls=%async_computation.27 | async-start | bytes 3932160 | tf_op jit(solution)/shard_map/reduce_scatter | solution.py:271
  632.2 14.3 %copy-start.121 = (bf16[2,512,1024]{2,1,0:T(8,128)(2,1)S(1)}, bf16[2,512,1024]{2,1,0:T(8,128)(2,1)}, u32[]{:S(2)}) copy-start(bf16[2,512,1024]{2,1,0:T(8,128)(2,1)} %all-gather.21.cloned.1.call-done) | copy-start | bytes 6291460
  646.5 15.8 %copy-start.46 = (f32[5,512]{1,0:T(8,128)S(1)}, f32[5,512]{1,0:T(8,128)}, u32[]{:S(2)}) copy-start(f32[5,512]{1,0:T(8,128)} %copy-done.45) | copy-start | bytes 30724
  646.5 15.8 %copy-start.58 = (f32[1280]{0:T(1024)S(1)}, f32[1280]{0:T(1024)}, u32[]{:S(2)}) copy-start(f32[1280]{0:T(1024)} %copy-done.57) | copy-start | bytes 15364
  650.8 14.2 %copy-start.91 = (f32[1280]{0:T(1024)S(1)}, f32[1280]{0:T(1024)}, u32[]{:S(2)}) copy-start(f32[1280]{0:T(1024)} %copy-done.90) | copy-start | bytes 15364
  650.8 14.2 %copy-start.77 = (f32[1280]{0:T(1024)S(1)}, f32[1280]{0:T(1024)}, u32[]{:S(2)}) copy-start(f32[1280]{0:T(1024)} %copy-done.76) | copy-start | bytes 15364
  650.8 31.0 %all-gather.35.cloned.1.call-start = ((), (), s32[]{:S(2)}) async-start(), calls=%async_computation.28 | async-start | bytes 3932160 | tf_op jit(solution)/shard_map/all_gather | solution.py:283
  669.0 78.4 %reduce-scatter.27.cloned.1.call-start = ((), (), s32[]{:S(2)}) async-start(), calls=%async_computation.29 | async-start | bytes 3932160 | tf_op jit(solution)/shard_map/reduce_scatter | solution.py:310
  695.3 15.0 %slice-start = ((s8[10485760]{0:T(1024)(128)(4,1)}), s8[4194304]{0:T(1024)(128)(4,1)S(1)}, s32[]{:S(2)}) async-start(s8[10485760]{0:T(1024)(128)(4,1)} %bitcast.295), calls=%async_computation.33 | async-start | bytes 8388608
  695.4 15.0 %slice-start.1 = ((s8[10485760]{0:T(1024)(128)(4,1)}), s8[4194304]{0:T(1024)(128)(4,1)S(1)}, s32[]{:S(2)}) async-start(s8[10485760]{0:T(1024)(128)(4,1)} %bitcast.295), calls=%async_computation.34 | async-start | bytes 8388608
  728.5 166.8 %reduce-scatter.31.cloned.1.call-start = ((), (), s32[]{:S(2)}) async-start(), calls=%async_computation.31 | async-start | bytes 270336
  760.5 269.8 %reduce-scatter.29.cloned.1.call-start = ((), (), s32[]{:S(2)}) async-start(), calls=%async_computation.30 | async-start | bytes 2162688 | tf_op jit(solution)/shard_map/reduce_scatter | solution.py:352
  763.2 631.4 %all-reduce.3.cloned.1.call-start = ((), (), s32[]{:S(2)}) async-start(), calls=%async_computation.32 | async-start | bytes 25165824 | tf_op jit(solution)/shard_map/psum | solution.py:344
  790.6 43.4 %copy-start.103 = (f32[2,8,8]{2,1,0:T(8,128)S(1)}, f32[2,8,8]{2,1,0:T(8,128)}, u32[]{:S(2)}) copy-start(f32[2,8,8]{2,1,0:T(8,128)} %param.38) | copy-start | bytes 1540
  790.6 43.4 %copy-start.107 = (f32[2,8,8]{2,1,0:T(8,128)S(1)}, f32[2,8,8]{2,1,0:T(8,128)}, u32[]{:S(2)}) copy-start(f32[2,8,8]{2,1,0:T(8,128)} %param.39) | copy-start | bytes 1540
  790.6 43.4 %copy-start.108 = (f32[2,8,8]{2,1,0:T(8,128)S(1)}, f32[2,8,8]{2,1,0:T(8,128)}, u32[]{:S(2)}) copy-start(f32[2,8,8]{2,1,0:T(8,128)} %param.40) | copy-start | bytes 1540
  790.6 105.6 %copy-start.105 = (f32[2,5,16]{2,0,1:T(2,128)S(1)}, f32[2,5,16]{2,0,1:T(2,128)}, u32[]{:S(2)}) copy-start(f32[2,5,16]{2,0,1:T(2,128)} %param.44) | copy-start | bytes 1924
  790.7 105.6 %copy-start.110 = (f32[2,5,16]{2,0,1:T(2,128)S(1)}, f32[2,5,16]{2,0,1:T(2,128)}, u32[]{:S(2)}) copy-start(f32[2,5,16]{2,0,1:T(2,128)} %param.45) | copy-start | bytes 1924
  790.7 105.6 %copy-start.111 = (f32[2,5,16]{2,0,1:T(2,128)S(1)}, f32[2,5,16]{2,0,1:T(2,128)}, u32[]{:S(2)}) copy-start(f32[2,5,16]{2,0,1:T(2,128)} %param.46) | copy-start | bytes 1924
  790.7 239.6 %copy-start.65 = (f32[2,16,512]{2,1,0:T(8,128)S(1)}, f32[2,16,512]{2,1,0:T(8,128)}, u32[]{:S(2)}) copy-start(f32[2,16,512]{2,1,0:T(8,128)} %param.47) | copy-start | bytes 196612
  790.7 239.6 %copy-start.94 = (f32[2,16,512]{2,1,0:T(8,128)S(1)}, f32[2,16,512]{2,1,0:T(8,128)}, u32[]{:S(2)}) copy-start(f32[2,16,512]{2,1,0:T(8,128)} %param.48) | copy-start | bytes 196612
  790.7 239.6 %copy-start.95 = (f32[2,16,512]{2,1,0:T(8,128)S(1)}, f32[2,16,512]{2,1,0:T(8,128)}, u32[]{:S(2)}) copy-start(f32[2,16,512]{2,1,0:T(8,128)} %param.49) | copy-start | bytes 196612
  790.7 603.9 %copy-start.53 = (f32[2,32,3,256]{3,1,2,0:T(8,128)S(1)}, f32[2,32,3,256]{3,1,2,0:T(8,128)}, u32[]{:S(2)}) copy-start(f32[2,32,3,256]{3,1,2,0:T(8,128)} %param.29) | copy-start | bytes 589828
  790.7 603.9 %copy-start.78 = (f32[2,32,3,256]{3,1,2,0:T(8,128)S(1)}, f32[2,32,3,256]{3,1,2,0:T(8,128)}, u32[]{:S(2)}) copy-start(f32[2,32,3,256]{3,1,2,0:T(8,128)} %param.30) | copy-start | bytes 589828
  790.7 603.9 %copy-start.79 = (f32[2,32,3,256]{3,1,2,0:T(8,128)S(1)}, f32[2,32,3,256]{3,1,2,0:T(8,128)}, u32[]{:S(2)}) copy-start(f32[2,32,3,256]{3,1,2,0:T(8,128)} %param.31) | copy-start | bytes 589828
  790.8 607.0 %copy-start.67 = (f32[2,256,32]{1,2,0:T(8,128)S(1)}, f32[2,256,32]{1,2,0:T(8,128)}, u32[]{:S(2)}) copy-start(f32[2,256,32]{1,2,0:T(8,128)} %param.32) | copy-start | bytes 196612
  790.8 607.0 %copy-start.96 = (f32[2,256,32]{1,2,0:T(8,128)S(1)}, f32[2,256,32]{1,2,0:T(8,128)}, u32[]{:S(2)}) copy-start(f32[2,256,32]{1,2,0:T(8,128)} %param.33) | copy-start | bytes 196612
  790.8 607.0 %copy-start.97 = (f32[2,256,32]{1,2,0:T(8,128)S(1)}, f32[2,256,32]{1,2,0:T(8,128)}, u32[]{:S(2)}) copy-start(f32[2,256,32]{1,2,0:T(8,128)} %param.34) | copy-start | bytes 196612
  790.8 608.5 %copy-start.50 = (f32[2,32,1024]{2,1,0:T(8,128)S(1)}, f32[2,32,1024]{2,1,0:T(8,128)}, u32[]{:S(2)}) copy-start(f32[2,32,1024]{2,1,0:T(8,128)} %param.35) | copy-start | bytes 786436
  790.8 608.5 %copy-start.68 = (f32[2,32,1024]{2,1,0:T(8,128)S(1)}, f32[2,32,1024]{2,1,0:T(8,128)}, u32[]{:S(2)}) copy-start(f32[2,32,1024]{2,1,0:T(8,128)} %param.36) | copy-start | bytes 786436
  790.8 608.5 %copy-start.69 = (f32[2,32,1024]{2,1,0:T(8,128)S(1)}, f32[2,32,1024]{2,1,0:T(8,128)}, u32[]{:S(2)}) copy-start(f32[2,32,1024]{2,1,0:T(8,128)} %param.37) | copy-start | bytes 786436
  790.9 610.5 %copy-start.52 = (f32[2,1024,32]{1,2,0:T(8,128)S(1)}, f32[2,1024,32]{1,2,0:T(8,128)}, u32[]{:S(2)}) copy-start(f32[2,1024,32]{1,2,0:T(8,128)} %param.41) | copy-start | bytes 786436
  790.9 610.5 %copy-start.70 = (f32[2,1024,32]{1,2,0:T(8,128)S(1)}, f32[2,1024,32]{1,2,0:T(8,128)}, u32[]{:S(2)}) copy-start(f32[2,1024,32]{1,2,0:T(8,128)} %param.42) | copy-start | bytes 786436
  790.9 610.5 %copy-start.71 = (f32[2,1024,32]{1,2,0:T(8,128)S(1)}, f32[2,1024,32]{1,2,0:T(8,128)}, u32[]{:S(2)}) copy-start(f32[2,1024,32]{1,2,0:T(8,128)} %param.43) | copy-start | bytes 786436
  (96 other events, 402.4 us)
Sparse Core Ops, SparseCore 0:
  11.0 59.4 all-gather.12
  73.8 58.0 all-gather.16
  134.1 10.0 all-gather.14
  199.4 11.3 reduce-scatter.12
  214.4 62.1 all-gather.20
  278.7 9.9 all-gather.18
  292.3 61.8 all-gather.22
  361.6 8.7 reduce-scatter.14
  375.7 12.5 all-gather.24
  438.1 11.3 reduce-scatter.16
  454.3 12.6 all-gather.26
  468.4 12.5 all-gather.28
  515.0 11.3 reduce-scatter.20
  528.5 11.4 reduce-scatter.18
  546.8 12.5 all-gather.30
  598.9 11.3 reduce-scatter.22
  619.6 12.5 all-gather.32
  650.9 11.3 reduce-scatter.24
  669.2 12.5 all-gather.34
  728.6 11.3 reduce-scatter.26
  760.6 134.6 reduce-scatter.30
  897.7 132.5 reduce-scatter.28
  1036.7 357.8 all-reduce.2
where the time goes:
time: 1420 us; the launch traced here: 1410 us
  waiting for transfers between devices  758 us (53%)
  matrix products  224 us (16%)
  blocking collectives  168 us (12%)
  local copies, waits for them, and re-layouts  158 us (11%)
  other arithmetic  83.7 us (6%)
  between operations  16.1 us (1%)
    psum x1, waiting for transfers between devices, per_device(): lax.psum((qkv_total, out_total, up_total, bias_total, down_total), 'dp')  363 us
    reduce_scatter x1, waiting for transfers between devices, per_device(): lax.psum_scatter(time_total, ('dp', 'tensor'), scatter_dimension=1, tiled...  132 us
    unnamed x299, local copies, waits for them, and re-layouts  69.1 us
    dot_general x2, matrix products, per_device(): jnp.dot(ffn_all, up_full[layer_index], preferred_element_type=jnp.float32)  65.9 us
    unnamed x24, waiting for transfers between devices  61.6 us
    all_gather x1, blocking collectives, per_device(): lax.all_gather(norm_params, ('dp', 'tensor'), axis=2, tiled=True)  44.7 us
    psum x1, blocking collectives, per_device(): lax.psum((qkv_total, out_total, up_total, bias_total, down_total), 'dp')  42.7 us
    all_gather x1, blocking collectives, per_device(): lax.all_gather(up_bias.astype(jnp.bfloat16), 'dp', axis=2, tiled=True)  41.4 us
  transfers between devices with their start and end apart: 23, of which 20 were waited for; matrix products, arithmetic and copies ran while one was open for 12% of the time, Pallas kernels for 0%

commit v1 on v0

v1 whole, which is shorter than its diff:
```python
import functools
import math

import jax
import jax.numpy as jnp
import numpy as np
from jax import lax
from jax.experimental import pallas as pl
from jax.experimental.pallas import tpu as pltpu
from jax.sharding import PartitionSpec as P

HEAD_DIM = 64
LENGTH = 256
LAYERS = 2
STEP = 8
GROUPS = 16
MESH = pl.DeviceIdType.MESH
F32 = jnp.float32
BF16 = jnp.bfloat16

beta_first = 0.5
beta_second = 0.5
learn_rate = 0.1
norm_rate = 0.4
weight_decay = 0.01
adam_eps = 1e-08
norm_eps = 1e-05


def nn(a, b):
    return lax.dot_general(a, b, (((1,), (0,)), ((), ())), preferred_element_type=F32)


def nt(a, b):
    return lax.dot_general(a, b, (((1,), (1,)), ((), ())), preferred_element_type=F32)


def tn(a, b):
    return lax.dot_general(a, b, (((0,), (0,)), ((), ())), preferred_element_type=F32)


def normalize(values):
    center = values - jnp.mean(values, -1, keepdims=True)
    inverse = lax.rsqrt(jnp.mean(center * center, -1, keepdims=True) + norm_eps)
    return center * inverse, inverse


def fold_rows(values):
    rows, cols = values.shape
    return jnp.sum(values.reshape(rows // 8, 8, cols), 0)


def gelu_and_slope(x):
    size = jnp.abs(x)
    denom = 1.0 + (0.3275911 / math.sqrt(2.0)) * size
    t = pl.reciprocal(denom, approx=True)
    t = t * (2.0 - denom * t)
    bell = jnp.exp(x * x * -0.5)
    poly = 0.5 * 1.061405429
    poly = poly * t + 0.5 * -1.453152027
    poly = poly * t + 0.5 * 1.421413741
    poly = poly * t + 0.5 * -0.284496736
    poly = poly * t + 0.5 * 0.254829592
    tail = poly * t * bell
    below = jnp.where(x >= 0.0, 1.0 - tail, tail)
    return x * below, below + x * bell * (1.0 / math.sqrt(2.0 * math.pi))


class Place:
    def __init__(self, rep):
        dp = lax.axis_index("dp")
        self.rep = rep
        self.copy = dp % rep
        self.group = dp // rep
        self.t = lax.axis_index("tensor")
        self.z = self.group // 4
        self.yx = self.group % 4
        x, y = self.yx % 2, self.yx // 2
        self.yx_x = self.yx + 1 - 2 * x
        self.yx_y = self.yx + 2 - 4 * y
        self.yx_d = 3 - self.yx
        self.cols = pl.ds(pl.multiple_of(self.t * 256, 256), 256)
        self.other_cols = pl.ds(pl.multiple_of((1 - self.t) * 256, 256), 256)

    def device(self, z, yx, t):
        return ((z * 4 + yx) * self.rep + self.copy, t)

    def z_ahead(self, k):
        return (self.z + k) % 4

    @property
    def partners(self):
        return [self.device(self.z_ahead(k), self.yx, self.t) for k in (1, 2, 3)] + [
            self.device(self.z, self.yx_x, self.t),
            self.device(self.z, self.yx_y, self.t),
            self.device(self.z, self.yx, 1 - self.t),
        ]

    def greet(self):
        barrier = pltpu.get_barrier_semaphore()
        for partner in self.partners:
            pl.semaphore_signal(barrier, inc=1, device_id=partner, device_id_type=MESH)
        pl.semaphore_wait(barrier, len(self.partners))


class Gather:
    def __init__(self, place, view, core_view, send, recv):
        self.place, self.view, self.core_view, self.send, self.recv = place, view, core_view, send, recv
        self.copies = {}

    def start(self, slot, ref, device):
        copy = pltpu.make_async_remote_copy(
            src_ref=ref, dst_ref=ref, send_sem=self.send.at[slot], recv_sem=self.recv.at[slot],
            device_id=device, device_id_type=MESH,
        )
        copy.start()
        self.copies[slot] = copy

    def step(self, number):
        p = self.place
        if number == 0:
            for k in (1, 2, 3):
                self.start(k - 1, self.view(p.z, p.yx), p.device(p.z_ahead(k), p.yx, p.t))
        elif number == 1:
            for slot in (0, 1, 2):
                self.copies[slot].wait_recv()
            column = self.view(slice(None), p.yx)
            self.start(3, column, p.device(p.z, p.yx_x, p.t))
            self.start(4, column, p.device(p.z, p.yx_y, p.t))
        elif number == 2:
            self.copies[3].wait_recv()
            self.start(5, self.view(pl.ds(0, 2), p.yx_x), p.device(p.z, p.yx_y, p.t))
            self.copies[4].wait_recv()
            self.start(6, self.view(pl.ds(2, 2), p.yx_y), p.device(p.z, p.yx_x, p.t))
        elif number == 3:
            self.copies[5].wait_recv()
            self.copies[6].wait_recv()
            self.start(7, self.core_view(), p.device(p.z, p.yx, 1 - p.t))
        elif number == 4:
            self.copies[7].wait_recv()

    def finish(self):
        for copy in self.copies.values():
            copy.wait_send()


GATHER_PIECES = 10
GATHER_GROUPS = ((0, 3), (3, 1), (4, 4), (8, 4))


def forward_kernel(
    rep,
    steps_ref, freq_ref, x_ref, qkv_ref, out_ref, up_ref, down_ref, time_ref, norm_ref, bias_ref,
    w_out, small_out, feats_out, entry_out, middle_out, qkv_out, probs_out, attn_out, hidden_out, slope_out, act_out,
    w, tw, nb, norms, bias, shifts, stream, attn, send, recv, keep_sem,
):
    place = Place(rep)
    z, yx, t = place.z, place.yx, place.t
    items = stream.shape[0] // LENGTH

    for layer in range(LAYERS):
        for slot in range(3):
            w[layer, slot, z, yx, :, place.cols] = qkv_ref[layer, slot].astype(BF16)
        w[layer, 3, z, yx, :, place.cols] = out_ref[layer].astype(BF16)
        for part in range(4):
            own = slice(part * 256, (part + 1) * 256)
            w[layer, 4 + part, z, yx, :, place.cols] = up_ref[layer, :, own].astype(BF16)
            w[layer, 8 + part, z, yx, :, place.cols] = down_ref[layer, :, own].astype(BF16)
        tw[layer, z, yx, t] = time_ref[layer].astype(BF16)
    nb[z, yx, t, 0:16] = norm_ref[...]
    nb[z, yx, t, 16:32] = bias_ref[...]
    place.greet()

    pieces = [
        Gather(place, lambda a, b: nb.at[a, b, t], lambda: nb.at[:, :, t], send.at[0], recv.at[0]),
        Gather(place, lambda a, b: tw.at[:, a, b, t], lambda: tw.at[:, :, :, t], send.at[1], recv.at[1]),
    ]
    for layer in range(LAYERS):
        for first, count in GATHER_GROUPS:
            span = w.at[layer, pl.ds(first, count)]
            number = len(pieces)
            pieces.append(
                Gather(
                    place,
                    lambda a, b, span=span: span.at[:, a, b, :, place.cols],
                    lambda span=span: span.at[:, :, :, :, place.cols],
                    send.at[number],
                    recv.at[number],
                )
            )
    for piece in pieces:
        piece.step(0)
    events = []
    for turn in range(len(pieces) + 3):
        for number in (1, 2, 3, 4):
            index = turn - (number - 1)
            if 0 <= index < len(pieces):
                events.append((index, number))
    position = [0]

    def run_until(index):
        while position[0] < len(events):
            piece, number = events[position[0]]
            pieces[piece].step(number)
            position[0] += 1
            if (piece, number) == (index, 4):
                break

    rows = lax.broadcasted_iota(jnp.int32, (8, 256), 0)
    angles = jnp.zeros((8, 256), F32)
    for item in range(items):
        step_value = steps_ref[t * items + item].astype(F32)
        angles = jnp.where(rows == item, step_value * freq_ref[0:1, :], angles)
    live = rows < items
    feats = jnp.concatenate(
        [jnp.where(live, jnp.sin(angles), 0.0), jnp.where(live, jnp.cos(angles), 0.0)], 1
    )
    feats_out[...] = feats
    feats_high = feats.astype(BF16)
    feats_low = (feats - feats_high.astype(F32)).astype(BF16)

    run_until(2)
    for zz in range(4):
        total = jnp.zeros((16, 128), F32)
        for part in range(8):
            total = total + nb[zz, part // 2, part % 2, 0:16]
        norms[:, zz * 128 : (zz + 1) * 128] = total
    for core in range(2):
        total = jnp.zeros((16, 128), F32)
        for part in range(16):
            total = total + nb[part // 4, part % 4, core, 16:32]
        total = total.astype(BF16).astype(F32)
        for layer in range(LAYERS):
            for part in range(4):
                for half in range(2):
                    row = layer * 8 + part * 2 + half
                    col = core * 256 + half * 128
                    bias[layer * 4 + part : layer * 4 + part + 1, col : col + 128] = total[row : row + 1]
    small_out[...] = norms[...]
    for layer in range(LAYERS):
        table = tw[layer].reshape(512, 512)
        shifts[layer * 8 : (layer + 1) * 8] = nn(feats_high, table) + nn(feats_low, table)

    lane = lax.broadcasted_iota(jnp.int32, (1, 128), 1)
    even = lane < HEAD_DIM
    even_mask = jnp.where(even, 1.0, 0.0).astype(BF16)
    odd_mask = jnp.where(even, 0.0, 1.0).astype(BF16)

    def attention_phase(layer):
        def body(*refs):
            if layer == 0:
                x_blk, *refs = refs
            entry_blk, qkv_blk, probs_blk, attn_blk = refs
            item = pl.program_id(0)
            here = pl.ds(pl.multiple_of(item * LENGTH, LENGTH), LENGTH)
            start = x_blk[...].astype(F32) if layer == 0 else stream[here]
            entry = start + shifts[pl.ds(layer * 8 + item, 1)]
            entry_blk[...] = entry
            stream[here] = entry
            hat, _ = normalize(entry)
            normed = (hat * norms[layer * 5 : layer * 5 + 1] + norms[layer * 5 + 1 : layer * 5 + 2]).astype(BF16)
            for slot in range(3):
                projected = nn(normed, w[layer, slot].reshape(512, 512)).astype(BF16)
                if slot == 0:
                    projected = projected * jnp.asarray(HEAD_DIM**-0.5, BF16)
                qkv_blk[:, slot * 512 : (slot + 1) * 512] = projected
            for pair in range(4):
                span = slice(pair * 128, (pair + 1) * 128)
                query = qkv_blk[:, span]
                key = qkv_blk[:, 512 + pair * 128 : 512 + (pair + 1) * 128]
                value = qkv_blk[:, 1024 + pair * 128 : 1024 + (pair + 1) * 128]
                mixed = []
                for side, mask in enumerate((even_mask, odd_mask)):
                    scores = nt(query * mask, key)
                    weight = jnp.exp(scores - jnp.max(scores, -1, keepdims=True))
                    probs = (weight * (1.0 / jnp.sum(weight, -1, keepdims=True))).astype(BF16)
                    probs_blk[0, pair * 2 + side] = probs
                    mixed.append(nn(probs, value))
                joined = jnp.where(even, mixed[0], mixed[1]).astype(BF16)
                attn_blk[:, span] = joined
                attn[here, span] = joined

        wide = lambda cols: pl.BlockSpec((LENGTH, cols), lambda i: (i, 0))
        pipeline = pltpu.emit_pipeline(
            body,
            grid=(items,),
            in_specs=[wide(512)] if layer == 0 else [],
            out_specs=[wide(512), wide(1536), pl.BlockSpec((1, 8, 256, 256), lambda i: (i, 0, 0, 0)), wide(512)],
        )
        ins = [x_ref] if layer == 0 else []
        pipeline(*ins, entry_out.at[layer], qkv_out.at[layer], probs_out.at[layer], attn_out.at[layer])

    def feed_phase(layer):
        def body(*refs):
            middle_blk, hidden_blk, slope_blk, *rest = refs
            item = pl.program_id(0)
            here = pl.ds(pl.multiple_of(item * LENGTH, LENGTH), LENGTH)
            middle = stream[here] + nt(attn[here], w[layer, 3].reshape(512, 512))
            middle_blk[...] = middle
            hat, _ = normalize(middle)
            normed = (hat * norms[layer * 5 + 2 : layer * 5 + 3] + norms[layer * 5 + 3 : layer * 5 + 4]).astype(BF16)
            total = middle + norms[layer * 5 + 4 : layer * 5 + 5]
            for part in range(4):
                row = layer * 4 + part
                span = slice(part * 512, (part + 1) * 512)
                pre = nn(normed, w[layer, 4 + part].reshape(512, 512)) + bias[row : row + 1]
                hidden, slope = gelu_and_slope(pre)
                hidden = hidden.astype(BF16)
                hidden_blk[:, span] = hidden
                slope_blk[:, span] = slope.astype(BF16)
                total = total + nt(hidden, w[layer, 8 + part].reshape(512, 512))
            if layer == LAYERS - 1:
                rest[0][...] = total.astype(BF16)
            else:
                stream[here] = total

        wide = lambda cols: pl.BlockSpec((LENGTH, cols), lambda i: (i, 0))
        last = layer == LAYERS - 1
        pipeline = pltpu.emit_pipeline(
            body,
            grid=(items,),
            in_specs=[],
            out_specs=[wide(512), wide(2048), wide(2048)] + ([wide(512)] if last else []),
        )
        pipeline(middle_out.at[layer], hidden_out.at[layer], slope_out.at[layer], *([act_out] if last else []))

    keeps = []
    for layer in range(LAYERS):
        run_until(2 + layer * 4)
        with jax.named_scope("attention"):
            attention_phase(layer)
        run_until(5 + layer * 4)
        keep = pltpu.make_async_copy(w.at[layer], w_out.at[layer], keep_sem.at[layer])
        keep.start()
        keeps.append(keep)
        with jax.named_scope("feed"):
            feed_phase(layer)
    for piece in pieces:
        piece.finish()
    for keep in keeps:
        keep.wait()


def forward_call(rep, rows, steps, freq, x, qkv, out, up, down, time, norm, bias):
    items = rows // LENGTH
    hbm = pl.BlockSpec(memory_space=pl.ANY)
    vmem = pl.BlockSpec(memory_space=pltpu.VMEM)
    smem = pl.BlockSpec(memory_space=pltpu.SMEM)
    shape = jax.ShapeDtypeStruct
    return pl.pallas_call(
        functools.partial(forward_kernel, rep),
        name="forward",
        in_specs=[smem, vmem, hbm] + [vmem] * 7,
        out_shape=[
            shape((LAYERS, 12, 4, 4, 32, 512), BF16),
            shape((16, 512), F32),
            shape((8, 512), F32),
            shape((LAYERS, rows, 512), F32),
            shape((LAYERS, rows, 512), F32),
            shape((LAYERS, rows, 1536), BF16),
            shape((LAYERS, items, 8, 256, 256), BF16),
            shape((LAYERS, rows, 512), BF16),
            shape((LAYERS, rows, 2048), BF16),
            shape((LAYERS, rows, 2048), BF16),
            shape((rows, 512), BF16),
        ],
        out_specs=[hbm, vmem, vmem] + [hbm] * 8,
        scratch_shapes=[
            pltpu.VMEM((LAYERS, 12, 4, 4, 32, 512), BF16),
            pltpu.VMEM((LAYERS, 4, 4, 2, 16, 512), BF16),
            pltpu.VMEM((4, 4, 2, 32, 128), F32),
            pltpu.VMEM((16, 512), F32),
            pltpu.VMEM((8, 512), F32),
            pltpu.VMEM((16, 512), F32),
            pltpu.VMEM((rows, 512), F32),
            pltpu.VMEM((rows, 512), BF16),
            pltpu.SemaphoreType.DMA((GATHER_PIECES, 8)),
            pltpu.SemaphoreType.DMA((GATHER_PIECES, 8)),
            pltpu.SemaphoreType.DMA((LAYERS,)),
        ],
        compiler_params=pltpu.CompilerParams(collective_id=1, has_side_effects=True, vmem_limit_bytes=56 << 20),
    )(steps, freq, x, qkv, out, up, down, time, norm, bias)


class Scatter:
    def __init__(self, place, grads, received, total, groups, send, recv):
        self.place, self.grads, self.received, self.total = place, grads, received, total
        self.first, self.count = groups
        self.span = pl.ds(*groups)
        self.send, self.recv = send, recv
        self.copies = {}

    def start(self, slot, src, dst, device):
        copy = pltpu.make_async_remote_copy(
            src_ref=src, dst_ref=dst, send_sem=self.send.at[slot], recv_sem=self.recv.at[slot],
            device_id=device, device_id_type=MESH,
        )
        copy.start()
        self.copies[slot] = copy

    def add(self, where, terms):
        def one(group, carry):
            ref = self.grads.at[(group,) + where]
            value = ref[...].astype(F32)
            for term in terms:
                value = value + term[group].astype(F32)
            ref[...] = value.astype(BF16)
            return carry

        lax.fori_loop(self.first, self.first + self.count, one, 0)

    def step(self, number):
        p, span = self.place, self.span
        core, diag_y, diag_x, col_x, col_y, along = self.received
        every = slice(None)
        if number == 0:
            self.start(0, self.grads.at[span, :, :, :, p.other_cols], core.at[span], p.device(p.z, p.yx, 1 - p.t))
        elif number == 1:
            self.copies[0].wait_recv()
            self.add((every, every, every, p.cols), [core])
            low = self.grads.at[span, pl.ds(0, 2), p.yx_d, :, p.cols]
            high = self.grads.at[span, pl.ds(2, 2), p.yx_d, :, p.cols]
            self.start(1, low, diag_y.at[span], p.device(p.z, p.yx_y, p.t))
            self.start(2, high, diag_x.at[span], p.device(p.z, p.yx_x, p.t))
        elif number == 2:
            self.copies[1].wait_recv()
            self.add((pl.ds(0, 2), p.yx_x, every, p.cols), [diag_y])
            self.start(3, self.grads.at[span, :, p.yx_x, :, p.cols], col_x.at[span], p.device(p.z, p.yx_x, p.t))
            self.copies[2].wait_recv()
            self.add((pl.ds(2, 2), p.yx_y, every, p.cols), [diag_x])
            self.start(4, self.grads.at[span, :, p.yx_y, :, p.cols], col_y.at[span], p.device(p.z, p.yx_y, p.t))
        elif number == 3:
            self.copies[3].wait_recv()
            self.copies[4].wait_recv()
            self.add((every, p.yx, every, p.cols), [col_x, col_y])
            for k in (1, 2, 3):
                there = p.z_ahead(k)
                self.start(
                    4 + k, self.grads.at[span, there, p.yx, :, p.cols], along.at[k - 1, span],
                    p.device(there, p.yx, p.t),
                )
        elif number == 4:
            for k in (1, 2, 3):
                self.copies[4 + k].wait_recv()

            def one(group, carry):
                value = self.grads[group, p.z, p.yx, :, p.cols].astype(F32)
                for k in range(3):
                    value = value + along[k, group].astype(F32)
                self.total[group] = value
                return carry

            lax.fori_loop(self.first, self.first + self.count, one, 0)

    def finish(self):
        for copy in self.copies.values():
            copy.wait_send()


class SmallSum:
    def __init__(self, place, sums, received, total, send, recv):
        self.place, self.sums, self.received, self.total = place, sums, received, total
        self.send, self.recv = send, recv
        self.copies = {}

    def start(self, slot, stage, device):
        copy = pltpu.make_async_remote_copy(
            src_ref=self.sums.at[stage], dst_ref=self.received.at[slot], send_sem=self.send.at[slot],
            recv_sem=self.recv.at[slot], device_id=device, device_id_type=MESH,
        )
        copy.start()
        self.copies[slot] = copy

    def step(self, number):
        p = self.place
        if number > 0:
            slots = (0,) if number == 1 else (1,) if number == 2 else (2,) if number == 3 else (3, 4, 5)
            value = self.sums[number - 1]
            for slot in slots:
                self.copies[slot].wait_recv()
                value = value + self.received[slot]
            if number < 4:
                self.sums[number] = value
            else:
                self.total[...] = value
        if number == 0:
            self.start(0, 0, p.device(p.z, p.yx, 1 - p.t))
        elif number == 1:
            self.start(1, 1, p.device(p.z, p.yx_x, p.t))
        elif number == 2:
            self.start(2, 2, p.device(p.z, p.yx_y, p.t))
        elif number == 3:
            for k in (1, 2, 3):
                self.start(2 + k, 3, p.device(p.z_ahead(k), p.yx, p.t))

    def finish(self):
        for copy in self.copies.values():
            copy.wait_send()


GRAD_GROUPS = 13
SCATTER_PIECES = ((4, 4), (8, 4), (3, 1), (0, 3), (12, 1))


def backward_kernel(
    rep,
    scale_ref, small_ref, feats_ref, cot_ref, w_in, entry_in, middle_in, qkv_in, probs_in, attn_in, hidden_in, slope_in,
    grad_out, total_out, sums_out, time_out,
    w, gx, dattn, du, hidden, attn, n1t, n2t, gdt, got, dqkv, grads, item_grad, acc, acc_bias,
    r_core, r_dy, r_dx, r_x, r_y, r_z, sums, r_sums, r_time,
    w_sem, in_sem, send, recv, small_send, small_recv, time_send, time_recv,
):
    place = Place(rep)
    t = place.t
    rows = gx.shape[0]
    items = rows // LENGTH
    wide = lambda cols: pl.BlockSpec((LENGTH, cols), lambda i: (i, 0))
    lane = lax.broadcasted_iota(jnp.int32, (1, 128), 1)
    even = lane < HEAD_DIM
    even_mask = jnp.where(even, 1.0, 0.0).astype(BF16)
    odd_mask = jnp.where(even, 0.0, 1.0).astype(BF16)

    def load_weights(layer):
        copies = []
        for number, (first, count) in enumerate(((3, 9), (0, 3))):
            copy = pltpu.make_async_copy(
                w_in.at[layer, pl.ds(first, count)], w.at[pl.ds(first, count)], w_sem.at[layer, number]
            )
            copies.append(copy)
        return copies

    def load_stash(layer):
        return [
            pltpu.make_async_copy(hidden_in.at[layer], hidden, in_sem.at[layer, 0]),
            pltpu.make_async_copy(attn_in.at[layer], attn, in_sem.at[layer, 1]),
        ]

    def norm_back(hat, inverse, dy, layer, row, here):
        acc[row] += fold_rows(dy * hat)
        acc[row + 1] += fold_rows(dy)
        scaled = dy * small_ref[layer * 5 + row : layer * 5 + row + 1]
        mean = jnp.mean(scaled, -1, keepdims=True)
        along = jnp.mean(scaled * hat, -1, keepdims=True)
        return inverse * (scaled - mean - hat * along)

    def feed_phase(layer):
        last = layer == LAYERS - 1

        def body(*refs):
            middle_blk, slope_blk, *rest = refs
            item = pl.program_id(0)
            here = pl.ds(pl.multiple_of(item * LENGTH, LENGTH), LENGTH)
            if last:
                grad = rest[0][...].astype(F32) * scale_ref[t * items + item]
            else:
                grad = gx[here]
            acc[4] += fold_rows(grad)
            low = grad.astype(BF16)
            gdt[:, here] = low.T
            back = jnp.zeros((LENGTH, 512), F32)
            for part in range(4):
                span = slice(part * 512, (part + 1) * 512)
                dh = nn(low, w[8 + part].reshape(512, 512))
                pre_grad = (dh * slope_blk[:, span].astype(F32)).astype(BF16)
                du[here, span] = pre_grad
                acc_bias[part] += fold_rows(pre_grad.astype(F32))
                back = back + nt(pre_grad, w[4 + part].reshape(512, 512))
            hat, inverse = normalize(middle_blk[...])
            normed = hat * small_ref[layer * 5 + 2 : layer * 5 + 3] + small_ref[layer * 5 + 3 : layer * 5 + 4]
            n2t[:, here] = normed.astype(BF16).T
            grad = grad + norm_back(hat, inverse, back, layer, 2, here)
            gx[here] = grad
            low = grad.astype(BF16)
            got[:, here] = low.T
            dattn[here] = nn(low, w[3].reshape(512, 512)).astype(BF16)

        pipeline = pltpu.emit_pipeline(
            body, grid=(items,), in_specs=[wide(512), wide(2048)] + ([wide(512)] if last else [])
        )
        pipeline(middle_in.at[layer], slope_in.at[layer], *([cot_ref] if last else []))

    def attention_phase(layer):
        def body(*refs):
            entry_blk, qkv_blk, probs_blk, *rest = refs
            item = pl.program_id(0)
            here = pl.ds(pl.multiple_of(item * LENGTH, LENGTH), LENGTH)
            for pair in range(4):
                span = slice(pair * 128, (pair + 1) * 128)
                query = qkv_blk[:, span]
                key = qkv_blk[:, 512 + pair * 128 : 512 + (pair + 1) * 128]
                value = qkv_blk[:, 1024 + pair * 128 : 1024 + (pair + 1) * 128]
                back = dattn[here, span]
                found = []
                for side, mask in enumerate((even_mask, odd_mask)):
                    probs = probs_blk[0, pair * 2 + side]
                    dprobs = nt(back * mask, value)
                    wide_probs = probs.astype(F32)
                    delta = jnp.sum(wide_probs * dprobs, -1, keepdims=True)
                    dscores = (wide_probs * (dprobs - delta)).astype(BF16)
                    found.append((nn(dscores, key), tn(dscores, query), tn(probs, back)))
                dq, dk, dv = [jnp.where(even, found[0][i], found[1][i]) for i in range(3)]
                dqkv[here, span] = (dq * HEAD_DIM**-0.5).astype(BF16)
                dqkv[here, 512 + pair * 128 : 512 + (pair + 1) * 128] = dk.astype(BF16)
                dqkv[here, 1024 + pair * 128 : 1024 + (pair + 1) * 128] = dv.astype(BF16)
            back = jnp.zeros((LENGTH, 512), F32)
            for slot in range(3):
                back = back + nt(dqkv[here, slot * 512 : (slot + 1) * 512], w[slot].reshape(512, 512))
            hat, inverse = normalize(entry_blk[...])
            normed = hat * small_ref[layer * 5 : layer * 5 + 1] + small_ref[layer * 5 + 1 : layer * 5 + 2]
            n1t[:, here] = normed.astype(BF16).T
            grad = gx[here] + norm_back(hat, inverse, back, layer, 0, here)
            item_grad[pl.ds(item, 1)] = jnp.sum(grad, 0, keepdims=True)
            if layer == 0:
                rest[0][...] = grad.astype(BF16)
            else:
                gx[here] = grad

        pipeline = pltpu.emit_pipeline(
            body,
            grid=(items,),
            in_specs=[wide(512), wide(1536), pl.BlockSpec((1, 8, 256, 256), lambda i: (i, 0, 0, 0))],
            out_specs=[wide(512)] if layer == 0 else [],
        )
        pipeline(entry_in.at[layer], qkv_in.at[layer], probs_in.at[layer], *([grad_out] if layer == 0 else []))

    def weight_grad(left, right, first, count):
        def one(part, carry):
            span = pl.ds(pl.multiple_of(part * 512, 512), 512)
            grads[first + part] = nn(left[...], right[:, span]).astype(BF16).reshape(4, 4, 32, 512)
            return carry

        lax.fori_loop(0, count, one, 0)

    scatters, smalls = [], []
    for layer in range(LAYERS):
        received = [r.at[layer] for r in (r_core, r_dy, r_dx, r_x, r_y, r_z)]
        scatters.append(
            [
                Scatter(place, grads, received, total_out.at[layer], groups, send.at[layer, i], recv.at[layer, i])
                for i, groups in enumerate(SCATTER_PIECES)
            ]
        )
        smalls.append(
            SmallSum(place, sums.at[layer], r_sums.at[layer], sums_out.at[layer], small_send.at[layer], small_recv.at[layer])
        )

    order = [LAYERS - 1 - i for i in range(LAYERS)]
    weights = {order[0]: load_weights(order[0])}
    stash = {order[0]: load_stash(order[0])}
    for copy in weights[order[0]] + stash[order[0]]:
        copy.start()
    item_grad[...] = jnp.zeros(item_grad.shape, F32)
    place.greet()

    for turn, layer in enumerate(order):
        acc[...] = jnp.zeros(acc.shape, F32)
        acc_bias[...] = jnp.zeros(acc_bias.shape, F32)
        weights[layer][0].wait()
        with jax.named_scope("feed_back"):
            feed_phase(layer)
        stash[layer][0].wait()
        stash[layer][1].wait()
        weights[layer][1].wait()
        if turn > 0:
            for piece in scatters[order[turn - 1]]:
                piece.finish()
        with jax.named_scope("feed_grads"):
            weight_grad(n2t, du, 4, 4)
            scatters[layer][0].step(0)
            weight_grad(gdt, hidden, 8, 4)
            scatters[layer][1].step(0)
            weight_grad(got, attn, 3, 1)
            scatters[layer][2].step(0)
        with jax.named_scope("attention_back"):
            attention_phase(layer)
        if turn + 1 < LAYERS:
            after = order[turn + 1]
            weights[after] = load_weights(after)
            stash[after] = load_stash(after)
            for copy in weights[after] + stash[after]:
                copy.start()
        with jax.named_scope("attention_grads"):
            weight_grad(n1t, dqkv, 0, 3)
            scatters[layer][3].step(0)
            spread = lax.dot_general(
                feats_ref[...], item_grad[...], (((0,), (0,)), ((), ())),
                precision=lax.Precision.HIGHEST, preferred_element_type=F32,
            )
            grads[12] = spread.astype(BF16).reshape(4, 4, 32, 512)
            scatters[layer][4].step(0)
            for row in range(5):
                sums[layer, 0, row : row + 1] = jnp.sum(acc[row], 0, keepdims=True)
            for part in range(4):
                sums[layer, 0, 5 + part : 6 + part] = jnp.sum(acc_bias[part], 0, keepdims=True)
            sums[layer, 0, 9:16] = jnp.zeros((7, 512), F32)
            smalls[layer].step(0)
        with jax.named_scope("scatter"):
            for number in (1, 2, 3, 4):
                for piece in scatters[layer]:
                    piece.step(number)
                smalls[layer].step(number)

    swaps = []
    for layer in range(LAYERS):
        swap = pltpu.make_async_remote_copy(
            src_ref=total_out.at[layer, 12, pl.ds(pl.multiple_of((1 - t) * 16, 16), 16)],
            dst_ref=r_time.at[layer], send_sem=time_send.at[layer], recv_sem=time_recv.at[layer],
            device_id=place.device(place.z, place.yx, 1 - t), device_id_type=MESH,
        )
        swap.start()
        swaps.append(swap)
    for layer in range(LAYERS):
        swaps[layer].wait()
        time_out[layer, :, place.cols] = total_out[layer, 12, pl.ds(pl.multiple_of(t * 16, 16), 16)]
        time_out[layer, :, place.other_cols] = r_time[layer]
    for piece in scatters[order[-1]]:
        piece.finish()
    for piece in smalls:
        piece.finish()


def backward_call(rep, rows, scale, small, feats, cot, w, entry, middle, qkv, probs, attn, hidden, slope):
    items = rows // LENGTH
    hbm = pl.BlockSpec(memory_space=pl.ANY)
    vmem = pl.BlockSpec(memory_space=pltpu.VMEM)
    smem = pl.BlockSpec(memory_space=pltpu.SMEM)
    shape = jax.ShapeDtypeStruct
    pieces = len(SCATTER_PIECES)
    dma = pltpu.SemaphoreType.DMA
    return pl.pallas_call(
        functools.partial(backward_kernel, rep),
        name="backward",
        in_specs=[smem, vmem, vmem] + [hbm] * 9,
        out_shape=[
            shape((rows, 512), BF16),
            shape((LAYERS, GRAD_GROUPS, 32, 256), F32),
            shape((LAYERS, 16, 512), F32),
            shape((LAYERS, 16, 512), F32),
        ],
        out_specs=[hbm, vmem, vmem, vmem],
        scratch_shapes=[
            pltpu.VMEM((12, 4, 4, 32, 512), BF16),
            pltpu.VMEM((rows, 512), F32),
            pltpu.VMEM((rows, 512), BF16),
            pltpu.VMEM((rows, 2048), BF16),
            pltpu.VMEM((rows, 2048), BF16),
            pltpu.VMEM((rows, 512), BF16),
            pltpu.VMEM((512, rows), BF16),
            pltpu.VMEM((512, rows), BF16),
            pltpu.VMEM((512, rows), BF16),
            pltpu.VMEM((512, rows), BF16),
            pltpu.VMEM((rows, 1536), BF16),
            pltpu.VMEM((GRAD_GROUPS, 4, 4, 32, 512), BF16),
            pltpu.VMEM((8, 512), F32),
            pltpu.VMEM((5, 8, 512), F32),
            pltpu.VMEM((4, 8, 512), F32),
            pltpu.VMEM((LAYERS, GRAD_GROUPS, 4, 4, 32, 256), BF16),
            pltpu.VMEM((LAYERS, GRAD_GROUPS, 2, 32, 256), BF16),
            pltpu.VMEM((LAYERS, GRAD_GROUPS, 2, 32, 256), BF16),
            pltpu.VMEM((LAYERS, GRAD_GROUPS, 4, 32, 256), BF16),
            pltpu.VMEM((LAYERS, GRAD_GROUPS, 4, 32, 256), BF16),
            pltpu.VMEM((LAYERS, 3, GRAD_GROUPS, 32, 256), BF16),
            pltpu.VMEM((LAYERS, 4, 16, 512), F32),
            pltpu.VMEM((LAYERS, 6, 16, 512), F32),
            pltpu.VMEM((LAYERS, 16, 256), F32),
            dma((LAYERS, 2)),
            dma((LAYERS, 2)),
            dma((LAYERS, pieces, 8)),
            dma((LAYERS, pieces, 8)),
            dma((LAYERS, 6)),
            dma((LAYERS, 6)),
            dma((LAYERS,)),
            dma((LAYERS,)),
        ],
        compiler_params=pltpu.CompilerParams(collective_id=2, has_side_effects=True, vmem_limit_bytes=62 << 20),
    )(scale, small, feats, cot, w, entry, middle, qkv, probs, attn, hidden, slope)


def adamw(weight, gradient, first_moment, second_moment, rate):
    first_new = beta_first * first_moment + (1.0 - beta_first) * gradient
    second_new = beta_second * second_moment + (1.0 - beta_second) * gradient * gradient
    first_corr = first_new / (1.0 - beta_first**STEP)
    second_corr = second_new / (1.0 - beta_second**STEP)
    weight_new = weight - rate * (first_corr / (jnp.sqrt(second_corr) + adam_eps) + weight_decay * weight)
    return (weight_new, first_new, second_new)


def per_device(
    rep,
    inputs, cotangent, timesteps, item_scale,
    qkv_weight, qkv_first, qkv_second,
    out_weight, out_first, out_second,
    up_weight, up_first, up_second,
    up_bias, bias_first, bias_second,
    down_weight, down_first, down_second,
    norm_params, norm_first, norm_second,
    time_weight, time_first, time_second,
):
    rows = inputs.shape[0]
    dp, t = lax.axis_index("dp"), lax.axis_index("tensor")
    group = dp // rep
    qkv, out, up, down, bias = qkv_weight, out_weight, up_weight, down_weight, up_bias
    norm, time = norm_params, time_weight
    teams = None
    if rep > 1:
        size = GROUPS * rep
        teams = [[g * rep + j for j in range(rep)] for g in range(GROUPS)]
        pairs = [[g * rep * 2 + j for j in range(rep * 2)] for g in range(GROUPS)]
        join = lambda v, axis: lax.all_gather(v, "dp", axis=axis, axis_index_groups=teams, tiled=True)
        join_both = lambda v, axis: lax.all_gather(
            v, ("dp", "tensor"), axis=axis, axis_index_groups=pairs, tiled=True
        )
        qkv, out, up, down, bias = join(qkv, 1), join(out, 2), join(up, 1), join(down, 2), join(bias, 2)
        norm, time = join_both(norm, 2), join_both(time, 1)
        norm = lax.dynamic_slice_in_dim(norm, t * 16, 16, 2)
        time = lax.dynamic_slice_in_dim(time, t * 16, 16, 1)

    lane = lax.broadcasted_iota(jnp.int32, (16, 128), 1)
    spot = (group % 4) * 2 + t
    norm_rows = jnp.pad(norm.reshape(10, 16), ((0, 6), (0, 0)))
    norm_block = jnp.where(lane // 16 == spot, jnp.tile(norm_rows, (1, 8)), 0.0)
    bias_block = jnp.where(lane // 8 == group, jnp.tile(bias.reshape(16, 8), (1, 16)), 0.0)
    half_width = 256
    freq = np.exp(-math.log(10000.0) / half_width * np.arange(half_width)).astype(np.float32)
    freq = jnp.asarray(np.broadcast_to(freq, (8, half_width)))

    w, small, feats, entry, middle, qkv_rows, probs, attn, hidden, slope, activations = forward_call(
        rep, rows, timesteps, freq, inputs,
        jnp.transpose(qkv, (0, 2, 1, 3)), jnp.swapaxes(out, 1, 2), up, jnp.swapaxes(down, 1, 2),
        time, norm_block, bias_block,
    )
    input_grad, total, sums, time_grad = backward_call(
        rep, rows, item_scale, small, feats, cotangent, w, entry, middle, qkv_rows, probs, attn, hidden, slope
    )

    qkv_grad = jnp.transpose(total[:, 0:3], (0, 2, 1, 3))
    out_grad = jnp.swapaxes(total[:, 3], 1, 2)
    up_grad = jnp.transpose(total[:, 4:8], (0, 2, 1, 3)).reshape(LAYERS, 32, 1024)
    down_grad = jnp.swapaxes(jnp.transpose(total[:, 8:12], (0, 2, 1, 3)).reshape(LAYERS, 32, 1024), 1, 2)
    norm_sum = sums[:, 0:5]
    bias_sum = sums[:, 5:9].reshape(LAYERS, 4, 2, 2, 128)
    if rep > 1:
        part = lambda v, axis: lax.psum_scatter(
            v, "dp", scatter_dimension=axis, axis_index_groups=teams, tiled=True
        )
        qkv_grad, out_grad, up_grad, down_grad = part(qkv_grad, 1), part(out_grad, 2), part(up_grad, 1), part(down_grad, 2)
        whole = lambda v: lax.psum(v, "dp", axis_index_groups=teams)
        norm_sum, bias_sum = whole(norm_sum), whole(bias_sum)
        time_grad = lax.all_gather(whole(time_grad), "tensor", axis=1, tiled=True)
        width = time_weight.shape[1]
        time_grad = lax.dynamic_slice_in_dim(time_grad, ((dp % rep) * 2 + t) * width, width, 1)
    width = norm_params.shape[2]
    norm_grad = lax.dynamic_slice_in_dim(norm_sum, (dp * 2 + t) * width, width, 2)
    bias_sum = lax.dynamic_index_in_dim(bias_sum, t, 2, keepdims=False).reshape(LAYERS, 8, 128)
    width = up_bias.shape[2]
    bias_grad = lax.dynamic_slice_in_dim(bias_sum, dp * width, width, 2)

    new_qkv = adamw(qkv_weight, qkv_grad, qkv_first, qkv_second, learn_rate)
    new_out = adamw(out_weight, out_grad, out_first, out_second, learn_rate)
    new_up = adamw(up_weight, up_grad, up_first, up_second, learn_rate)
    new_bias = adamw(up_bias, bias_grad, bias_first, bias_second, learn_rate)
    new_down = adamw(down_weight, down_grad, down_first, down_second, learn_rate)
    new_norm = adamw(norm_params, norm_grad, norm_first, norm_second, norm_rate)
    new_time = adamw(time_weight, time_grad, time_first, time_second, learn_rate)
    return (
        activations, input_grad,
        new_qkv[0], new_qkv[1], new_qkv[2][:, :, :2], new_qkv[2][:, :, 2],
        *new_out, *new_up, *new_bias, *new_down, *new_norm, *new_time,
    )


def solution(mesh):
    rep = mesh.shape["dp"] // GROUPS
    shard = P(None, "dp", None, "tensor")
    rows = P(("dp", "tensor"), None)
    trans = P(None, "tensor", "dp")
    flat = P(None, "dp", "tensor")
    norm = P(None, None, ("dp", "tensor"))
    time = P(None, ("dp", "tensor"), None)
    return jax.shard_map(
        functools.partial(per_device, rep),
        mesh=mesh,
        in_specs=(rows, rows, P("dp"), P("dp")) + (shard,) * 3 + (trans,) * 3 + (flat,) * 3 + (trans,) * 6 + (norm,) * 3 + (time,) * 3,
        out_specs=(rows, rows, shard, shard, shard, flat) + (trans,) * 3 + (flat,) * 3 + (trans,) * 6 + (norm,) * 3 + (time,) * 3,
        check_vma=False,
    )
```

time: 1420 us -> 341 us (0.24)
  waiting for transfers between devices: 758 us -> 0 us
  Pallas kernels: 0 us -> 316 us
  matrix products: 224 us -> 0 us
  blocking collectives: 168 us -> 0 us
  local copies, waits for them, and re-layouts: 158 us -> 11 us
  other arithmetic: 83.7 us -> 12.6 us
  between operations: 16.1 us -> 0.87 us
    psum x1 -> x0, waiting for transfers between devices: 363 us -> none  [per_device(): lax.psum((qkv_total, out_total, up_total, bias_total, down_total), 'dp')]
    pallas_call x0 -> x2, Pallas kernels: none -> 316 us  [the longest x1 177 us: backward_call(): pl.pallas_call(functools.partial(backward_kernel, rep), name='backward',...]
    dot_general x40 -> x0, matrix products: 224 us -> none  [the longest x2 65.9 us: per_device(): jnp.dot(ffn_all, up_full[layer_index], preferred_element_type=jnp.float32)]
    reduce_scatter x9 -> x0, waiting for transfers between devices: 199 us -> none  [the longest x1 132 us: per_device(): lax.psum_scatter(time_total, ('dp', 'tensor'), scatter_dimension=1, tiled...]
    all_gather x12 -> x0, waiting for transfers between devices: 135 us -> none  [the longest x1 28.5 us: per_device(): lax.all_gather(down_weight.astype(jnp.bfloat16), 'dp', axis=2, tiled=True)]
    all_gather x3 -> x0, blocking collectives: 125 us -> none  [the longest x1 44.7 us: per_device(): lax.all_gather(norm_params, ('dp', 'tensor'), axis=2, tiled=True)]
    unnamed x299 -> x34, local copies, waits for them, and re-layouts: 69.1 us -> 6.53 us
    unnamed x24 -> x0, waiting for transfers between devices: 61.6 us -> none
  transfers between devices with their start and end apart: 23 -> 0, of which waited for: 20 -> 0; matrix products, arithmetic and copies ran while one was open for 12% -> 0% of each run, Pallas kernels for 0% -> 0%
where the time goes in v1:
time: 341 us
  Pallas kernels  316 us (93%)
  other arithmetic  12.6 us (4%)
  local copies, waits for them, and re-layouts  11 us (3%)
    pallas_call x1, Pallas kernels, backward_call(): pl.pallas_call(functools.partial(backward_kernel, rep), name='backward',...  177 us
    pallas_call x1, Pallas kernels, forward_call(): pl.pallas_call(functools.partial(forward_kernel, rep), name='forward', in...  139 us
    sub x7, other arithmetic, adamw(): weight - rate * (first_corr / (jnp.sqrt(second_corr) + adam_eps) + weight...  11.3 us

profile of v1, /device:TPU:0, one launch (start us, length us, event | category | flops | bytes accessed | tf_op | source)
XLA Modules:
  0.0 340.8 jit_solution(865572217250244373)
XLA Ops:
  0.7 0.7 copy.60
  1.4 0.1 tile.20
  1.5 0.6 fusion.7.norm_ref
  2.1 0.8 copy.73
  2.9 0.1 copy.62
  2.9 0.6 fusion.8.bias_ref
  3.5 1.3 jit_solution_.3.freq_ref
  4.8 139.2 %forward.1 = (bf16[2,12,4,4,32,512]{5,4,3,2,1,0:T(8,128)(2,1)}, f32[16,512]{1,0:T(8,128)}, f32[8,512]{1,0:T(8,128)}, f32[2,1280,512]{2,1,0:T(8,128)}, f32[2,1280...) custom-call(s32[10]{0:T(128)} %steps_ref.1, ...), custom_call_target="tpu_custom_call" | custom-call | tf_op jit(solution)/shard_map/forward/pallas_call | solution.py:350
  144.0 0.0 copy-start.4
  144.0 0.0 copy-start.7
  144.0 0.0 copy-start.8
  144.0 0.0 copy-start.5
  144.0 0.0 copy-start.9
  144.0 0.0 copy-start.2
  144.1 177.1 %backward.1 = (bf16[1280,512]{1,0:T(8,128)(2,1)}, f32[2,13,32,256]{3,2,1,0:T(8,128)}, f32[2,16,512]{2,1,0:T(8,128)}, f32[2,16,512]{2,1,0:T(8,128)}) custom-call(f32[10]{0:T(128)} %scale_ref.1, f32[16,512]{1,0:T(8,128)} %get-tuple-element.40.small_ref, f32[8,512]{1,0:T(8,128)} %get-tuple-element.41.feats_ref, bf16[1280,512]{1,0:T(8,128)(2,1)} %cot_ref.1, ...), custom_call_target="tpu_custom_call" | custom-call | tf_op jit(solution)/shard_map/backward/pallas_call | solution.py:730
  321.2 0.0 copy-start.11
  321.2 0.0 copy-start.3
  321.2 0.0 copy-start.12
  321.2 0.0 copy-start.6
  321.3 0.0 copy-start
  321.3 0.0 copy-done.4
  321.3 0.0 copy-done.7
  321.3 0.0 copy-done.8
  321.3 1.9 multiply_subtract_fusion.2
  323.2 0.0 copy-start.1
  323.2 0.8 copy.69
  324.0 0.6 slice_bitcast_fusion.2
  324.6 0.0 copy-done.5
  324.6 0.0 copy-done.9
  324.6 1.6 multiply_subtract_fusion.4
  326.2 0.0 copy-start.10
  326.2 1.1 slice_bitcast_fusion
  327.3 0.0 copy-done.2
  327.3 2.0 multiply_subtract_fusion.1
  329.4 0.8 slice.29
  330.3 0.0 copy-done.11
  330.3 1.4 multiply_subtract_fusion.6
  331.7 0.0 copy-done.3
  331.7 2.0 multiply_subtract_fusion
  333.8 0.8 slice.31
  334.5 0.0 copy-done.12
  334.5 0.8 multiply_subtract_fusion.5
  335.3 0.6 copy.70
  335.9 0.6 copy.71
  336.5 0.6 copy.72
  337.1 0.0 copy-done.6
  337.1 0.0 copy-done.10
  337.1 1.6 multiply_subtract_fusion.3
  338.7 0.0 copy-done
  338.7 1.1 copy.87
  339.7 0.0 copy-done.1
  339.7 1.1 copy.88
  (12 shorter events, 0.1 us)
Async XLA Ops:
  144.0 177.3 %copy-start.4 = (f32[2,32,3,256]{3,1,2,0:T(8,128)S(1)}, f32[2,32,3,256]{3,1,2,0:T(8,128)}, u32[]{:S(2)}) copy-start(f32[2,32,3,256]{3,1,2,0:T(8,128)} %param.30) | copy-start | bytes 589828
  144.0 177.3 %copy-start.7 = (f32[2,32,3,256]{3,1,2,0:T(8,128)S(1)}, f32[2,32,3,256]{3,1,2,0:T(8,128)}, u32[]{:S(2)}) copy-start(f32[2,32,3,256]{3,1,2,0:T(8,128)} %param.31) | copy-start | bytes 589828
  144.0 177.3 %copy-start.8 = (f32[2,32,3,256]{3,1,2,0:T(8,128)S(1)}, f32[2,32,3,256]{3,1,2,0:T(8,128)}, u32[]{:S(2)}) copy-start(f32[2,32,3,256]{3,1,2,0:T(8,128)} %param.32) | copy-start | bytes 589828
  144.0 180.6 %copy-start.5 = (f32[2,256,32]{1,2,0:T(8,128)S(1)}, f32[2,256,32]{1,2,0:T(8,128)}, u32[]{:S(2)}) copy-start(f32[2,256,32]{1,2,0:T(8,128)} %param.33) | copy-start | bytes 196612
  144.0 180.6 %copy-start.9 = (f32[2,256,32]{1,2,0:T(8,128)S(1)}, f32[2,256,32]{1,2,0:T(8,128)}, u32[]{:S(2)}) copy-start(f32[2,256,32]{1,2,0:T(8,128)} %param.34) | copy-start | bytes 196612
  144.0 183.3 %copy-start.2 = (f32[2,32,1024]{2,1,0:T(8,128)S(1)}, f32[2,32,1024]{2,1,0:T(8,128)}, u32[]{:S(2)}) copy-start(f32[2,32,1024]{2,1,0:T(8,128)} %up_ref.1) | copy-start | bytes 786436
  321.2 9.1 %copy-start.11 = (f32[2,8,8]{2,1,0:T(8,128)S(1)}, f32[2,8,8]{2,1,0:T(8,128)}, u32[]{:S(2)}) copy-start(f32[2,8,8]{2,1,0:T(8,128)} %param.39) | copy-start | bytes 1540
  321.2 10.5 %copy-start.3 = (f32[2,1024,32]{1,2,0:T(8,128)S(1)}, f32[2,1024,32]{1,2,0:T(8,128)}, u32[]{:S(2)}) copy-start(f32[2,1024,32]{1,2,0:T(8,128)} %param.42) | copy-start | bytes 786436
  321.2 13.3 %copy-start.12 = (f32[2,5,16]{2,0,1:T(2,128)S(1)}, f32[2,5,16]{2,0,1:T(2,128)}, u32[]{:S(2)}) copy-start(f32[2,5,16]{2,0,1:T(2,128)} %param.45) | copy-start | bytes 1924
  321.2 15.9 %copy-start.6 = (f32[2,16,512]{2,1,0:T(8,128)S(1)}, f32[2,16,512]{2,1,0:T(8,128)}, u32[]{:S(2)}) copy-start(f32[2,16,512]{2,1,0:T(8,128)} %time_ref.1) | copy-start | bytes 196612
  321.3 17.4 %copy-start = (bf16[1280,512]{1,0:T(8,128)(2,1)S(1)}, bf16[1280,512]{1,0:T(8,128)(2,1)}, u32[]{:S(2)}) copy-start(bf16[1280,512]{1,0:T(8,128)(2,1)} %get-tuple-element.155) | copy-start | bytes 3932164
  323.2 16.5 %copy-start.1 = (bf16[1280,512]{1,0:T(8,128)(2,1)S(1)}, bf16[1280,512]{1,0:T(8,128)(2,1)}, u32[]{:S(2)}) copy-start(bf16[1280,512]{1,0:T(8,128)(2,1)} %get-tuple-element.156) | copy-start | bytes 3932164
  326.2 10.9 %copy-start.10 = (f32[2,16,512]{2,1,0:T(8,128)S(1)}, f32[2,16,512]{2,1,0:T(8,128)}, u32[]{:S(2)}) copy-start(f32[2,16,512]{2,1,0:T(8,128)} %get-tuple-element.53) | copy-start | bytes 196612

commit v2 on v1

v2 whole, which is shorter than its diff:
```python
import functools
import math

import jax
import jax.numpy as jnp
import numpy as np
from jax import lax
from jax.experimental import pallas as pl
from jax.experimental.pallas import tpu as pltpu
from jax.sharding import PartitionSpec as P

HEAD_DIM = 64
LENGTH = 256
LAYERS = 2
STEP = 8
GROUPS = 16
MESH = pl.DeviceIdType.MESH
LAG = 2
F32 = jnp.float32
BF16 = jnp.bfloat16

beta_first = 0.5
beta_second = 0.5
learn_rate = 0.1
norm_rate = 0.4
weight_decay = 0.01
adam_eps = 1e-08
norm_eps = 1e-05


def nn(a, b):
    return lax.dot_general(a, b, (((1,), (0,)), ((), ())), preferred_element_type=F32)


def nt(a, b):
    return lax.dot_general(a, b, (((1,), (1,)), ((), ())), preferred_element_type=F32)


def tn(a, b):
    return lax.dot_general(a, b, (((0,), (0,)), ((), ())), preferred_element_type=F32)


def normalize(values):
    center = values - jnp.mean(values, -1, keepdims=True)
    inverse = lax.rsqrt(jnp.mean(center * center, -1, keepdims=True) + norm_eps)
    return center * inverse, inverse


def fold_rows(values):
    rows, cols = values.shape
    return jnp.sum(values.reshape(rows // 8, 8, cols), 0)


def gelu_and_slope(x):
    size = jnp.abs(x)
    denom = 1.0 + (0.3275911 / math.sqrt(2.0)) * size
    t = pl.reciprocal(denom, approx=True)
    t = t * (2.0 - denom * t)
    bell = jnp.exp(x * x * -0.5)
    poly = 0.5 * 1.061405429
    poly = poly * t + 0.5 * -1.453152027
    poly = poly * t + 0.5 * 1.421413741
    poly = poly * t + 0.5 * -0.284496736
    poly = poly * t + 0.5 * 0.254829592
    tail = poly * t * bell
    below = jnp.where(x >= 0.0, 1.0 - tail, tail)
    return x * below, below + x * bell * (1.0 / math.sqrt(2.0 * math.pi))


class Place:
    def __init__(self, rep):
        dp = lax.axis_index("dp")
        self.rep = rep
        self.copy = dp % rep
        self.group = dp // rep
        self.t = lax.axis_index("tensor")
        self.z = self.group // 4
        self.yx = self.group % 4
        x, y = self.yx % 2, self.yx // 2
        self.yx_x = self.yx + 1 - 2 * x
        self.yx_y = self.yx + 2 - 4 * y
        self.yx_d = 3 - self.yx
        self.cols = pl.ds(pl.multiple_of(self.t * 256, 256), 256)
        self.other_cols = pl.ds(pl.multiple_of((1 - self.t) * 256, 256), 256)

    def device(self, z, yx, t):
        return ((z * 4 + yx) * self.rep + self.copy, t)

    def z_ahead(self, k):
        return (self.z + k) % 4

    @property
    def partners(self):
        return [self.device(self.z_ahead(k), self.yx, self.t) for k in (1, 2, 3)] + [
            self.device(self.z, self.yx_x, self.t),
            self.device(self.z, self.yx_y, self.t),
            self.device(self.z, self.yx, 1 - self.t),
        ]

    def greet(self):
        barrier = pltpu.get_barrier_semaphore()
        for partner in self.partners:
            pl.semaphore_signal(barrier, inc=1, device_id=partner, device_id_type=MESH)
        pl.semaphore_wait(barrier, len(self.partners))


class Exchange:
    def start(self, slot):
        self.copy(slot).start()

    def arrived(self, *slots):
        for slot in slots:
            self.copy(slot).wait_recv()

    def finish(self):
        for slot in range(self.slots):
            self.copy(slot).wait_send()

    def remote(self, slot, src, dst, device):
        return pltpu.make_async_remote_copy(
            src_ref=src, dst_ref=dst, send_sem=self.send.at[slot], recv_sem=self.recv.at[slot],
            device_id=device, device_id_type=MESH,
        )


class Gather(Exchange):
    slots = 8

    def __init__(self, place, view, core_view, send, recv):
        self.place, self.view, self.core_view, self.send, self.recv = place, view, core_view, send, recv

    def copy(self, slot):
        p = self.place
        if slot < 3:
            ref, device = self.view(p.z, p.yx), p.device(p.z_ahead(slot + 1), p.yx, p.t)
        elif slot < 5:
            ref, device = self.view(slice(None), p.yx), p.device(p.z, p.yx_x if slot == 3 else p.yx_y, p.t)
        elif slot == 5:
            ref, device = self.view(pl.ds(0, 2), p.yx_x), p.device(p.z, p.yx_y, p.t)
        elif slot == 6:
            ref, device = self.view(pl.ds(2, 2), p.yx_y), p.device(p.z, p.yx_x, p.t)
        else:
            ref, device = self.core_view(), p.device(p.z, p.yx, 1 - p.t)
        return self.remote(slot, ref, ref, device)

    def step(self, number):
        if number == 0:
            for slot in (0, 1, 2):
                self.start(slot)
        elif number == 1:
            self.arrived(0, 1, 2)
            self.start(3)
            self.start(4)
        elif number == 2:
            self.arrived(3)
            self.start(5)
            self.arrived(4)
            self.start(6)
        elif number == 3:
            self.arrived(5, 6)
            self.start(7)
        elif number == 4:
            self.arrived(7)


def play(events):
    for piece, number in events:
        piece.step(number)


def stagger(pieces, numbers, lag=1):
    events = []
    for turn in range(len(pieces) + lag * (len(numbers) - 1)):
        for place, number in enumerate(numbers):
            if 0 <= turn - lag * place < len(pieces):
                events.append((pieces[turn - lag * place], number))
    return events


def share(events, counts):
    runs = []
    for count in counts:
        runs.append(events[:count])
        events = events[count:]
    return runs + [events]


def each_item(body, agenda, items, in_specs, out_specs, refs):
    def whole(*blocks):
        item = pl.program_id(0)
        for number, events in enumerate(agenda[:-1]):
            if events:
                pl.when(item == number)(functools.partial(play, events))
        body(item, *blocks)

    pltpu.emit_pipeline(whole, grid=(items,), in_specs=in_specs, out_specs=out_specs)(*refs)
    play(agenda[-1])


GATHER_PIECES = 12


def weight(ref, group):
    return jnp.concatenate([ref[group, 0].reshape(512, 256), ref[group, 1].reshape(512, 256)], 1)


def forward_kernel(
    rep,
    steps_ref, freq_ref, x_ref, qkv_ref, out_ref, up_ref, down_ref, time_ref, norm_ref, bias_ref,
    w_out, small_out, feats_out, entry_out, middle_out, qkv_out, probs_out, attn_out, hidden_out, slope_out, act_out,
    w, tw, nb, norms, bias, shifts, stream, attn, send, recv, keep_sem,
):
    place = Place(rep)
    z, yx, t = place.z, place.yx, place.t
    items = stream.shape[0] // LENGTH

    for layer in range(LAYERS):
        for slot in range(3):
            w[layer, slot, t, z, yx] = qkv_ref[layer, slot].astype(BF16)
        w[layer, 3, t, z, yx] = out_ref[layer].astype(BF16)
        for part in range(4):
            own = slice(part * 256, (part + 1) * 256)
            w[layer, 4 + part, t, z, yx] = up_ref[layer, :, own].astype(BF16)
            w[layer, 8 + part, t, z, yx] = down_ref[layer, :, own].astype(BF16)
        tw[layer, t, z, yx] = time_ref[layer].astype(BF16)
    nb[0, t, z, yx] = norm_ref[...]
    nb[1, t, z, yx] = bias_ref[...]
    place.greet()

    pieces = []

    def piece(ref, *lead):
        number = len(pieces)
        pieces.append(
            Gather(
                place,
                lambda a, b: ref.at[(*lead, t, a, b)],
                lambda: ref.at[(*lead, t)],
                send.at[number],
                recv.at[number],
            )
        )
        return pieces[-1]

    norm_piece = piece(nb, 0)
    time_pieces, layer_pieces = [], []
    for layer in range(LAYERS):
        time_pieces.append(piece(tw, layer))
        layer_pieces.append([piece(w, layer, pl.ds(first, count)) for first, count in ((0, 3), (3, 1), (4, 4), (8, 4))])
        if layer == 0:
            bias_piece = piece(nb, 1)
    opening = [norm_piece, time_pieces[0], layer_pieces[0][0]]
    rest = [layer_pieces[0][1], bias_piece] + layer_pieces[0][2:] + [time_pieces[1]] + layer_pieces[1]
    for entry in opening + rest:
        entry.step(0)
    for number in (1, 2, 3):
        for entry in opening:
            entry.step(number)
    events = stagger(rest, (1, 2, 3, 4), LAG)

    def until(entry):
        last = events.index((entry, 4)) + 1
        first, events[:] = events[:last], events[last:]
        return first

    rows = lax.broadcasted_iota(jnp.int32, (8, 256), 0)
    angles = jnp.zeros((8, 256), F32)
    for item in range(items):
        step_value = steps_ref[t * items + item].astype(F32)
        angles = jnp.where(rows == item, step_value * freq_ref[0:1, :], angles)
    live = rows < items
    feats = jnp.concatenate(
        [jnp.where(live, jnp.sin(angles), 0.0), jnp.where(live, jnp.cos(angles), 0.0)], 1
    )
    feats_out[...] = feats
    feats_high = feats.astype(BF16)
    feats_low = (feats - feats_high.astype(F32)).astype(BF16)

    for entry in opening:
        entry.step(4)
    for zz in range(4):
        total = jnp.zeros((16, 128), F32)
        for part in range(8):
            total = total + nb[0, part % 2, zz, part // 2]
        norms[:, zz * 128 : (zz + 1) * 128] = total
    small_out[...] = norms[...]

    def spread_times(layer):
        table = [tw[layer, core].reshape(GROUPS, 16, 512) for core in range(2)]
        table = jnp.concatenate([table[0][:, None], table[1][:, None]], 1).reshape(512, 512)
        shifts[layer * 8 : (layer + 1) * 8] = nn(feats_high, table) + nn(feats_low, table)

    def spread_bias():
        for core in range(2):
            total = jnp.zeros((16, 128), F32)
            for part in range(16):
                total = total + nb[1, core, part // 4, part % 4]
            total = total.astype(BF16).astype(F32)
            for layer in range(LAYERS):
                for part in range(4):
                    for half in range(2):
                        row = layer * 8 + part * 2 + half
                        col = core * 256 + half * 128
                        bias[layer * 4 + part : layer * 4 + part + 1, col : col + 128] = total[row : row + 1]

    lane = lax.broadcasted_iota(jnp.int32, (1, 128), 1)
    even = lane < HEAD_DIM
    even_mask = jnp.where(even, 1.0, 0.0).astype(BF16)
    odd_mask = jnp.where(even, 0.0, 1.0).astype(BF16)

    def attention_phase(layer, agenda):
        def body(item, *refs):
            if layer == 0:
                x_blk, *refs = refs
            entry_blk, qkv_blk, probs_blk, attn_blk = refs
            here = pl.ds(pl.multiple_of(item * LENGTH, LENGTH), LENGTH)
            start = x_blk[...].astype(F32) if layer == 0 else stream[here]
            entry = start + shifts[pl.ds(layer * 8 + item, 1)]
            entry_blk[...] = entry
            stream[here] = entry
            hat, _ = normalize(entry)
            normed = (hat * norms[layer * 5 : layer * 5 + 1] + norms[layer * 5 + 1 : layer * 5 + 2]).astype(BF16)
            for slot in range(3):
                projected = nn(normed, weight(w.at[layer], slot)).astype(BF16)
                if slot == 0:
                    projected = projected * jnp.asarray(HEAD_DIM**-0.5, BF16)
                qkv_blk[:, slot * 512 : (slot + 1) * 512] = projected
            for pair in range(4):
                span = slice(pair * 128, (pair + 1) * 128)
                query = qkv_blk[:, span]
                key = qkv_blk[:, 512 + pair * 128 : 512 + (pair + 1) * 128]
                value = qkv_blk[:, 1024 + pair * 128 : 1024 + (pair + 1) * 128]
                mixed = []
                for side, mask in enumerate((even_mask, odd_mask)):
                    scores = nt(query * mask, key)
                    raised = jnp.exp(scores - jnp.max(scores, -1, keepdims=True))
                    probs = (raised * (1.0 / jnp.sum(raised, -1, keepdims=True))).astype(BF16)
                    probs_blk[0, pair * 2 + side] = probs
                    mixed.append(nn(probs, value))
                joined = jnp.where(even, mixed[0], mixed[1]).astype(BF16)
                attn_blk[:, span] = joined
                attn[here, span] = joined

        wide = lambda cols: pl.BlockSpec((LENGTH, cols), lambda i: (i, 0))
        each_item(
            body, agenda, items,
            [wide(512)] if layer == 0 else [],
            [wide(512), wide(1536), pl.BlockSpec((1, 8, 256, 256), lambda i: (i, 0, 0, 0)), wide(512)],
            ([x_ref] if layer == 0 else [])
            + [entry_out.at[layer], qkv_out.at[layer], probs_out.at[layer], attn_out.at[layer]],
        )

    def feed_phase(layer, agenda):
        def body(item, middle_blk, hidden_blk, slope_blk, *rest):
            here = pl.ds(pl.multiple_of(item * LENGTH, LENGTH), LENGTH)
            middle = stream[here] + nt(attn[here], weight(w.at[layer], 3))
            middle_blk[...] = middle
            hat, _ = normalize(middle)
            normed = (hat * norms[layer * 5 + 2 : layer * 5 + 3] + norms[layer * 5 + 3 : layer * 5 + 4]).astype(BF16)
            total = middle + norms[layer * 5 + 4 : layer * 5 + 5]
            for part in range(4):
                row = layer * 4 + part
                span = slice(part * 512, (part + 1) * 512)
                pre = nn(normed, weight(w.at[layer], 4 + part)) + bias[row : row + 1]
                hidden, slope = gelu_and_slope(pre)
                hidden = hidden.astype(BF16)
                hidden_blk[:, span] = hidden
                slope_blk[:, span] = slope.astype(BF16)
                total = total + nt(hidden, weight(w.at[layer], 8 + part))
            if layer == LAYERS - 1:
                rest[0][...] = total.astype(BF16)
            else:
                stream[here] = total

        wide = lambda cols: pl.BlockSpec((LENGTH, cols), lambda i: (i, 0))
        last = layer == LAYERS - 1
        each_item(
            body, agenda, items, [],
            [wide(512), wide(2048), wide(2048)] + ([wide(512)] if last else []),
            [middle_out.at[layer], hidden_out.at[layer], slope_out.at[layer]] + ([act_out] if last else []),
        )

    spread_times(0)
    keeps = []
    for layer in range(LAYERS):
        qkv_piece, out_piece, up_piece, down_piece = layer_pieces[layer]
        if layer > 0:
            spread_times(layer)
        attention_phase(layer, share(until(down_piece), AGENDA[layer][0]))
        if layer == 0:
            spread_bias()
        keep = pltpu.make_async_copy(w.at[layer], w_out.at[layer], keep_sem.at[layer])
        keep.start()
        keeps.append(keep)
        feed_phase(layer, share(until(layer_pieces[1][0]) if layer == 0 else [], AGENDA[layer][1]))
    for entry in pieces:
        entry.finish()
    for keep in keeps:
        keep.wait()


AGENDA = (((1, 2, 2, 3, 3), (2, 3, 3, 3, 3)), ((2, 3, 3, 3, 3), ()))


def forward_call(rep, rows, steps, freq, x, qkv, out, up, down, time, norm, bias):
    items = rows // LENGTH
    hbm = pl.BlockSpec(memory_space=pl.ANY)
    vmem = pl.BlockSpec(memory_space=pltpu.VMEM)
    smem = pl.BlockSpec(memory_space=pltpu.SMEM)
    shape = jax.ShapeDtypeStruct
    return pl.pallas_call(
        functools.partial(forward_kernel, rep),
        name="forward",
        in_specs=[smem, vmem, hbm] + [vmem] * 7,
        out_shape=[
            shape((LAYERS, 12, 2, 4, 4, 32, 256), BF16),
            shape((16, 512), F32),
            shape((8, 512), F32),
            shape((LAYERS, rows, 512), F32),
            shape((LAYERS, rows, 512), F32),
            shape((LAYERS, rows, 1536), BF16),
            shape((LAYERS, items, 8, 256, 256), BF16),
            shape((LAYERS, rows, 512), BF16),
            shape((LAYERS, rows, 2048), BF16),
            shape((LAYERS, rows, 2048), BF16),
            shape((rows, 512), BF16),
        ],
        out_specs=[hbm, vmem, vmem] + [hbm] * 8,
        scratch_shapes=[
            pltpu.VMEM((LAYERS, 12, 2, 4, 4, 32, 256), BF16),
            pltpu.VMEM((LAYERS, 2, 4, 4, 16, 512), BF16),
            pltpu.VMEM((2, 2, 4, 4, 16, 128), F32),
            pltpu.VMEM((16, 512), F32),
            pltpu.VMEM((8, 512), F32),
            pltpu.VMEM((16, 512), F32),
            pltpu.VMEM((rows, 512), F32),
            pltpu.VMEM((rows, 512), BF16),
            pltpu.SemaphoreType.DMA((GATHER_PIECES, 8)),
            pltpu.SemaphoreType.DMA((GATHER_PIECES, 8)),
            pltpu.SemaphoreType.DMA((LAYERS,)),
        ],
        compiler_params=pltpu.CompilerParams(collective_id=1, has_side_effects=True, vmem_limit_bytes=56 << 20),
    )(steps, freq, x, qkv, out, up, down, time, norm, bias)


class Scatter(Exchange):
    slots = 10

    def __init__(self, place, grads, received, total, groups, send, recv):
        self.place, self.grads, self.received, self.total = place, grads, received, total
        self.first, self.count = groups
        self.span = pl.ds(*groups)
        self.send, self.recv = send, recv

    def copy(self, slot):
        p, span = self.place, self.span
        core, diag_y, diag_x, col_x, col_y, along = self.received
        low, high = pl.ds(0, 2), pl.ds(2, 2)
        to_x, to_y = p.device(p.z, p.yx_x, p.t), p.device(p.z, p.yx_y, p.t)
        if slot == 0:
            src, dst, device = self.grads.at[span, 1 - p.t], core.at[span], p.device(p.z, p.yx, 1 - p.t)
        elif slot == 1:
            src, dst, device = self.grads.at[span, p.t, low, p.yx_d], diag_y.at[span], to_y
        elif slot == 2:
            src, dst, device = self.grads.at[span, p.t, high, p.yx_d], diag_x.at[span], to_x
        elif slot == 3:
            src, dst, device = self.grads.at[span, p.t, low, p.yx_x], col_x.at[span, low], to_x
        elif slot == 4:
            src, dst, device = self.grads.at[span, p.t, high, p.yx_y], col_y.at[span, high], to_y
        elif slot == 5:
            src, dst, device = self.grads.at[span, p.t, high, p.yx_x], col_x.at[span, high], to_x
        elif slot == 6:
            src, dst, device = self.grads.at[span, p.t, low, p.yx_y], col_y.at[span, low], to_y
        else:
            there = p.z_ahead(slot - 6)
            src, dst, device = self.grads.at[span, p.t, there, p.yx], along.at[slot - 7, span], p.device(there, p.yx, p.t)
        return self.remote(slot, src, dst, device)

    def add(self, where, terms):
        def one(group, carry):
            ref = self.grads.at[(group, self.place.t) + where]
            value = ref[...].astype(F32)
            for term in terms:
                value = value + term[group].astype(F32)
            ref[...] = value.astype(BF16)
            return carry

        lax.fori_loop(self.first, self.first + self.count, one, 0)

    def step(self, number):
        p = self.place
        core, diag_y, diag_x, col_x, col_y, along = self.received
        every = slice(None)
        if number == 0:
            self.start(0)
        elif number == 1:
            self.arrived(0)
            self.add((every, every), [core])
            for slot in (1, 2, 5, 6):
                self.start(slot)
        elif number == 2:
            self.arrived(1)
            self.add((pl.ds(0, 2), p.yx_x), [diag_y])
            self.start(3)
            self.arrived(2)
            self.add((pl.ds(2, 2), p.yx_y), [diag_x])
            self.start(4)
        elif number == 3:
            self.arrived(3, 4, 5, 6)
            self.add((every, p.yx), [col_x, col_y])
            for slot in (7, 8, 9):
                self.start(slot)
        elif number == 4:
            self.arrived(7, 8, 9)

            def one(group, carry):
                value = self.grads[group, p.t, p.z, p.yx].astype(F32)
                for k in range(3):
                    value = value + along[k, group].astype(F32)
                self.total[group] = value
                return carry

            lax.fori_loop(self.first, self.first + self.count, one, 0)


class SmallSum(Exchange):
    slots = 6

    def __init__(self, place, sums, received, total, send, recv):
        self.place, self.sums, self.received, self.total = place, sums, received, total
        self.send, self.recv = send, recv

    def copy(self, slot):
        p = self.place
        if slot == 0:
            device = p.device(p.z, p.yx, 1 - p.t)
        elif slot < 3:
            device = p.device(p.z, p.yx_x if slot == 1 else p.yx_y, p.t)
        else:
            device = p.device(p.z_ahead(slot - 2), p.yx, p.t)
        return self.remote(slot, self.sums.at[min(slot, 3)], self.received.at[slot], device)

    def step(self, number):
        if number > 0:
            slots = (3, 4, 5) if number == 4 else (number - 1,)
            value = self.sums[number - 1]
            self.arrived(*slots)
            for slot in slots:
                value = value + self.received[slot]
            if number < 4:
                self.sums[number] = value
            else:
                self.total[...] = value
        if number < 3:
            self.start(number)
        elif number == 3:
            for slot in (3, 4, 5):
                self.start(slot)


GRAD_GROUPS = 13
SCATTER_PIECES = ((4, 2), (6, 2), (8, 2), (10, 2), (3, 1), (0, 1), (1, 1), (2, 1), (12, 1))
BACK_AGENDA = ((3, 3, 3, 3, 3), (4, 4, 4, 4, 4))


def backward_kernel(
    rep,
    scale_ref, small_ref, feats_ref, cot_ref, w_in, entry_in, middle_in, qkv_in, probs_in, attn_in, hidden_in, slope_in,
    grad_out, total_out, sums_out, time_out,
    w, gx, dattn, du, hidden, attn, n1t, n2t, gdt, got, dqkv, grads, item_grad, acc, acc_bias,
    r_core, r_dy, r_dx, r_x, r_y, r_z, sums, r_sums, r_time,
    w_sem, in_sem, send, recv, small_send, small_recv, time_send, time_recv,
):
    place = Place(rep)
    t = place.t
    rows = gx.shape[0]
    items = rows // LENGTH
    wide = lambda cols: pl.BlockSpec((LENGTH, cols), lambda i: (i, 0))
    lane = lax.broadcasted_iota(jnp.int32, (1, 128), 1)
    even = lane < HEAD_DIM
    even_mask = jnp.where(even, 1.0, 0.0).astype(BF16)
    odd_mask = jnp.where(even, 0.0, 1.0).astype(BF16)

    def load_weights(layer):
        copies = []
        for number, (first, count) in enumerate(((3, 9), (0, 3))):
            copy = pltpu.make_async_copy(
                w_in.at[layer, pl.ds(first, count)], w.at[pl.ds(first, count)], w_sem.at[layer, number]
            )
            copies.append(copy)
        return copies

    def load_stash(layer):
        return [
            pltpu.make_async_copy(hidden_in.at[layer], hidden, in_sem.at[layer, 0]),
            pltpu.make_async_copy(attn_in.at[layer], attn, in_sem.at[layer, 1]),
        ]

    def norm_back(hat, inverse, dy, layer, row, here):
        acc[row] += fold_rows(dy * hat)
        acc[row + 1] += fold_rows(dy)
        scaled = dy * small_ref[layer * 5 + row : layer * 5 + row + 1]
        mean = jnp.mean(scaled, -1, keepdims=True)
        along = jnp.mean(scaled * hat, -1, keepdims=True)
        return inverse * (scaled - mean - hat * along)

    def feed_phase(layer, agenda):
        last = layer == LAYERS - 1

        def body(item, middle_blk, slope_blk, *rest):
            here = pl.ds(pl.multiple_of(item * LENGTH, LENGTH), LENGTH)
            if last:
                grad = rest[0][...].astype(F32) * scale_ref[t * items + item]
            else:
                grad = gx[here]
            acc[4] += fold_rows(grad)
            low = grad.astype(BF16)
            gdt[:, here] = low.T
            back = jnp.zeros((LENGTH, 512), F32)
            for part in range(4):
                span = slice(part * 512, (part + 1) * 512)
                dh = nn(low, weight(w, 8 + part))
                pre_grad = (dh * slope_blk[:, span].astype(F32)).astype(BF16)
                du[here, span] = pre_grad
                acc_bias[part] += fold_rows(pre_grad.astype(F32))
                back = back + nt(pre_grad, weight(w, 4 + part))
            hat, inverse = normalize(middle_blk[...])
            normed = hat * small_ref[layer * 5 + 2 : layer * 5 + 3] + small_ref[layer * 5 + 3 : layer * 5 + 4]
            n2t[:, here] = normed.astype(BF16).T
            grad = grad + norm_back(hat, inverse, back, layer, 2, here)
            gx[here] = grad
            low = grad.astype(BF16)
            got[:, here] = low.T
            dattn[here] = nn(low, weight(w, 3)).astype(BF16)

        each_item(
            body, agenda, items, [wide(512), wide(2048)] + ([wide(512)] if last else []), [],
            [middle_in.at[layer], slope_in.at[layer]] + ([cot_ref] if last else []),
        )

    def attention_phase(layer, agenda):
        def body(item, entry_blk, qkv_blk, probs_blk, *rest):
            here = pl.ds(pl.multiple_of(item * LENGTH, LENGTH), LENGTH)
            for pair in range(4):
                span = slice(pair * 128, (pair + 1) * 128)
                query = qkv_blk[:, span]
                key = qkv_blk[:, 512 + pair * 128 : 512 + (pair + 1) * 128]
                value = qkv_blk[:, 1024 + pair * 128 : 1024 + (pair + 1) * 128]
                back = dattn[here, span]
                found = []
                for side, mask in enumerate((even_mask, odd_mask)):
                    probs = probs_blk[0, pair * 2 + side]
                    dprobs = nt(back * mask, value)
                    wide_probs = probs.astype(F32)
                    delta = jnp.sum(wide_probs * dprobs, -1, keepdims=True)
                    dscores = (wide_probs * (dprobs - delta)).astype(BF16)
                    found.append((nn(dscores, key), tn(dscores, query), tn(probs, back)))
                dq, dk, dv = [jnp.where(even, found[0][i], found[1][i]) for i in range(3)]
                dqkv[here, span] = (dq * HEAD_DIM**-0.5).astype(BF16)
                dqkv[here, 512 + pair * 128 : 512 + (pair + 1) * 128] = dk.astype(BF16)
                dqkv[here, 1024 + pair * 128 : 1024 + (pair + 1) * 128] = dv.astype(BF16)
            back = jnp.zeros((LENGTH, 512), F32)
            for slot in range(3):
                back = back + nt(dqkv[here, slot * 512 : (slot + 1) * 512], weight(w, slot))
            hat, inverse = normalize(entry_blk[...])
            normed = hat * small_ref[layer * 5 : layer * 5 + 1] + small_ref[layer * 5 + 1 : layer * 5 + 2]
            n1t[:, here] = normed.astype(BF16).T
            grad = gx[here] + norm_back(hat, inverse, back, layer, 0, here)
            item_grad[pl.ds(item, 1)] = jnp.sum(grad, 0, keepdims=True)
            if layer == 0:
                rest[0][...] = grad.astype(BF16)
            else:
                gx[here] = grad

        each_item(
            body, agenda, items,
            [wide(512), wide(1536), pl.BlockSpec((1, 8, 256, 256), lambda i: (i, 0, 0, 0))],
            [wide(512)] if layer == 0 else [],
            [entry_in.at[layer], qkv_in.at[layer], probs_in.at[layer]] + ([grad_out] if layer == 0 else []),
        )

    def keep_grad(group, value):
        for half in range(2):
            grads[group, half] = value[:, half * 256 : (half + 1) * 256].astype(BF16).reshape(4, 4, 32, 256)

    def weight_grad(left, right, first, offset, count):
        def one(part, carry):
            span = pl.ds(pl.multiple_of((offset + part) * 512, 512), 512)
            keep_grad(first + part, nn(left[...], right[:, span]))
            return carry

        lax.fori_loop(0, count, one, 0)

    scatters, smalls = [], []
    for layer in range(LAYERS):
        received = [r.at[layer] for r in (r_core, r_dy, r_dx, r_x, r_y, r_z)]
        scatters.append(
            [
                Scatter(place, grads, received, total_out.at[layer], groups, send.at[layer, i], recv.at[layer, i])
                for i, groups in enumerate(SCATTER_PIECES)
            ]
        )
        smalls.append(
            SmallSum(place, sums.at[layer], r_sums.at[layer], sums_out.at[layer], small_send.at[layer], small_recv.at[layer])
        )

    order = [LAYERS - 1 - i for i in range(LAYERS)]
    weights = {order[0]: load_weights(order[0])}
    stash = {order[0]: load_stash(order[0])}
    for copy in weights[order[0]] + stash[order[0]]:
        copy.start()
    item_grad[...] = jnp.zeros(item_grad.shape, F32)
    place.greet()

    pending = []
    for turn, layer in enumerate(order):
        feed_pieces, late_pieces = scatters[layer][:5], scatters[layer][5:]
        acc[...] = jnp.zeros(acc.shape, F32)
        acc_bias[...] = jnp.zeros(acc_bias.shape, F32)
        weights[layer][0].wait()
        with jax.named_scope("feed_back"):
            feed_phase(layer, share(pending, BACK_AGENDA[1]))
        stash[layer][0].wait()
        stash[layer][1].wait()
        weights[layer][1].wait()
        if turn > 0:
            for piece in scatters[order[turn - 1]]:
                piece.finish()
        with jax.named_scope("feed_grads"):
            made = ((n2t, du, 4, 0), (n2t, du, 6, 2), (gdt, hidden, 8, 0), (gdt, hidden, 10, 2), (got, attn, 3, 0))
            pending = stagger(feed_pieces, (0, 1, 2, 3, 4), LAG)
            for piece, (left, right, first, part) in zip(feed_pieces, made):
                weight_grad(left, right, first, part, piece.count)
                ready = pending.index((piece, 0)) + 1
                play(pending[:ready])
                pending = pending[ready:]
        with jax.named_scope("attention_back"):
            attention_phase(layer, share(pending, BACK_AGENDA[0]))
        if turn + 1 < LAYERS:
            after = order[turn + 1]
            weights[after] = load_weights(after)
            stash[after] = load_stash(after)
            for copy in weights[after] + stash[after]:
                copy.start()
        with jax.named_scope("attention_grads"):
            spread = lax.dot_general(
                feats_ref[...], item_grad[...], (((0,), (0,)), ((), ())),
                precision=lax.Precision.HIGHEST, preferred_element_type=F32,
            )
            keep_grad(12, spread)
            for row in range(5):
                sums[layer, 0, row : row + 1] = jnp.sum(acc[row], 0, keepdims=True)
            for part in range(4):
                sums[layer, 0, 5 + part : 6 + part] = jnp.sum(acc_bias[part], 0, keepdims=True)
            sums[layer, 0, 9:16] = jnp.zeros((7, 512), F32)
            late_pieces = [late_pieces[3], smalls[layer]] + late_pieces[:3]
            pending = stagger(late_pieces, (0, 1, 2, 3, 4), LAG)
            for slot in range(3):
                weight_grad(n1t, dqkv, slot, slot, 1)
                ready = pending.index((late_pieces[2 + slot], 0)) + 1
                play(pending[:ready])
                pending = pending[ready:]
    with jax.named_scope("scatter"):
        play(pending)

    swaps = []
    for layer in range(LAYERS):
        swap = pltpu.make_async_remote_copy(
            src_ref=total_out.at[layer, 12, pl.ds(pl.multiple_of((1 - t) * 16, 16), 16)],
            dst_ref=r_time.at[layer], send_sem=time_send.at[layer], recv_sem=time_recv.at[layer],
            device_id=place.device(place.z, place.yx, 1 - t), device_id_type=MESH,
        )
        swap.start()
        swaps.append(swap)
    for layer in range(LAYERS):
        swaps[layer].wait()
        time_out[layer, :, place.cols] = total_out[layer, 12, pl.ds(pl.multiple_of(t * 16, 16), 16)]
        time_out[layer, :, place.other_cols] = r_time[layer]
    for piece in scatters[order[-1]]:
        piece.finish()
    for piece in smalls:
        piece.finish()


def backward_call(rep, rows, scale, small, feats, cot, w, entry, middle, qkv, probs, attn, hidden, slope):
    items = rows // LENGTH
    hbm = pl.BlockSpec(memory_space=pl.ANY)
    vmem = pl.BlockSpec(memory_space=pltpu.VMEM)
    smem = pl.BlockSpec(memory_space=pltpu.SMEM)
    shape = jax.ShapeDtypeStruct
    pieces = len(SCATTER_PIECES)
    dma = pltpu.SemaphoreType.DMA
    return pl.pallas_call(
        functools.partial(backward_kernel, rep),
        name="backward",
        in_specs=[smem, vmem, vmem] + [hbm] * 9,
        out_shape=[
            shape((rows, 512), BF16),
            shape((LAYERS, GRAD_GROUPS, 32, 256), F32),
            shape((LAYERS, 16, 512), F32),
            shape((LAYERS, 16, 512), F32),
        ],
        out_specs=[hbm, vmem, vmem, vmem],
        scratch_shapes=[
            pltpu.VMEM((12, 2, 4, 4, 32, 256), BF16),
            pltpu.VMEM((rows, 512), F32),
            pltpu.VMEM((rows, 512), BF16),
            pltpu.VMEM((rows, 2048), BF16),
            pltpu.VMEM((rows, 2048), BF16),
            pltpu.VMEM((rows, 512), BF16),
            pltpu.VMEM((512, rows), BF16),
            pltpu.VMEM((512, rows), BF16),
            pltpu.VMEM((512, rows), BF16),
            pltpu.VMEM((512, rows), BF16),
            pltpu.VMEM((rows, 1536), BF16),
            pltpu.VMEM((GRAD_GROUPS, 2, 4, 4, 32, 256), BF16),
            pltpu.VMEM((8, 512), F32),
            pltpu.VMEM((5, 8, 512), F32),
            pltpu.VMEM((4, 8, 512), F32),
            pltpu.VMEM((LAYERS, GRAD_GROUPS, 4, 4, 32, 256), BF16),
            pltpu.VMEM((LAYERS, GRAD_GROUPS, 2, 32, 256), BF16),
            pltpu.VMEM((LAYERS, GRAD_GROUPS, 2, 32, 256), BF16),
            pltpu.VMEM((LAYERS, GRAD_GROUPS, 4, 32, 256), BF16),
            pltpu.VMEM((LAYERS, GRAD_GROUPS, 4, 32, 256), BF16),
            pltpu.VMEM((LAYERS, 3, GRAD_GROUPS, 32, 256), BF16),
            pltpu.VMEM((LAYERS, 4, 16, 512), F32),
            pltpu.VMEM((LAYERS, 6, 16, 512), F32),
            pltpu.VMEM((LAYERS, 16, 256), F32),
            dma((LAYERS, 2)),
            dma((LAYERS, 2)),
            dma((LAYERS, pieces, 10)),
            dma((LAYERS, pieces, 10)),
            dma((LAYERS, 6)),
            dma((LAYERS, 6)),
            dma((LAYERS,)),
            dma((LAYERS,)),
        ],
        compiler_params=pltpu.CompilerParams(collective_id=2, has_side_effects=True, vmem_limit_bytes=62 << 20),
    )(scale, small, feats, cot, w, entry, middle, qkv, probs, attn, hidden, slope)


def adamw(weight, gradient, first_moment, second_moment, rate):
    first_new = beta_first * first_moment + (1.0 - beta_first) * gradient
    second_new = beta_second * second_moment + (1.0 - beta_second) * gradient * gradient
    first_corr = first_new * (1.0 / (1.0 - beta_first**STEP))
    second_corr = second_new * (1.0 / (1.0 - beta_second**STEP))
    weight_new = weight - rate * (first_corr / (jnp.sqrt(second_corr) + adam_eps) + weight_decay * weight)
    return (weight_new, first_new, second_new)


def update_kernel(total, sums, time_grad, *refs):
    ins, outs, (row,) = refs[:21], refs[21:43], refs[43:]
    qkv, out, up, bias, down, norm, time = [ins[i * 3 : i * 3 + 3] for i in range(7)]
    qkv_new, key_second, value_second = outs[0:2], outs[2], outs[3]
    out_new, up_new, bias_new, down_new, norm_new, time_new = [outs[4 + i * 3 : 7 + i * 3] for i in range(6)]
    dp, t = lax.axis_index("dp"), lax.axis_index("tensor")

    def one(old, new, where, gradient, rate):
        values = adamw(old[0][where], gradient, old[1][where], old[2][where], rate)
        for ref, value in zip(new, values):
            ref[where] = value
        return values

    for layer in range(LAYERS):
        for slot in range(3):
            values = adamw(qkv[0][layer, slot], total[layer, slot], qkv[1][layer, slot], qkv[2][layer, slot], learn_rate)
            for ref, value in zip(qkv_new, values):
                ref[layer, slot] = value
            if slot < 2:
                key_second[layer, :, slot] = values[2]
            else:
                value_second[layer] = values[2]
        one(out, out_new, (layer,), total[layer, 3], learn_rate)
        for part in range(4):
            where = (layer, slice(None), slice(part * 256, (part + 1) * 256))
            one(up, up_new, where, total[layer, 4 + part], learn_rate)
            one(down, down_new, where, total[layer, 8 + part], learn_rate)
        one(time, time_new, (layer,), time_grad[layer], learn_rate)

        width = norm[0].shape[2]
        start = (dp * 2 + t) * width
        tile = sums[layer, :, pl.ds(pl.multiple_of(start // 128 * 128, 128), 128)]
        mine = pltpu.roll(tile, (128 - start % 128) % 128, 1)[0:5, 0:width]
        one(norm, norm_new, (slice(None), layer), mine, norm_rate)
        for part in range(4):
            for half in range(2):
                span = pl.ds(pl.multiple_of(t * 256 + half * 128, 128), 128)
                row[part * 2 + half : part * 2 + half + 1] = sums[layer, 5 + part : 6 + part, span]
        width = bias[0].shape[2]
        mine = pltpu.roll(row[...], (128 - dp * width) % 128, 1)[:, 0:width]
        one(bias, bias_new, (layer,), mine, learn_rate)


def update_call(total, sums, time_grad, states):
    flat = [array for state in states for array in state]
    like = lambda array: jax.ShapeDtypeStruct(array.shape, F32)
    rows = states[0][0].shape[2]
    shapes = [like(array) for array in flat]
    shapes[2:3] = [
        jax.ShapeDtypeStruct((LAYERS, rows, 2, 256), F32),
        jax.ShapeDtypeStruct((LAYERS, rows, 256), F32),
    ]
    vmem = pl.BlockSpec(memory_space=pltpu.VMEM)
    return pl.pallas_call(
        update_kernel,
        name="update",
        in_specs=[vmem] * 24,
        out_shape=shapes,
        out_specs=[vmem] * 22,
        scratch_shapes=[pltpu.VMEM((8, 128), F32)],
        compiler_params=pltpu.CompilerParams(vmem_limit_bytes=48 << 20),
    )(total, sums, time_grad, *flat)


def per_device(
    rep,
    inputs, cotangent, timesteps, item_scale,
    qkv_weight, qkv_first, qkv_second,
    out_weight, out_first, out_second,
    up_weight, up_first, up_second,
    up_bias, bias_first, bias_second,
    down_weight, down_first, down_second,
    norm_params, norm_first, norm_second,
    time_weight, time_first, time_second,
):
    rows = inputs.shape[0]
    dp, t = lax.axis_index("dp"), lax.axis_index("tensor")
    group = dp // rep
    qkv, out, up, down, bias = qkv_weight, out_weight, up_weight, down_weight, up_bias
    norm, time = norm_params, time_weight
    teams = None
    if rep > 1:
        size = GROUPS * rep
        teams = [[g * rep + j for j in range(rep)] for g in range(GROUPS)]
        pairs = [[g * rep * 2 + j for j in range(rep * 2)] for g in range(GROUPS)]
        join = lambda v, axis: lax.all_gather(v, "dp", axis=axis, axis_index_groups=teams, tiled=True)
        join_both = lambda v, axis: lax.all_gather(
            v, ("dp", "tensor"), axis=axis, axis_index_groups=pairs, tiled=True
        )
        qkv, out, up, down, bias = join(qkv, 1), join(out, 2), join(up, 1), join(down, 2), join(bias, 2)
        norm, time = join_both(norm, 2), join_both(time, 1)
        norm = lax.dynamic_slice_in_dim(norm, t * 16, 16, 2)
        time = lax.dynamic_slice_in_dim(time, t * 16, 16, 1)

    lane = lax.broadcasted_iota(jnp.int32, (16, 128), 1)
    spot = (group % 4) * 2 + t
    norm_rows = jnp.pad(norm.reshape(10, 16), ((0, 6), (0, 0)))
    norm_block = jnp.where(lane // 16 == spot, jnp.tile(norm_rows, (1, 8)), 0.0)
    bias_block = jnp.where(lane // 8 == group, jnp.tile(bias.reshape(16, 8), (1, 16)), 0.0)
    half_width = 256
    freq = np.exp(-math.log(10000.0) / half_width * np.arange(half_width)).astype(np.float32)
    freq = jnp.asarray(np.broadcast_to(freq, (8, half_width)))

    w, small, feats, entry, middle, qkv_rows, probs, attn, hidden, slope, activations = forward_call(
        rep, rows, timesteps, freq, inputs,
        jnp.transpose(qkv, (0, 2, 1, 3)), jnp.swapaxes(out, 1, 2), up, jnp.swapaxes(down, 1, 2),
        time, norm_block, bias_block,
    )
    input_grad, total, sums, time_grad = backward_call(
        rep, rows, item_scale, small, feats, cotangent, w, entry, middle, qkv_rows, probs, attn, hidden, slope
    )

    if rep > 1:
        total = lax.psum_scatter(total, "dp", scatter_dimension=2, axis_index_groups=teams, tiled=True)
        sums, time_grad = lax.psum((sums, time_grad), "dp", axis_index_groups=teams)
        time_grad = lax.all_gather(time_grad, "tensor", axis=1, tiled=True)
        width = time_weight.shape[1]
        time_grad = lax.dynamic_slice_in_dim(time_grad, ((dp % rep) * 2 + t) * width, width, 1)

    slots = lambda *arrays: [jnp.transpose(v, (0, 2, 1, 3)) for v in arrays]
    flip = lambda *arrays: [jnp.swapaxes(v, 1, 2) for v in arrays]
    front = lambda *arrays: [jnp.swapaxes(v, 0, 1) for v in arrays]
    new = update_call(
        total, sums, time_grad,
        [
            slots(qkv_weight, qkv_first, qkv_second),
            flip(out_weight, out_first, out_second),
            [up_weight, up_first, up_second],
            [up_bias, bias_first, bias_second],
            flip(down_weight, down_first, down_second),
            front(norm_params, norm_first, norm_second),
            [time_weight, time_first, time_second],
        ],
    )
    return (
        activations, input_grad,
        *slots(*new[0:2]), new[2], new[3],
        *flip(*new[4:7]), *new[7:10], *new[10:13], *flip(*new[13:16]), *front(*new[16:19]), *new[19:22],
    )


def solution(mesh):
    rep = mesh.shape["dp"] // GROUPS
    shard = P(None, "dp", None, "tensor")
    rows = P(("dp", "tensor"), None)
    trans = P(None, "tensor", "dp")
    flat = P(None, "dp", "tensor")
    norm = P(None, None, ("dp", "tensor"))
    time = P(None, ("dp", "tensor"), None)
    return jax.shard_map(
        functools.partial(per_device, rep),
        mesh=mesh,
        in_specs=(rows, rows, P("dp"), P("dp")) + (shard,) * 3 + (trans,) * 3 + (flat,) * 3 + (trans,) * 6 + (norm,) * 3 + (time,) * 3,
        out_specs=(rows, rows, shard, shard, shard, flat) + (trans,) * 3 + (flat,) * 3 + (trans,) * 6 + (norm,) * 3 + (time,) * 3,
        check_vma=False,
    )
```

time: 341 us -> 289 us (0.85)
  Pallas kernels: 316 us -> 269 us
  other arithmetic: 12.6 us -> 1.26 us
  local copies, waits for them, and re-layouts: 11 us -> 17 us
    pallas_call x1, Pallas kernels: 177 us -> 141 us  [backward_call(): pl.pallas_call(functools.partial(backward_kernel, rep), name='backward',...]
    pallas_call x1, Pallas kernels: 139 us -> 127 us  [forward_call(): pl.pallas_call(functools.partial(forward_kernel, rep), name='forward', in...]
    sub x7 -> x0, other arithmetic: 11.3 us -> none  [adamw(): weight - rate * (first_corr / (jnp.sqrt(second_corr) + adam_eps) + weight...]
    unnamed x34 -> x53, local copies, waits for them, and re-layouts: 6.53 us -> 14.8 us
where the time goes in v2:
time: 289 us
  Pallas kernels  269 us (93%)
  local copies, waits for them, and re-layouts  17 us (6%)
    pallas_call x1, Pallas kernels, backward_call(): pl.pallas_call(functools.partial(backward_kernel, rep), name='backward',...  141 us
    pallas_call x1, Pallas kernels, forward_call(): pl.pallas_call(functools.partial(forward_kernel, rep), name='forward', in...  127 us
    unnamed x53, local copies, waits for them, and re-layouts  14.8 us

profile of v2, /device:TPU:0, one launch (start us, length us, event | category | flops | bytes accessed | tf_op | source)
XLA Modules:
  0.0 288.5 jit_solution(10834970487598166493)
XLA Ops:
  0.7 0.8 copy.55
  1.5 0.7 copy.52
  2.2 0.1 tile.20
  2.3 0.6 fusion.norm_ref
  2.9 0.1 copy.54
  3.0 0.6 fusion.1.bias_ref
  3.6 1.3 jit_solution_.3.freq_ref
  4.9 127.1 %forward.1 = (bf16[2,12,2,4,4,32,256]{6,5,4,3,2,1,0:T(8,128)(2,1)}, f32[16,512]{1,0:T(8,128)}, f32[8,512]{1,0:T(8,128)}, f32[2,1280,512]{2,1,0:T(8,128)}, f32[2,...) custom-call(s32[10]{0:T(128)} %steps_ref.1, ...), custom_call_target="tpu_custom_call" | custom-call | tf_op jit(solution)/shard_map/forward/pallas_call | solution.py:411
  132.0 0.0 copy-start
  132.0 0.0 copy-start.1
  132.0 0.0 copy-start.3
  132.0 0.0 copy-start.4
  132.0 0.0 copy-start.5
  132.1 0.0 copy-start.6
  132.1 0.0 copy-start.7
  132.1 0.0 copy-start.8
  132.1 0.0 copy-start.9
  132.1 0.0 copy-start.12
  132.1 0.0 copy-start.13
  132.1 140.6 %backward.1 = (bf16[1280,512]{1,0:T(8,128)(2,1)}, f32[2,13,32,256]{3,2,1,0:T(8,128)}, f32[2,16,512]{2,1,0:T(8,128)}, f32[2,16,512]{2,1,0:T(8,128)}) custom-call(f32[10]{0:T(128)} %scale_ref.1, f32[16,512]{1,0:T(8,128)} %get-tuple-element.62.small_ref, f32[8,512]{1,0:T(8,128)} %get-tuple-element.63.feats_ref, bf16[1280,512]{1,0:T(8,128)(2,1)} %cot_ref.1, ...), custom_call_target="tpu_custom_call" | custom-call | tf_op jit(solution)/shard_map/backward/pallas_call | solution.py:793
  272.7 0.0 copy-done
  272.7 0.0 copy-done.1
  272.7 0.0 copy-done.3
  272.7 0.0 copy-done.4
  272.8 0.0 copy-done.5
  272.8 0.0 copy-done.6
  272.8 0.0 copy-done.7
  272.8 0.0 copy-done.8
  272.8 0.0 copy-done.9
  272.8 0.0 copy-done.12
  272.8 0.0 copy-done.13
  272.8 0.0 copy-start.2
  272.8 1.1 copy-done.2
  274.0 0.0 copy-start.10
  274.0 0.9 copy-done.10
  274.9 0.0 copy-start.11
  274.9 0.9 copy-done.11
  275.8 0.0 copy-start.14
  275.8 0.8 copy-done.14
  276.7 0.0 copy-start.15
  276.7 0.8 copy-done.15
  277.5 0.0 copy-start.16
  277.5 0.8 copy-done.16
  278.4 0.0 copy-start.17
  278.4 0.8 copy-done.17
  279.2 0.0 copy-start.18
  279.2 0.7 copy-done.18
  279.9 0.0 copy-start.19
  279.9 0.7 copy-done.19
  280.6 0.0 copy-start.20
  280.6 0.7 copy-done.20
  281.3 0.0 copy-start.21
  281.3 0.7 copy-done.21
  282.0 0.0 copy-start.22
  282.0 0.7 copy-done.22
  282.7 0.0 copy-start.23
  282.7 0.7 copy-done.23
  283.4 0.0 copy-start.24
  283.4 1.7 update.1
  285.0 2.5 copy.58
  287.5 0.0 copy-done.24
  287.5 1.1 copy.59
  (8 shorter events, 0.1 us)
Async XLA Ops:
  132.0 140.7 %copy-start = (f32[2,32,1024]{2,1,0:T(8,128)S(1)}, f32[2,32,1024]{2,1,0:T(8,128)}, u32[]{:S(2)}) copy-start(f32[2,32,1024]{2,1,0:T(8,128)} %refs_6_.1) | copy-start | bytes 786436
  132.0 140.7 %copy-start.1 = (f32[2,1024,32]{1,2,0:T(8,128)S(1)}, f32[2,1024,32]{1,2,0:T(8,128)}, u32[]{:S(2)}) copy-start(f32[2,1024,32]{1,2,0:T(8,128)} %param.42) | copy-start | bytes 786436
  132.0 140.7 %copy-start.3 = (f32[2,32,3,256]{3,1,2,0:T(8,128)S(1)}, f32[2,32,3,256]{3,1,2,0:T(8,128)}, u32[]{:S(2)}) copy-start(f32[2,32,3,256]{3,1,2,0:T(8,128)} %param.30) | copy-start | bytes 589828
  132.0 140.7 %copy-start.4 = (f32[2,256,32]{1,2,0:T(8,128)S(1)}, f32[2,256,32]{1,2,0:T(8,128)}, u32[]{:S(2)}) copy-start(f32[2,256,32]{1,2,0:T(8,128)} %param.33) | copy-start | bytes 196612
  132.0 140.7 %copy-start.5 = (f32[2,16,512]{2,1,0:T(8,128)S(1)}, f32[2,16,512]{2,1,0:T(8,128)}, u32[]{:S(2)}) copy-start(f32[2,16,512]{2,1,0:T(8,128)} %refs_18_.1) | copy-start | bytes 196612
  132.1 140.7 %copy-start.6 = (f32[2,32,1024]{2,1,0:T(8,128)S(1)}, f32[2,32,1024]{2,1,0:T(8,128)}, u32[]{:S(2)}) copy-start(f32[2,32,1024]{2,1,0:T(8,128)} %refs_7_.1) | copy-start | bytes 786436
  132.1 140.7 %copy-start.7 = (f32[2,32,1024]{2,1,0:T(8,128)S(1)}, f32[2,32,1024]{2,1,0:T(8,128)}, u32[]{:S(2)}) copy-start(f32[2,32,1024]{2,1,0:T(8,128)} %refs_8_.1) | copy-start | bytes 786436
  132.1 140.7 %copy-start.8 = (f32[2,1024,32]{1,2,0:T(8,128)S(1)}, f32[2,1024,32]{1,2,0:T(8,128)}, u32[]{:S(2)}) copy-start(f32[2,1024,32]{1,2,0:T(8,128)} %param.43) | copy-start | bytes 786436
  132.1 140.7 %copy-start.9 = (f32[2,1024,32]{1,2,0:T(8,128)S(1)}, f32[2,1024,32]{1,2,0:T(8,128)}, u32[]{:S(2)}) copy-start(f32[2,1024,32]{1,2,0:T(8,128)} %param.44) | copy-start | bytes 786436
  132.1 140.7 %copy-start.12 = (f32[2,256,32]{1,2,0:T(8,128)S(1)}, f32[2,256,32]{1,2,0:T(8,128)}, u32[]{:S(2)}) copy-start(f32[2,256,32]{1,2,0:T(8,128)} %param.34) | copy-start | bytes 196612
  132.1 140.7 %copy-start.13 = (f32[2,256,32]{1,2,0:T(8,128)S(1)}, f32[2,256,32]{1,2,0:T(8,128)}, u32[]{:S(2)}) copy-start(f32[2,256,32]{1,2,0:T(8,128)} %param.35) | copy-start | bytes 196612
  272.8 1.2 copy-start.2
  274.0 0.9 copy-start.10
  274.9 0.9 copy-start.11
  275.8 0.8 copy-start.14
  276.7 0.8 copy-start.15
  277.5 0.8 copy-start.16
  278.4 0.8 copy-start.17
  279.2 0.7 copy-start.18
  279.9 0.7 copy-start.19
  280.6 0.7 copy-start.20
  281.3 0.7 copy-start.21
  282.0 0.7 copy-start.22
  282.7 0.7 copy-start.23
  283.4 4.1 %copy-start.24 = (bf16[1280,512]{1,0:T(8,128)(2,1)S(1)}, bf16[1280,512]{1,0:T(8,128)(2,1)}, u32[]{:S(2)}) copy-start(bf16[1280,512]{1,0:T(8,128)(2,1)} %get-tuple-element.127) | copy-start | bytes 3932164

commit v3 on v2

--- a/solution.py
+++ b/solution.py
@@ -3,7 +3,6 @@
 
 import jax
 import jax.numpy as jnp
-import numpy as np
 from jax import lax
 from jax.experimental import pallas as pl
 from jax.experimental.pallas import tpu as pltpu
@@ -15,7 +14,6 @@
 STEP = 8
 GROUPS = 16
 MESH = pl.DeviceIdType.MESH
-LAG = 2
 F32 = jnp.float32
 BF16 = jnp.bfloat16
 
@@ -52,19 +50,8 @@
 
 
 def gelu_and_slope(x):
-    size = jnp.abs(x)
-    denom = 1.0 + (0.3275911 / math.sqrt(2.0)) * size
-    t = pl.reciprocal(denom, approx=True)
-    t = t * (2.0 - denom * t)
-    bell = jnp.exp(x * x * -0.5)
-    poly = 0.5 * 1.061405429
-    poly = poly * t + 0.5 * -1.453152027
-    poly = poly * t + 0.5 * 1.421413741
-    poly = poly * t + 0.5 * -0.284496736
-    poly = poly * t + 0.5 * 0.254829592
-    tail = poly * t * bell
-    below = jnp.where(x >= 0.0, 1.0 - tail, tail)
-    return x * below, below + x * bell * (1.0 / math.sqrt(2.0 * math.pi))
+    below = 0.5 + 0.5 * lax.erf(x * math.sqrt(0.5))
+    return x * below, below + x * (jnp.exp(x * x * -0.5) * (1.0 / math.sqrt(2.0 * math.pi)))
 
 
 class Place:
@@ -168,36 +155,84 @@
         piece.step(number)
 
 
-def stagger(pieces, numbers, lag=1):
-    events = []
-    for turn in range(len(pieces) + lag * (len(numbers) - 1)):
-        for place, number in enumerate(numbers):
-            if 0 <= turn - lag * place < len(pieces):
-                events.append((pieces[turn - lag * place], number))
-    return events
-
-
-def share(events, counts):
-    runs = []
-    for count in counts:
-        runs.append(events[:count])
-        events = events[count:]
-    return runs + [events]
-
-
-def each_item(body, agenda, items, in_specs, out_specs, refs):
+class Timeline:
+    def __init__(self):
+        self.now = 0.0
+        self.queue = []
+        self.links = 0.0
+        self.along = 0.0
+        self.count = 0
+
+    def push(self, piece, dues):
+        for number, due in enumerate(dues, 1):
+            turn = self.count + (number - 1) * LAG
+            self.queue.append((turn, number if FIRST else -number, due, number, piece))
+        self.queue.sort(key=lambda event: event[:2])
+        self.count += 1
+
+    def gather(self, piece, unit):
+        self.along += 4 * unit
+        arrived = self.along + WAIT
+        begun = max(self.links, arrived)
+        self.links = begun + 6 * unit
+        columns, diagonal = begun + 4 * unit + WAIT, begun + 8 * unit + WAIT
+        self.push(piece, [max(arrived, begun - LEAD), columns, diagonal, diagonal + 1.6 * unit + WAIT])
+
+    def scatter(self, piece, unit):
+        added = self.now + 1.6 * unit + WAIT
+        begun = max(self.links, added)
+        self.links = begun + 6 * unit
+        summed = begun + 8 * unit + WAIT
+        self.along = max(self.along, summed) + 4 * unit
+        self.push(piece, [max(added, begun - LEAD), begun + 4 * unit + WAIT, summed, self.along + WAIT])
+
+    def small(self, piece):
+        self.push(piece, [self.now + 3.0 * number for number in (1, 2, 3, 4)])
+
+    def take(self, count):
+        ready, self.queue = self.queue[:count], self.queue[count:]
+        return [(piece, number) for _, _, _, number, piece in ready]
+
+    def slot(self, length):
+        count = 0
+        while count < len(self.queue) and self.queue[count][2] <= self.now:
+            count += 1
+        self.now += length + COST * count
+        return self.take(count)
+
+    def passed(self, length):
+        self.now += length
+
+    def force(self, *wanted):
+        count = max([i + 1 for i, event in enumerate(self.queue) if (event[4], event[3]) in wanted], default=0)
+        self.now = max([self.now] + [event[2] for event in self.queue[:count]])
+        return self.take(count)
+
+
+WAIT = 2.0
+LEAD = 2.0
+LAG = 2
+FIRST = True
+COST = 0.2
+UNIT = 0.33
+
+
+def each_item(body, slots, count, in_specs, out_specs, refs):
     def whole(*blocks):
         item = pl.program_id(0)
-        for number, events in enumerate(agenda[:-1]):
-            if events:
-                pl.when(item == number)(functools.partial(play, events))
-        body(item, *blocks)
-
-    pltpu.emit_pipeline(whole, grid=(items,), in_specs=in_specs, out_specs=out_specs)(*refs)
-    play(agenda[-1])
-
-
-GATHER_PIECES = 12
+
+        def poll(half):
+            for number, events in enumerate(slots):
+                if events[half]:
+                    pl.when(item == number)(functools.partial(play, events[half]))
+
+        poll(0)
+        body(item, lambda: poll(1), *blocks)
+
+    pltpu.emit_pipeline(whole, grid=(count,), in_specs=in_specs, out_specs=out_specs)(*refs)
+
+
+GATHER_PIECES = 16
 
 
 def weight(ref, group):
@@ -206,26 +241,14 @@
 
 def forward_kernel(
     rep,
-    steps_ref, freq_ref, x_ref, qkv_ref, out_ref, up_ref, down_ref, time_ref, norm_ref, bias_ref,
+    steps_ref, x_ref, qkv_ref, out_ref, up_ref, down_ref, time_ref, norm_ref, bias_ref,
     w_out, small_out, feats_out, entry_out, middle_out, qkv_out, probs_out, attn_out, hidden_out, slope_out, act_out,
-    w, tw, nb, norms, bias, shifts, stream, attn, send, recv, keep_sem,
+    w, tw, nb, norms, bias, shifts, stream, attn, rounded, tile, send, recv, keep_sem, act_sem,
 ):
     place = Place(rep)
     z, yx, t = place.z, place.yx, place.t
-    items = stream.shape[0] // LENGTH
-
-    for layer in range(LAYERS):
-        for slot in range(3):
-            w[layer, slot, t, z, yx] = qkv_ref[layer, slot].astype(BF16)
-        w[layer, 3, t, z, yx] = out_ref[layer].astype(BF16)
-        for part in range(4):
-            own = slice(part * 256, (part + 1) * 256)
-            w[layer, 4 + part, t, z, yx] = up_ref[layer, :, own].astype(BF16)
-            w[layer, 8 + part, t, z, yx] = down_ref[layer, :, own].astype(BF16)
-        tw[layer, t, z, yx] = time_ref[layer].astype(BF16)
-    nb[0, t, z, yx] = norm_ref[...]
-    nb[1, t, z, yx] = bias_ref[...]
-    place.greet()
+    rows = stream.shape[0]
+    items = rows // LENGTH
 
     pieces = []
 
@@ -242,33 +265,63 @@
         )
         return pieces[-1]
 
-    norm_piece = piece(nb, 0)
-    time_pieces, layer_pieces = [], []
+    norm_piece, bias_piece = piece(nb, 0), piece(nb, 1)
+    time_pieces = [piece(tw, layer) for layer in range(LAYERS)]
+    spans = ((0, 3), (3, 1), (4, 2), (6, 2), (8, 2), (10, 2))
+    layer_pieces = [[piece(w, layer, pl.ds(*span)) for span in spans] for layer in range(LAYERS)]
+
+    tile[...] = jnp.zeros(tile.shape, F32)
     for layer in range(LAYERS):
-        time_pieces.append(piece(tw, layer))
-        layer_pieces.append([piece(w, layer, pl.ds(first, count)) for first, count in ((0, 3), (3, 1), (4, 4), (8, 4))])
-        if layer == 0:
-            bias_piece = piece(nb, 1)
+        for row in range(5):
+            at = layer * 5 + row
+            tile[0, at : at + 1, 0:16] = norm_ref[row, layer : layer + 1]
+        tile[1, layer * 8 : (layer + 1) * 8, 0:8] = bias_ref[layer]
+    nb[0, t, z, yx] = pltpu.roll(tile[0], (yx * 2 + t) * 16, 1)
+    nb[1, t, z, yx] = pltpu.roll(tile[1], place.group * 8, 1)
+
+    def own_attention(layer):
+        tw[layer, t, z, yx] = time_ref[layer].astype(BF16)
+        for slot in range(3):
+            w[layer, slot, t, z, yx] = qkv_ref[layer, slot].astype(BF16)
+
+    def own_feed(layer):
+        w[layer, 3, t, z, yx] = out_ref[layer].astype(BF16)
+        for part in range(4):
+            own = slice(part * 256, (part + 1) * 256)
+            w[layer, 4 + 2 * part, t, z, yx] = up_ref[layer, :, own].astype(BF16)
+            w[layer, 5 + 2 * part, t, z, yx] = down_ref[layer, :, own].astype(BF16)
+
+    own_attention(0)
+    place.greet()
     opening = [norm_piece, time_pieces[0], layer_pieces[0][0]]
     rest = [layer_pieces[0][1], bias_piece] + layer_pieces[0][2:] + [time_pieces[1]] + layer_pieces[1]
-    for entry in opening + rest:
+    for entry in opening:
+        entry.step(0)
+    own_feed(0)
+    own_attention(1)
+    own_feed(1)
+    for entry in rest:
         entry.step(0)
     for number in (1, 2, 3):
         for entry in opening:
             entry.step(number)
-    events = stagger(rest, (1, 2, 3, 4), LAG)
-
-    def until(entry):
-        last = events.index((entry, 4)) + 1
-        first, events[:] = events[:last], events[last:]
-        return first
-
-    rows = lax.broadcasted_iota(jnp.int32, (8, 256), 0)
+
+    times = Timeline()
+    times.along, times.links = 6.0, 1.0
+    for entry in rest:
+        count = 0.25 if entry is bias_piece else 2 if entry is time_pieces[1] else None
+        if count is None:
+            count = [span[1] for layer in layer_pieces for one, span in zip(layer, spans) if one is entry][0]
+        times.gather(entry, UNIT * count)
+    times.now = 4.0
+
+    line = lax.broadcasted_iota(jnp.int32, (8, 256), 0)
+    column = lax.broadcasted_iota(jnp.int32, (8, 256), 1).astype(F32)
     angles = jnp.zeros((8, 256), F32)
     for item in range(items):
-        step_value = steps_ref[t * items + item].astype(F32)
-        angles = jnp.where(rows == item, step_value * freq_ref[0:1, :], angles)
-    live = rows < items
+        angles = jnp.where(line == item, steps_ref[t * items + item].astype(F32), angles)
+    angles = angles * jnp.exp(column * (-math.log(10000.0) / 256))
+    live = line < items
     feats = jnp.concatenate(
         [jnp.where(live, jnp.sin(angles), 0.0), jnp.where(live, jnp.cos(angles), 0.0)], 1
     )
@@ -301,15 +354,15 @@
                     for half in range(2):
                         row = layer * 8 + part * 2 + half
                         col = core * 256 + half * 128
-                        bias[layer * 4 + part : layer * 4 + part + 1, col : col + 128] = total[row : row + 1]
+                        bias[layer, part, 0:1, col : col + 128] = total[row : row + 1]
 
     lane = lax.broadcasted_iota(jnp.int32, (1, 128), 1)
-    even = lane < HEAD_DIM
-    even_mask = jnp.where(even, 1.0, 0.0).astype(BF16)
-    odd_mask = jnp.where(even, 0.0, 1.0).astype(BF16)
-
-    def attention_phase(layer, agenda):
-        def body(item, *refs):
+    even_mask = jnp.where(lane < HEAD_DIM, 1.0, 0.0).astype(BF16)
+    odd_mask = jnp.where(lane < HEAD_DIM, 0.0, 1.0).astype(BF16)
+    wide = lambda cols: pl.BlockSpec((LENGTH, cols), lambda i: (i, 0))
+
+    def attention_phase(layer):
+        def body(item, poll, *refs):
             if layer == 0:
                 x_blk, *refs = refs
             entry_blk, qkv_blk, probs_blk, attn_blk = refs
@@ -325,84 +378,127 @@
                 if slot == 0:
                     projected = projected * jnp.asarray(HEAD_DIM**-0.5, BF16)
                 qkv_blk[:, slot * 512 : (slot + 1) * 512] = projected
+
+            def scores(pair):
+                query = qkv_blk[:, pair * 128 : (pair + 1) * 128]
+                key = qkv_blk[:, 512 + pair * 128 : 512 + (pair + 1) * 128]
+                return [nt(query * mask, key) for mask in (even_mask, odd_mask)]
+
+            ahead = scores(0)
             for pair in range(4):
+                both = ahead
+                if pair < 3:
+                    ahead = scores(pair + 1)
                 span = slice(pair * 128, (pair + 1) * 128)
-                query = qkv_blk[:, span]
-                key = qkv_blk[:, 512 + pair * 128 : 512 + (pair + 1) * 128]
                 value = qkv_blk[:, 1024 + pair * 128 : 1024 + (pair + 1) * 128]
-                mixed = []
-                for side, mask in enumerate((even_mask, odd_mask)):
-                    scores = nt(query * mask, key)
-                    raised = jnp.exp(scores - jnp.max(scores, -1, keepdims=True))
-                    probs = (raised * (1.0 / jnp.sum(raised, -1, keepdims=True))).astype(BF16)
-                    probs_blk[0, pair * 2 + side] = probs
-                    mixed.append(nn(probs, value))
-                joined = jnp.where(even, mixed[0], mixed[1]).astype(BF16)
+                probs = []
+                for side in range(2):
+                    raised = jnp.exp(both[side] - jnp.max(both[side], -1, keepdims=True))
+                    probs.append((raised * (1.0 / jnp.sum(raised, -1, keepdims=True))).astype(BF16))
+                    probs_blk[0, pair * 2 + side] = probs[side]
+                values = jnp.concatenate([value * even_mask, value * odd_mask], 0)
+                joined = nn(jnp.concatenate(probs, 1), values).astype(BF16)
                 attn_blk[:, span] = joined
                 attn[here, span] = joined
 
-        wide = lambda cols: pl.BlockSpec((LENGTH, cols), lambda i: (i, 0))
         each_item(
-            body, agenda, items,
+            body, [(times.slot(ATTENTION), []) for _ in range(items)], items,
             [wide(512)] if layer == 0 else [],
             [wide(512), wide(1536), pl.BlockSpec((1, 8, 256, 256), lambda i: (i, 0, 0, 0)), wide(512)],
             ([x_ref] if layer == 0 else [])
             + [entry_out.at[layer], qkv_out.at[layer], probs_out.at[layer], attn_out.at[layer]],
         )
 
-    def feed_phase(layer, agenda):
-        def body(item, middle_blk, hidden_blk, slope_blk, *rest):
+    def middle_phase(layer):
+        def body(item, poll, middle_blk):
             here = pl.ds(pl.multiple_of(item * LENGTH, LENGTH), LENGTH)
             middle = stream[here] + nt(attn[here], weight(w.at[layer], 3))
             middle_blk[...] = middle
             hat, _ = normalize(middle)
-            normed = (hat * norms[layer * 5 + 2 : layer * 5 + 3] + norms[layer * 5 + 3 : layer * 5 + 4]).astype(BF16)
-            total = middle + norms[layer * 5 + 4 : layer * 5 + 5]
-            for part in range(4):
-                row = layer * 4 + part
-                span = slice(part * 512, (part + 1) * 512)
-                pre = nn(normed, weight(w.at[layer], 4 + part)) + bias[row : row + 1]
+            normed = hat * norms[layer * 5 + 2 : layer * 5 + 3] + norms[layer * 5 + 3 : layer * 5 + 4]
+            rounded[here] = normed.astype(BF16)
+            stream[here] = middle + norms[layer * 5 + 4 : layer * 5 + 5]
+
+        slots = [(times.slot(MIDDLE), []) for _ in range(items)]
+        each_item(body, slots, items, [], [wide(512)], [middle_out.at[layer]])
+
+    def feed_phase(layer, keep):
+        def body(part, poll, hidden_blk, slope_blk):
+            blocks = [slice(i * LENGTH, (i + 1) * LENGTH) for i in range(items)]
+            up, down, shift = weight(w.at[layer], 4 + 2 * part), weight(w.at[layer], 5 + 2 * part), bias[layer, part]
+            lift = lambda i: nn(rounded[blocks[i]], up) + shift[0:1]
+
+            def lower(i, hidden):
+                stream[blocks[i]] += nt(hidden, down)
+
+            ahead, held = lift(0), None
+            for i in range(items):
+                pre = ahead
+                if i + 1 < items:
+                    ahead = lift(i + 1)
                 hidden, slope = gelu_and_slope(pre)
-                hidden = hidden.astype(BF16)
-                hidden_blk[:, span] = hidden
-                slope_blk[:, span] = slope.astype(BF16)
-                total = total + nt(hidden, weight(w.at[layer], 8 + part))
-            if layer == LAYERS - 1:
-                rest[0][...] = total.astype(BF16)
-            else:
-                stream[here] = total
-
-        wide = lambda cols: pl.BlockSpec((LENGTH, cols), lambda i: (i, 0))
-        last = layer == LAYERS - 1
-        each_item(
-            body, agenda, items, [],
-            [wide(512), wide(2048), wide(2048)] + ([wide(512)] if last else []),
-            [middle_out.at[layer], hidden_out.at[layer], slope_out.at[layer]] + ([act_out] if last else []),
-        )
+                if held is not None:
+                    lower(i - 1, held)
+                held = hidden.astype(BF16)
+                hidden_blk[blocks[i]] = held
+                slope_blk[blocks[i]] = slope.astype(BF16)
+            lower(items - 1, held)
+
+        slots = []
+        for part in range(4):
+            entry = layer_pieces[layer][2 + part]
+            slots.append((times.force((entry, 4)) + [(Start(keep[2 + part]), 0)], []))
+            times.passed(FEED)
+        tall = pl.BlockSpec((rows, 512), lambda i: (0, i))
+        each_item(body, slots, 4, [], [tall, tall], [hidden_out.at[layer], slope_out.at[layer]])
 
     spread_times(0)
     keeps = []
     for layer in range(LAYERS):
-        qkv_piece, out_piece, up_piece, down_piece = layer_pieces[layer]
+        keep = [
+            pltpu.make_async_copy(w.at[layer, pl.ds(*span)], w_out.at[layer, pl.ds(*span)], keep_sem.at[layer, i])
+            for i, span in enumerate(spans)
+        ]
+        keeps += keep
         if layer > 0:
+            play(times.force((time_pieces[layer], 4), (layer_pieces[layer][0], 4)))
             spread_times(layer)
-        attention_phase(layer, share(until(down_piece), AGENDA[layer][0]))
+        keep[0].start()
+        attention_phase(layer)
+        play(times.force((layer_pieces[layer][1], 4), (bias_piece, 4)))
+        keep[1].start()
         if layer == 0:
             spread_bias()
-        keep = pltpu.make_async_copy(w.at[layer], w_out.at[layer], keep_sem.at[layer])
-        keep.start()
-        keeps.append(keep)
-        feed_phase(layer, share(until(layer_pieces[1][0]) if layer == 0 else [], AGENDA[layer][1]))
+        middle_phase(layer)
+        feed_phase(layer, keep)
+
+    def finish_rows(item, carry):
+        here = pl.ds(pl.multiple_of(item * LENGTH, LENGTH), LENGTH)
+        rounded[here] = stream[here].astype(BF16)
+        return carry
+
+    lax.fori_loop(0, items, finish_rows, 0)
+    last = pltpu.make_async_copy(rounded, act_out, act_sem)
+    last.start()
     for entry in pieces:
         entry.finish()
-    for keep in keeps:
-        keep.wait()
-
-
-AGENDA = (((1, 2, 2, 3, 3), (2, 3, 3, 3, 3)), ((2, 3, 3, 3, 3), ()))
-
-
-def forward_call(rep, rows, steps, freq, x, qkv, out, up, down, time, norm, bias):
+    for copy in keeps + [last]:
+        copy.wait()
+
+
+ATTENTION, MIDDLE, FEED = 2.4, 0.8, 2.6
+FEED_BACK, ATTENTION_BACK, GRAD = 2.2, 4.0, 0.9
+
+
+class Start:
+    def __init__(self, copy):
+        self.copy = copy
+
+    def step(self, number):
+        self.copy.start()
+
+
+def forward_call(rep, rows, steps, x, qkv, out, up, down, time, norm, bias):
     items = rows // LENGTH
     hbm = pl.BlockSpec(memory_space=pl.ANY)
     vmem = pl.BlockSpec(memory_space=pltpu.VMEM)
@@ -411,7 +507,7 @@
     return pl.pallas_call(
         functools.partial(forward_kernel, rep),
         name="forward",
-        in_specs=[smem, vmem, hbm] + [vmem] * 7,
+        in_specs=[smem, hbm] + [vmem] * 7,
         out_shape=[
             shape((LAYERS, 12, 2, 4, 4, 32, 256), BF16),
             shape((16, 512), F32),
@@ -431,16 +527,19 @@
             pltpu.VMEM((LAYERS, 2, 4, 4, 16, 512), BF16),
             pltpu.VMEM((2, 2, 4, 4, 16, 128), F32),
             pltpu.VMEM((16, 512), F32),
-            pltpu.VMEM((8, 512), F32),
+            pltpu.VMEM((LAYERS, 4, 8, 512), F32),
             pltpu.VMEM((16, 512), F32),
             pltpu.VMEM((rows, 512), F32),
             pltpu.VMEM((rows, 512), BF16),
+            pltpu.VMEM((rows, 512), BF16),
+            pltpu.VMEM((2, 16, 128), F32),
             pltpu.SemaphoreType.DMA((GATHER_PIECES, 8)),
             pltpu.SemaphoreType.DMA((GATHER_PIECES, 8)),
-            pltpu.SemaphoreType.DMA((LAYERS,)),
+            pltpu.SemaphoreType.DMA((LAYERS, 6)),
+            pltpu.SemaphoreType.DMA,
         ],
         compiler_params=pltpu.CompilerParams(collective_id=1, has_side_effects=True, vmem_limit_bytes=56 << 20),
-    )(steps, freq, x, qkv, out, up, down, time, norm, bias)
+    )(steps, x, qkv, out, up, down, time, norm, bias)
 
 
 class Scatter(Exchange):
@@ -560,7 +659,6 @@
 
 GRAD_GROUPS = 13
 SCATTER_PIECES = ((4, 2), (6, 2), (8, 2), (10, 2), (3, 1), (0, 1), (1, 1), (2, 1), (12, 1))
-BACK_AGENDA = ((3, 3, 3, 3, 3), (4, 4, 4, 4, 4))
 
 
 def backward_kernel(
@@ -577,9 +675,9 @@
     items = rows // LENGTH
     wide = lambda cols: pl.BlockSpec((LENGTH, cols), lambda i: (i, 0))
     lane = lax.broadcasted_iota(jnp.int32, (1, 128), 1)
-    even = lane < HEAD_DIM
-    even_mask = jnp.where(even, 1.0, 0.0).astype(BF16)
-    odd_mask = jnp.where(even, 0.0, 1.0).astype(BF16)
+    even_mask = jnp.where(lane < HEAD_DIM, 1.0, 0.0).astype(BF16)
+    odd_mask = jnp.where(lane < HEAD_DIM, 0.0, 1.0).astype(BF16)
+    times = Timeline()
 
     def load_weights(layer):
         copies = []
@@ -604,10 +702,10 @@
         along = jnp.mean(scaled * hat, -1, keepdims=True)
         return inverse * (scaled - mean - hat * along)
 
-    def feed_phase(layer, agenda):
+    def feed_phase(layer):
         last = layer == LAYERS - 1
 
-        def body(item, middle_blk, slope_blk, *rest):
+        def body(item, poll, middle_blk, slope_blk, *rest):
             here = pl.ds(pl.multiple_of(item * LENGTH, LENGTH), LENGTH)
             if last:
                 grad = rest[0][...].astype(F32) * scale_ref[t * items + item]
@@ -619,11 +717,11 @@
             back = jnp.zeros((LENGTH, 512), F32)
             for part in range(4):
                 span = slice(part * 512, (part + 1) * 512)
-                dh = nn(low, weight(w, 8 + part))
+                dh = nn(low, weight(w, 5 + 2 * part))
                 pre_grad = (dh * slope_blk[:, span].astype(F32)).astype(BF16)
                 du[here, span] = pre_grad
                 acc_bias[part] += fold_rows(pre_grad.astype(F32))
-                back = back + nt(pre_grad, weight(w, 4 + part))
+                back = back + nt(pre_grad, weight(w, 4 + 2 * part))
             hat, inverse = normalize(middle_blk[...])
             normed = hat * small_ref[layer * 5 + 2 : layer * 5 + 3] + small_ref[layer * 5 + 3 : layer * 5 + 4]
             n2t[:, here] = normed.astype(BF16).T
@@ -634,31 +732,51 @@
             dattn[here] = nn(low, weight(w, 3)).astype(BF16)
 
         each_item(
-            body, agenda, items, [wide(512), wide(2048)] + ([wide(512)] if last else []), [],
+            body, [(times.slot(FEED_BACK), []) for _ in range(items)], items, [wide(512), wide(2048)] + ([wide(512)] if last else []), [],
             [middle_in.at[layer], slope_in.at[layer]] + ([cot_ref] if last else []),
         )
 
-    def attention_phase(layer, agenda):
-        def body(item, entry_blk, qkv_blk, probs_blk, *rest):
+    def attention_phase(layer):
+        def body(item, poll, entry_blk, qkv_blk, probs_blk, *rest):
             here = pl.ds(pl.multiple_of(item * LENGTH, LENGTH), LENGTH)
-            for pair in range(4):
-                span = slice(pair * 128, (pair + 1) * 128)
-                query = qkv_blk[:, span]
+            def sides(pair):
+                query = qkv_blk[:, pair * 128 : (pair + 1) * 128]
                 key = qkv_blk[:, 512 + pair * 128 : 512 + (pair + 1) * 128]
                 value = qkv_blk[:, 1024 + pair * 128 : 1024 + (pair + 1) * 128]
-                back = dattn[here, span]
-                found = []
-                for side, mask in enumerate((even_mask, odd_mask)):
-                    probs = probs_blk[0, pair * 2 + side]
-                    dprobs = nt(back * mask, value)
-                    wide_probs = probs.astype(F32)
-                    delta = jnp.sum(wide_probs * dprobs, -1, keepdims=True)
-                    dscores = (wide_probs * (dprobs - delta)).astype(BF16)
-                    found.append((nn(dscores, key), tn(dscores, query), tn(probs, back)))
-                dq, dk, dv = [jnp.where(even, found[0][i], found[1][i]) for i in range(3)]
-                dqkv[here, span] = (dq * HEAD_DIM**-0.5).astype(BF16)
-                dqkv[here, 512 + pair * 128 : 512 + (pair + 1) * 128] = dk.astype(BF16)
-                dqkv[here, 1024 + pair * 128 : 1024 + (pair + 1) * 128] = dv.astype(BF16)
+                back = dattn[here, pair * 128 : (pair + 1) * 128]
+                split = lambda v: [v * even_mask, v * odd_mask]
+                return split(query), split(key), value, split(back)
+
+            def scores(pair):
+                _, _, value, back = sides(pair)
+                return [nt(side, value) for side in back]
+
+            def products(pair, dscores):
+                query, key, _, back = sides(pair)
+                probs = [probs_blk[0, pair * 2 + side] for side in range(2)]
+                tall = jnp.concatenate(dscores, 0)
+                dq = nn(jnp.concatenate(dscores, 1), jnp.concatenate(key, 0)) * HEAD_DIM**-0.5
+                dk = tn(tall, jnp.concatenate(query, 0))
+                dv = tn(jnp.concatenate(probs, 0), jnp.concatenate(back, 0))
+                for slot, value in enumerate((dq, dk, dv)):
+                    dqkv[here, slot * 512 + pair * 128 : slot * 512 + (pair + 1) * 128] = value.astype(BF16)
+
+            ahead, held = scores(0), None
+            for pair in range(4):
+                both = ahead
+                if pair == 2:
+                    poll()
+                if pair < 3:
+                    ahead = scores(pair + 1)
+                dscores = []
+                for side in range(2):
+                    probs = probs_blk[0, pair * 2 + side].astype(F32)
+                    mixed = probs * both[side]
+                    dscores.append((mixed - probs * jnp.sum(mixed, -1, keepdims=True)).astype(BF16))
+                if held is not None:
+                    products(pair - 1, held)
+                held = dscores
+            products(3, held)
             back = jnp.zeros((LENGTH, 512), F32)
             for slot in range(3):
                 back = back + nt(dqkv[here, slot * 512 : (slot + 1) * 512], weight(w, slot))
@@ -672,8 +790,9 @@
             else:
                 gx[here] = grad
 
+        slots = [(times.slot(ATTENTION_BACK / 2), times.slot(ATTENTION_BACK / 2)) for _ in range(items)]
         each_item(
-            body, agenda, items,
+            body, slots, items,
             [wide(512), wide(1536), pl.BlockSpec((1, 8, 256, 256), lambda i: (i, 0, 0, 0))],
             [wide(512)] if layer == 0 else [],
             [entry_in.at[layer], qkv_in.at[layer], probs_in.at[layer]] + ([grad_out] if layer == 0 else []),
@@ -683,13 +802,8 @@
         for half in range(2):
             grads[group, half] = value[:, half * 256 : (half + 1) * 256].astype(BF16).reshape(4, 4, 32, 256)
 
-    def weight_grad(left, right, first, offset, count):
-        def one(part, carry):
-            span = pl.ds(pl.multiple_of((offset + part) * 512, 512), 512)
-            keep_grad(first + part, nn(left[...], right[:, span]))
-            return carry
-
-        lax.fori_loop(0, count, one, 0)
+    def weight_grad(left, right, group, part):
+        keep_grad(group, nn(left[...], right[:, part * 512 : (part + 1) * 512]))
 
     scatters, smalls = [], []
     for layer in range(LAYERS):
@@ -712,56 +826,63 @@
     item_grad[...] = jnp.zeros(item_grad.shape, F32)
     place.greet()
 
-    pending = []
+    def clear(layer, piece):
+        if layer != order[0]:
+            before = scatters[order[order.index(layer) - 1]][scatters[layer].index(piece)]
+            play(times.force((before, 4)))
+            before.finish()
+
+    def begin(piece):
+        piece.step(0)
+        times.scatter(piece, UNIT * piece.count)
+
     for turn, layer in enumerate(order):
         feed_pieces, late_pieces = scatters[layer][:5], scatters[layer][5:]
         acc[...] = jnp.zeros(acc.shape, F32)
         acc_bias[...] = jnp.zeros(acc_bias.shape, F32)
         weights[layer][0].wait()
-        with jax.named_scope("feed_back"):
-            feed_phase(layer, share(pending, BACK_AGENDA[1]))
+        feed_phase(layer)
         stash[layer][0].wait()
         stash[layer][1].wait()
         weights[layer][1].wait()
-        if turn > 0:
-            for piece in scatters[order[turn - 1]]:
-                piece.finish()
-        with jax.named_scope("feed_grads"):
-            made = ((n2t, du, 4, 0), (n2t, du, 6, 2), (gdt, hidden, 8, 0), (gdt, hidden, 10, 2), (got, attn, 3, 0))
-            pending = stagger(feed_pieces, (0, 1, 2, 3, 4), LAG)
-            for piece, (left, right, first, part) in zip(feed_pieces, made):
-                weight_grad(left, right, first, part, piece.count)
-                ready = pending.index((piece, 0)) + 1
-                play(pending[:ready])
-                pending = pending[ready:]
-        with jax.named_scope("attention_back"):
-            attention_phase(layer, share(pending, BACK_AGENDA[0]))
+        for part, piece in enumerate(feed_pieces):
+            clear(layer, piece)
+            if part < 4:
+                weight_grad(n2t, du, 4 + 2 * part, part)
+                weight_grad(gdt, hidden, 5 + 2 * part, part)
+            else:
+                weight_grad(got, attn, 3, 0)
+            times.passed(GRAD * piece.count)
+            begin(piece)
+            play(times.slot(0.0))
+        attention_phase(layer)
         if turn + 1 < LAYERS:
             after = order[turn + 1]
             weights[after] = load_weights(after)
             stash[after] = load_stash(after)
             for copy in weights[after] + stash[after]:
                 copy.start()
-        with jax.named_scope("attention_grads"):
-            spread = lax.dot_general(
-                feats_ref[...], item_grad[...], (((0,), (0,)), ((), ())),
-                precision=lax.Precision.HIGHEST, preferred_element_type=F32,
-            )
-            keep_grad(12, spread)
-            for row in range(5):
-                sums[layer, 0, row : row + 1] = jnp.sum(acc[row], 0, keepdims=True)
-            for part in range(4):
-                sums[layer, 0, 5 + part : 6 + part] = jnp.sum(acc_bias[part], 0, keepdims=True)
-            sums[layer, 0, 9:16] = jnp.zeros((7, 512), F32)
-            late_pieces = [late_pieces[3], smalls[layer]] + late_pieces[:3]
-            pending = stagger(late_pieces, (0, 1, 2, 3, 4), LAG)
-            for slot in range(3):
-                weight_grad(n1t, dqkv, slot, slot, 1)
-                ready = pending.index((late_pieces[2 + slot], 0)) + 1
-                play(pending[:ready])
-                pending = pending[ready:]
-    with jax.named_scope("scatter"):
-        play(pending)
+        for piece in late_pieces:
+            clear(layer, piece)
+        spread = lax.dot_general(
+            feats_ref[...], item_grad[...], (((0,), (0,)), ((), ())),
+            precision=lax.Precision.HIGHEST, preferred_element_type=F32,
+        )
+        keep_grad(12, spread)
+        begin(late_pieces[3])
+        for row in range(5):
+            sums[layer, 0, row : row + 1] = jnp.sum(acc[row], 0, keepdims=True)
+        for part in range(4):
+            sums[layer, 0, 5 + part : 6 + part] = jnp.sum(acc_bias[part], 0, keepdims=True)
+        sums[layer, 0, 9:16] = jnp.zeros((7, 512), F32)
+        smalls[layer].step(0)
+        times.small(smalls[layer])
+        for slot in range(3):
+            weight_grad(n1t, dqkv, slot, slot)
+            times.passed(GRAD)
+            begin(late_pieces[slot])
+            play(times.slot(0.0))
+    play(times.force(*[(piece, 4) for layer in range(LAYERS) for piece in scatters[layer] + [smalls[layer]]]))
 
     swaps = []
     for layer in range(LAYERS):
@@ -848,8 +969,17 @@
     return (weight_new, first_new, second_new)
 
 
-def update_kernel(total, sums, time_grad, *refs):
-    ins, outs, (row,) = refs[:21], refs[21:43], refs[43:]
+def update_kernel(*refs):
+    hbm, outs, ins = refs[:26], refs[26:50], refs[50:74]
+    row, sems = refs[74:]
+    copies = [pltpu.make_async_copy(src, dst, sems.at[i]) for i, (src, dst) in enumerate(zip(hbm[:24], ins))]
+    copies += [pltpu.make_async_copy(hbm[24 + i], outs[i], sems.at[24 + i]) for i in range(2)]
+    for copy in copies:
+        copy.start()
+    for copy in copies[:24]:
+        copy.wait()
+    total, sums, time_grad, *ins = ins
+    outs = outs[2:]
     qkv, out, up, bias, down, norm, time = [ins[i * 3 : i * 3 + 3] for i in range(7)]
     qkv_new, key_second, value_second = outs[0:2], outs[2], outs[3]
     out_new, up_new, bias_new, down_new, norm_new, time_new = [outs[4 + i * 3 : 7 + i * 3] for i in range(6)]
@@ -873,8 +1003,8 @@
         one(out, out_new, (layer,), total[layer, 3], learn_rate)
         for part in range(4):
             where = (layer, slice(None), slice(part * 256, (part + 1) * 256))
-            one(up, up_new, where, total[layer, 4 + part], learn_rate)
-            one(down, down_new, where, total[layer, 8 + part], learn_rate)
+            one(up, up_new, where, total[layer, 4 + 2 * part], learn_rate)
+            one(down, down_new, where, total[layer, 5 + 2 * part], learn_rate)
         one(time, time_new, (layer,), time_grad[layer], learn_rate)
 
         width = norm[0].shape[2]
@@ -889,27 +1019,31 @@
         width = bias[0].shape[2]
         mine = pltpu.roll(row[...], (128 - dp * width) % 128, 1)[:, 0:width]
         one(bias, bias_new, (layer,), mine, learn_rate)
-
-
-def update_call(total, sums, time_grad, states):
-    flat = [array for state in states for array in state]
-    like = lambda array: jax.ShapeDtypeStruct(array.shape, F32)
+    for copy in copies[24:]:
+        copy.wait()
+
+
+def update_call(total, sums, time_grad, states, row_results):
+    flat = [total, sums, time_grad] + [array for state in states for array in state]
+    like = lambda array: jax.ShapeDtypeStruct(array.shape, array.dtype)
     rows = states[0][0].shape[2]
-    shapes = [like(array) for array in flat]
-    shapes[2:3] = [
+    shapes = [like(array) for array in list(row_results) + flat[3:]]
+    shapes[4:5] = [
         jax.ShapeDtypeStruct((LAYERS, rows, 2, 256), F32),
         jax.ShapeDtypeStruct((LAYERS, rows, 256), F32),
     ]
     vmem = pl.BlockSpec(memory_space=pltpu.VMEM)
+    hbm = pl.BlockSpec(memory_space=pl.ANY)
     return pl.pallas_call(
         update_kernel,
         name="update",
-        in_specs=[vmem] * 24,
+        in_specs=[hbm] * 26,
         out_shape=shapes,
-        out_specs=[vmem] * 22,
-        scratch_shapes=[pltpu.VMEM((8, 128), F32)],
-        compiler_params=pltpu.CompilerParams(vmem_limit_bytes=48 << 20),
-    )(total, sums, time_grad, *flat)
+        out_specs=[hbm] * 2 + [vmem] * 22,
+        scratch_shapes=[pltpu.VMEM(array.shape, F32) for array in flat]
+        + [pltpu.VMEM((8, 128), F32), pltpu.SemaphoreType.DMA((26,))],
+        compiler_params=pltpu.CompilerParams(vmem_limit_bytes=56 << 20),
+    )(*flat, *row_results)
 
 
 def per_device(
@@ -925,7 +1059,6 @@
 ):
     rows = inputs.shape[0]
     dp, t = lax.axis_index("dp"), lax.axis_index("tensor")
-    group = dp // rep
     qkv, out, up, down, bias = qkv_weight, out_weight, up_weight, down_weight, up_bias
     norm, time = norm_params, time_weight
     teams = None
@@ -942,19 +1075,11 @@
         norm = lax.dynamic_slice_in_dim(norm, t * 16, 16, 2)
         time = lax.dynamic_slice_in_dim(time, t * 16, 16, 1)
 
-    lane = lax.broadcasted_iota(jnp.int32, (16, 128), 1)
-    spot = (group % 4) * 2 + t
-    norm_rows = jnp.pad(norm.reshape(10, 16), ((0, 6), (0, 0)))
-    norm_block = jnp.where(lane // 16 == spot, jnp.tile(norm_rows, (1, 8)), 0.0)
-    bias_block = jnp.where(lane // 8 == group, jnp.tile(bias.reshape(16, 8), (1, 16)), 0.0)
-    half_width = 256
-    freq = np.exp(-math.log(10000.0) / half_width * np.arange(half_width)).astype(np.float32)
-    freq = jnp.asarray(np.broadcast_to(freq, (8, half_width)))
-
+    slots = lambda *arrays: [jnp.transpose(v, (0, 2, 1, 3)) for v in arrays]
+    flip = lambda *arrays: [jnp.swapaxes(v, 1, 2) for v in arrays]
+    front = lambda *arrays: [jnp.swapaxes(v, 0, 1) for v in arrays]
     w, small, feats, entry, middle, qkv_rows, probs, attn, hidden, slope, activations = forward_call(
-        rep, rows, timesteps, freq, inputs,
-        jnp.transpose(qkv, (0, 2, 1, 3)), jnp.swapaxes(out, 1, 2), up, jnp.swapaxes(down, 1, 2),
-        time, norm_block, bias_block,
+        rep, rows, timesteps, inputs, *slots(qkv), *flip(out), up, *flip(down), time, *front(norm), bias
     )
     input_grad, total, sums, time_grad = backward_call(
         rep, rows, item_scale, small, feats, cotangent, w, entry, middle, qkv_rows, probs, attn, hidden, slope
@@ -967,10 +1092,7 @@
         width = time_weight.shape[1]
         time_grad = lax.dynamic_slice_in_dim(time_grad, ((dp % rep) * 2 + t) * width, width, 1)
 
-    slots = lambda *arrays: [jnp.transpose(v, (0, 2, 1, 3)) for v in arrays]
-    flip = lambda *arrays: [jnp.swapaxes(v, 1, 2) for v in arrays]
-    front = lambda *arrays: [jnp.swapaxes(v, 0, 1) for v in arrays]
-    new = update_call(
+    activations, input_grad, *new = update_call(
         total, sums, time_grad,
         [
             slots(qkv_weight, qkv_first, qkv_second),
@@ -981,6 +1103,7 @@
             front(norm_params, norm_first, norm_second),
             [time_weight, time_first, time_second],
         ],
+        (activations, input_grad),
     )
     return (
         activations, input_grad,

time: 289 us -> 328 us (1.13)
  Pallas kernels: 269 us -> 327 us
  local copies, waits for them, and re-layouts: 17 us -> 0 us
    pallas_call x1, Pallas kernels: 1.65 us -> 82.4 us  [update_call(): pl.pallas_call(update_kernel, name='update', in_specs=[hbm] * 26, out_sha...]
    pallas_call x1, Pallas kernels: 127 us -> 106 us  [forward_call(): pl.pallas_call(functools.partial(forward_kernel, rep), name='forward', in...]
    unnamed x53 -> x0, local copies, waits for them, and re-layouts: 14.8 us -> none
where the time goes in v3:
time: 328 us
  Pallas kernels  327 us (100%)
    pallas_call x1, Pallas kernels, backward_call(): pl.pallas_call(functools.partial(backward_kernel, rep), name='backward',...  139 us
    pallas_call x1, Pallas kernels, forward_call(): pl.pallas_call(functools.partial(forward_kernel, rep), name='forward', in...  106 us
    pallas_call x1, Pallas kernels, update_call(): pl.pallas_call(update_kernel, name='update', in_specs=[hbm] * 26, out_sha...  82.4 us

profile of v3, /device:TPU:0, one launch (start us, length us, event | category | flops | bytes accessed | tf_op | source)
XLA Modules:
  0.0 327.9 jit_solution(15715985138558545348)
XLA Ops:
  0.7 105.6 %forward.1 = (bf16[2,12,2,4,4,32,256]{6,5,4,3,2,1,0:T(8,128)(2,1)}, f32[16,512]{1,0:T(8,128)}, f32[8,512]{1,0:T(8,128)}, f32[2,1280,512]{2,1,0:T(8,128)}, f32[2,...) custom-call(s32[10]{0:T(128)} %steps_ref.1, ...), custom_call_target="tpu_custom_call" | custom-call | tf_op jit(solution)/shard_map/forward/pallas_call | solution.py:507
  106.3 139.1 %backward.1 = (bf16[1280,512]{1,0:T(8,128)(2,1)}, f32[2,13,32,256]{3,2,1,0:T(8,128)}, f32[2,16,512]{2,1,0:T(8,128)}, f32[2,16,512]{2,1,0:T(8,128)}) custom-call(f32[10]{0:T(128)} %scale_ref.1, f32[16,512]{1,0:T(8,128)} %get-tuple-element.63.small_ref, f32[8,512]{1,0:T(8,128)} %get-tuple-element.64.feats_ref, bf16[1280,512]{1,0:T(8,128)(2,1)} %cot_ref.1, ...), custom_call_target="tpu_custom_call" | custom-call | tf_op jit(solution)/shard_map/backward/pallas_call | solution.py:914
  245.4 82.4 %update.1 = (bf16[1280,512]{1,0:T(8,128)(2,1)}, bf16[1280,512]{1,0:T(8,128)(2,1)}, f32[2,3,32,256]{3,2,1,0:T(8,128)}, f32[2,3,32,256]{3,2,1,0:T(8,128)}, f32[2,3...) custom-call(f32[2,13,32,256]{3,2,1,0:T(8,128)} %get-tuple-element.73, ...), custom_call_target="tpu_custom_call" | custom-call | tf_op jit(solution)/shard_map/update/pallas_call | solution.py:1037

commit v4 on v3

--- a/solution.py
+++ b/solution.py
@@ -209,7 +209,7 @@
         return self.take(count)
 
 
-WAIT = 2.0
+WAIT = 5.0
 LEAD = 2.0
 LAG = 2
 FIRST = True
@@ -486,8 +486,8 @@
         copy.wait()
 
 
-ATTENTION, MIDDLE, FEED = 2.4, 0.8, 2.6
-FEED_BACK, ATTENTION_BACK, GRAD = 2.2, 4.0, 0.9
+ATTENTION, MIDDLE, FEED = 2.2, 0.8, 2.4
+FEED_BACK, ATTENTION_BACK, GRAD = 2.1, 2.7, 0.76
 
 
 class Start:
@@ -1039,7 +1039,7 @@
         name="update",
         in_specs=[hbm] * 26,
         out_shape=shapes,
-        out_specs=[hbm] * 2 + [vmem] * 22,
+        out_specs=[vmem] * 24,
         scratch_shapes=[pltpu.VMEM(array.shape, F32) for array in flat]
         + [pltpu.VMEM((8, 128), F32), pltpu.SemaphoreType.DMA((26,))],
         compiler_params=pltpu.CompilerParams(vmem_limit_bytes=56 << 20),

time: 328 us -> 227 us (0.69)
  Pallas kernels: 327 us -> 225 us
    pallas_call x1, Pallas kernels: 82.4 us -> 5.5 us  [update_call(): pl.pallas_call(update_kernel, name='update', in_specs=[hbm] * 26, out_sha...]
    pallas_call x1, Pallas kernels: 139 us -> 113 us  [backward_call(): pl.pallas_call(functools.partial(backward_kernel, rep), name='backward',...]
where the time goes in v4:
time: 227 us; the launch traced here: 226 us
  Pallas kernels  225 us (99%)
    pallas_call x1, Pallas kernels, backward_call(): pl.pallas_call(functools.partial(backward_kernel, rep), name='backward',...  113 us
    pallas_call x1, Pallas kernels, forward_call(): pl.pallas_call(functools.partial(forward_kernel, rep), name='forward', in...  106 us
    pallas_call x1, Pallas kernels, update_call(): pl.pallas_call(update_kernel, name='update', in_specs=[hbm] * 26, out_sha...  5.5 us

profile of v4, /device:TPU:0, one launch (start us, length us, event | category | flops | bytes accessed | tf_op | source)
XLA Modules:
  0.0 226.3 jit_solution(3847117402491789753)
XLA Ops:
  0.7 106.5 %forward.1 = (bf16[2,12,2,4,4,32,256]{6,5,4,3,2,1,0:T(8,128)(2,1)}, f32[16,512]{1,0:T(8,128)}, f32[8,512]{1,0:T(8,128)}, f32[2,1280,512]{2,1,0:T(8,128)}, f32[2,...) custom-call(s32[10]{0:T(128)} %steps_ref.1, ...), custom_call_target="tpu_custom_call" | custom-call | tf_op jit(solution)/shard_map/forward/pallas_call | solution.py:507
  107.2 113.4 %backward.1 = (bf16[1280,512]{1,0:T(8,128)(2,1)}, f32[2,13,32,256]{3,2,1,0:T(8,128)}, f32[2,16,512]{2,1,0:T(8,128)}, f32[2,16,512]{2,1,0:T(8,128)}) custom-call(f32[10]{0:T(128)} %scale_ref.1, f32[16,512]{1,0:T(8,128)} %get-tuple-element.63.small_ref, f32[8,512]{1,0:T(8,128)} %get-tuple-element.64.feats_ref, bf16[1280,512]{1,0:T(8,128)(2,1)} %cot_ref.1, ...), custom_call_target="tpu_custom_call" | custom-call | tf_op jit(solution)/shard_map/backward/pallas_call | solution.py:914
  220.6 5.5 %update.1 = (bf16[1280,512]{1,0:T(8,128)(2,1)}, bf16[1280,512]{1,0:T(8,128)(2,1)}, f32[2,3,32,256]{3,2,1,0:T(8,128)}, f32[2,3,32,256]{3,2,1,0:T(8,128)}, f32[2,3...) custom-call(f32[2,13,32,256]{3,2,1,0:T(8,128)} %get-tuple-element.73, ...), custom_call_target="tpu_custom_call" | custom-call | tf_op jit(solution)/shard_map/update/pallas_call | solution.py:1037

commit v5 on v4

--- a/solution.py
+++ b/solution.py
@@ -163,20 +163,19 @@
         self.along = 0.0
         self.count = 0
 
-    def push(self, piece, dues):
-        for number, due in enumerate(dues, 1):
-            turn = self.count + (number - 1) * LAG
-            self.queue.append((turn, number if FIRST else -number, due, number, piece))
-        self.queue.sort(key=lambda event: event[:2])
+    def push(self, piece, dues, turns):
+        for number, (due, turn) in enumerate(zip(dues, turns), 1):
+            self.queue.append((self.count + turn, due, number, piece))
+        self.queue.sort(key=lambda event: event[0])
         self.count += 1
 
     def gather(self, piece, unit):
         self.along += 4 * unit
-        arrived = self.along + WAIT
+        arrived = self.along + GATHER_WAIT
         begun = max(self.links, arrived)
         self.links = begun + 6 * unit
-        columns, diagonal = begun + 4 * unit + WAIT, begun + 8 * unit + WAIT
-        self.push(piece, [max(arrived, begun - LEAD), columns, diagonal, diagonal + 1.6 * unit + WAIT])
+        columns, diagonal = begun + 4 * unit + GATHER_WAIT, begun + 6 * unit + GATHER_WAIT
+        self.push(piece, [max(arrived, begun - LEAD), columns, diagonal, diagonal + 1.6 * unit + GATHER_WAIT], GATHER_TURNS)
 
     def scatter(self, piece, unit):
         added = self.now + 1.6 * unit + WAIT
@@ -184,18 +183,18 @@
         self.links = begun + 6 * unit
         summed = begun + 8 * unit + WAIT
         self.along = max(self.along, summed) + 4 * unit
-        self.push(piece, [max(added, begun - LEAD), begun + 4 * unit + WAIT, summed, self.along + WAIT])
+        self.push(piece, [max(added, begun - LEAD), begun + 4 * unit + WAIT, summed, self.along + WAIT], SCATTER_TURNS)
 
     def small(self, piece):
-        self.push(piece, [self.now + 3.0 * number for number in (1, 2, 3, 4)])
+        self.push(piece, [self.now + 3.0 * number for number in (1, 2, 3, 4)], SCATTER_TURNS)
 
     def take(self, count):
         ready, self.queue = self.queue[:count], self.queue[count:]
-        return [(piece, number) for _, _, _, number, piece in ready]
+        return [(piece, number) for _, _, number, piece in ready]
 
     def slot(self, length):
         count = 0
-        while count < len(self.queue) and self.queue[count][2] <= self.now:
+        while count < len(self.queue) and self.queue[count][1] <= self.now:
             count += 1
         self.now += length + COST * count
         return self.take(count)
@@ -204,15 +203,16 @@
         self.now += length
 
     def force(self, *wanted):
-        count = max([i + 1 for i, event in enumerate(self.queue) if (event[4], event[3]) in wanted], default=0)
-        self.now = max([self.now] + [event[2] for event in self.queue[:count]])
+        count = max([i + 1 for i, event in enumerate(self.queue) if (event[3], event[2]) in wanted], default=0)
+        self.now = max([self.now] + [event[1] for event in self.queue[:count]])
         return self.take(count)
 
 
 WAIT = 5.0
+GATHER_WAIT = 3.0
 LEAD = 2.0
-LAG = 2
-FIRST = True
+GATHER_TURNS = (-1.9, 0.0, 1.05, 2.3)
+SCATTER_TURNS = (0.0, 2.1, 4.2, 6.3)
 COST = 0.2
 UNIT = 0.33
 
@@ -302,18 +302,15 @@
     own_feed(1)
     for entry in rest:
         entry.step(0)
-    for number in (1, 2, 3):
-        for entry in opening:
-            entry.step(number)
-
+    sizes = {norm_piece: 0.25, bias_piece: 0.25}
+    for layer in range(LAYERS):
+        sizes[time_pieces[layer]] = 2
+        sizes.update((entry, span[1]) for entry, span in zip(layer_pieces[layer], spans))
     times = Timeline()
-    times.along, times.links = 6.0, 1.0
-    for entry in rest:
-        count = 0.25 if entry is bias_piece else 2 if entry is time_pieces[1] else None
-        if count is None:
-            count = [span[1] for layer in layer_pieces for one, span in zip(layer, spans) if one is entry][0]
-        times.gather(entry, UNIT * count)
-    times.now = 4.0
+    for entry in opening + rest:
+        times.gather(entry, UNIT * sizes[entry])
+    wanted = [(entry, 4) for entry in opening]
+    play(times.force(*[(entry, 3) for entry in opening]))
 
     line = lax.broadcasted_iota(jnp.int32, (8, 256), 0)
     column = lax.broadcasted_iota(jnp.int32, (8, 256), 1).astype(F32)
@@ -329,8 +326,7 @@
     feats_high = feats.astype(BF16)
     feats_low = (feats - feats_high.astype(F32)).astype(BF16)
 
-    for entry in opening:
-        entry.step(4)
+    play(times.force(*wanted))
     for zz in range(4):
         total = jnp.zeros((16, 128), F32)
         for part in range(8):

time: 227 us -> 212 us (0.934)
  Pallas kernels: 225 us -> 211 us
    pallas_call x1, Pallas kernels: 106 us -> 94.8 us  [forward_call(): pl.pallas_call(functools.partial(forward_kernel, rep), name='forward', in...]
    pallas_call x1, Pallas kernels: 113 us -> 111 us  [backward_call(): pl.pallas_call(functools.partial(backward_kernel, rep), name='backward',...]
where the time goes in v5:
time: 212 us
  Pallas kernels  211 us (100%)
    pallas_call x1, Pallas kernels, backward_call(): pl.pallas_call(functools.partial(backward_kernel, rep), name='backward',...  111 us
    pallas_call x1, Pallas kernels, forward_call(): pl.pallas_call(functools.partial(forward_kernel, rep), name='forward', in...  94.8 us
    pallas_call x1, Pallas kernels, update_call(): pl.pallas_call(update_kernel, name='update', in_specs=[hbm] * 26, out_sha...  5.5 us

profile of v5, /device:TPU:0, one launch (start us, length us, event | category | flops | bytes accessed | tf_op | source)
XLA Modules:
  0.0 212.2 jit_solution(5468142415588401025)
XLA Ops:
  0.7 94.8 %forward.1 = (bf16[2,12,2,4,4,32,256]{6,5,4,3,2,1,0:T(8,128)(2,1)}, f32[16,512]{1,0:T(8,128)}, f32[8,512]{1,0:T(8,128)}, f32[2,1280,512]{2,1,0:T(8,128)}, f32[2,...) custom-call(s32[10]{0:T(128)} %steps_ref.1, ...), custom_call_target="tpu_custom_call" | custom-call | tf_op jit(solution)/shard_map/forward/pallas_call | solution.py:503
  95.5 111.0 %backward.1 = (bf16[1280,512]{1,0:T(8,128)(2,1)}, f32[2,13,32,256]{3,2,1,0:T(8,128)}, f32[2,16,512]{2,1,0:T(8,128)}, f32[2,16,512]{2,1,0:T(8,128)}) custom-call(f32[10]{0:T(128)} %scale_ref.1, f32[16,512]{1,0:T(8,128)} %get-tuple-element.63.small_ref, f32[8,512]{1,0:T(8,128)} %get-tuple-element.64.feats_ref, bf16[1280,512]{1,0:T(8,128)(2,1)} %cot_ref.1, ...), custom_call_target="tpu_custom_call" | custom-call | tf_op jit(solution)/shard_map/backward/pallas_call | solution.py:910
  206.5 5.5 %update.1 = (bf16[1280,512]{1,0:T(8,128)(2,1)}, bf16[1280,512]{1,0:T(8,128)(2,1)}, f32[2,3,32,256]{3,2,1,0:T(8,128)}, f32[2,3,32,256]{3,2,1,0:T(8,128)}, f32[2,3...) custom-call(f32[2,13,32,256]{3,2,1,0:T(8,128)} %get-tuple-element.73, ...), custom_call_target="tpu_custom_call" | custom-call | tf_op jit(solution)/shard_map/update/pallas_call | solution.py:1033

commit v6 on v5

--- a/solution.py
+++ b/solution.py
@@ -212,7 +212,7 @@
 GATHER_WAIT = 3.0
 LEAD = 2.0
 GATHER_TURNS = (-1.9, 0.0, 1.05, 2.3)
-SCATTER_TURNS = (0.0, 2.1, 4.2, 6.3)
+SCATTER_TURNS = (0.0, 1.1, 3.2, 5.3)
 COST = 0.2
 UNIT = 0.33
 
@@ -227,7 +227,7 @@
                     pl.when(item == number)(functools.partial(play, events[half]))
 
         poll(0)
-        body(item, lambda: poll(1), *blocks)
+        body(item, poll, *blocks)
 
     pltpu.emit_pipeline(whole, grid=(count,), in_specs=in_specs, out_specs=out_specs)(*refs)
 
@@ -398,7 +398,7 @@
                 attn[here, span] = joined
 
         each_item(
-            body, [(times.slot(ATTENTION), []) for _ in range(items)], items,
+            body, [(times.slot(ATTENTION),) for _ in range(items)], items,
             [wide(512)] if layer == 0 else [],
             [wide(512), wide(1536), pl.BlockSpec((1, 8, 256, 256), lambda i: (i, 0, 0, 0)), wide(512)],
             ([x_ref] if layer == 0 else [])
@@ -483,7 +483,7 @@
 
 
 ATTENTION, MIDDLE, FEED = 2.2, 0.8, 2.4
-FEED_BACK, ATTENTION_BACK, GRAD = 2.1, 2.7, 0.76
+FEED_BACK, ATTENTION_BACK, GRAD = 1.9, 2.7, 0.76
 
 
 class Start:
@@ -710,14 +710,23 @@
             acc[4] += fold_rows(grad)
             low = grad.astype(BF16)
             gdt[:, here] = low.T
-            back = jnp.zeros((LENGTH, 512), F32)
+            lift = lambda part: nn(low, weight(w, 5 + 2 * part))
+            lower = lambda part, value: nt(value, weight(w, 4 + 2 * part))
+            back, ahead, held = jnp.zeros((LENGTH, 512), F32), lift(0), None
             for part in range(4):
                 span = slice(part * 512, (part + 1) * 512)
-                dh = nn(low, weight(w, 5 + 2 * part))
+                dh = ahead
+                if part == 2:
+                    poll(1)
+                if part < 3:
+                    ahead = lift(part + 1)
                 pre_grad = (dh * slope_blk[:, span].astype(F32)).astype(BF16)
                 du[here, span] = pre_grad
                 acc_bias[part] += fold_rows(pre_grad.astype(F32))
-                back = back + nt(pre_grad, weight(w, 4 + 2 * part))
+                if held is not None:
+                    back = back + lower(part - 1, held)
+                held = pre_grad
+            back = back + lower(3, held)
             hat, inverse = normalize(middle_blk[...])
             normed = hat * small_ref[layer * 5 + 2 : layer * 5 + 3] + small_ref[layer * 5 + 3 : layer * 5 + 4]
             n2t[:, here] = normed.astype(BF16).T
@@ -728,7 +737,7 @@
             dattn[here] = nn(low, weight(w, 3)).astype(BF16)
 
         each_item(
-            body, [(times.slot(FEED_BACK), []) for _ in range(items)], items, [wide(512), wide(2048)] + ([wide(512)] if last else []), [],
+            body, [[times.slot(FEED_BACK / 2) for _ in range(2)] for _ in range(items)], items, [wide(512), wide(2048)] + ([wide(512)] if last else []), [],
             [middle_in.at[layer], slope_in.at[layer]] + ([cot_ref] if last else []),
         )
 
@@ -760,8 +769,8 @@
             ahead, held = scores(0), None
             for pair in range(4):
                 both = ahead
-                if pair == 2:
-                    poll()
+                if pair > 0:
+                    poll(pair)
                 if pair < 3:
                     ahead = scores(pair + 1)
                 dscores = []
@@ -786,7 +795,7 @@
             else:
                 gx[here] = grad
 
-        slots = [(times.slot(ATTENTION_BACK / 2), times.slot(ATTENTION_BACK / 2)) for _ in range(items)]
+        slots = [[times.slot(ATTENTION_BACK / 4) for _ in range(4)] for _ in range(items)]
         each_item(
             body, slots, items,
             [wide(512), wide(1536), pl.BlockSpec((1, 8, 256, 256), lambda i: (i, 0, 0, 0))],

time: 212 us -> 210 us (level)
    pallas_call x1, Pallas kernels: 111 us -> 108 us  [backward_call(): pl.pallas_call(functools.partial(backward_kernel, rep), name='backward',...]
where the time goes in v6:
time: 210 us; the launch traced here: 209 us
  Pallas kernels  209 us (100%)
    pallas_call x1, Pallas kernels, backward_call(): pl.pallas_call(functools.partial(backward_kernel, rep), name='backward',...  108 us
    pallas_call x1, Pallas kernels, forward_call(): pl.pallas_call(functools.partial(forward_kernel, rep), name='forward', in...  94.8 us
    pallas_call x1, Pallas kernels, update_call(): pl.pallas_call(update_kernel, name='update', in_specs=[hbm] * 26, out_sha...  5.5 us

profile of v6, /device:TPU:0, one launch (start us, length us, event | category | flops | bytes accessed | tf_op | source)
XLA Modules:
  0.0 209.4 jit_solution(14502003199199463171)
XLA Ops:
  0.7 94.8 %forward.1 = (bf16[2,12,2,4,4,32,256]{6,5,4,3,2,1,0:T(8,128)(2,1)}, f32[16,512]{1,0:T(8,128)}, f32[8,512]{1,0:T(8,128)}, f32[2,1280,512]{2,1,0:T(8,128)}, f32[2,...) custom-call(s32[10]{0:T(128)} %steps_ref.1, ...), custom_call_target="tpu_custom_call" | custom-call | tf_op jit(solution)/shard_map/forward/pallas_call | solution.py:503
  95.5 108.2 %backward.1 = (bf16[1280,512]{1,0:T(8,128)(2,1)}, f32[2,13,32,256]{3,2,1,0:T(8,128)}, f32[2,16,512]{2,1,0:T(8,128)}, f32[2,16,512]{2,1,0:T(8,128)}) custom-call(f32[10]{0:T(128)} %scale_ref.1, f32[16,512]{1,0:T(8,128)} %get-tuple-element.63.small_ref, f32[8,512]{1,0:T(8,128)} %get-tuple-element.64.feats_ref, bf16[1280,512]{1,0:T(8,128)(2,1)} %cot_ref.1, ...), custom_call_target="tpu_custom_call" | custom-call | tf_op jit(solution)/shard_map/backward/pallas_call | solution.py:919
  203.7 5.5 %update.1 = (bf16[1280,512]{1,0:T(8,128)(2,1)}, bf16[1280,512]{1,0:T(8,128)(2,1)}, f32[2,3,32,256]{3,2,1,0:T(8,128)}, f32[2,3,32,256]{3,2,1,0:T(8,128)}, f32[2,3...) custom-call(f32[2,13,32,256]{3,2,1,0:T(8,128)} %get-tuple-element.73, ...), custom_call_target="tpu_custom_call" | custom-call | tf_op jit(solution)/shard_map/update/pallas_call | solution.py:1042

commit v7 on v6

--- a/solution.py
+++ b/solution.py
@@ -976,13 +976,16 @@
 
 def update_kernel(*refs):
     hbm, outs, ins = refs[:26], refs[26:50], refs[50:74]
-    row, sems = refs[74:]
+    row, *passing, sems = refs[74:]
     copies = [pltpu.make_async_copy(src, dst, sems.at[i]) for i, (src, dst) in enumerate(zip(hbm[:24], ins))]
-    copies += [pltpu.make_async_copy(hbm[24 + i], outs[i], sems.at[24 + i]) for i in range(2)]
+    copies += [pltpu.make_async_copy(hbm[24 + i], passing[i], sems.at[24 + i]) for i in range(2)]
+    leaving = [pltpu.make_async_copy(passing[i], outs[i], sems.at[26 + i]) for i in range(2)]
     for copy in copies:
         copy.start()
-    for copy in copies[:24]:
+    for copy in copies:
         copy.wait()
+    for copy in leaving:
+        copy.start()
     total, sums, time_grad, *ins = ins
     outs = outs[2:]
     qkv, out, up, bias, down, norm, time = [ins[i * 3 : i * 3 + 3] for i in range(7)]
@@ -1024,7 +1027,7 @@
         width = bias[0].shape[2]
         mine = pltpu.roll(row[...], (128 - dp * width) % 128, 1)[:, 0:width]
         one(bias, bias_new, (layer,), mine, learn_rate)
-    for copy in copies[24:]:
+    for copy in leaving:
         copy.wait()
 
 
@@ -1044,9 +1047,11 @@
         name="update",
         in_specs=[hbm] * 26,
         out_shape=shapes,
-        out_specs=[vmem] * 24,
+        out_specs=[hbm] * 2 + [vmem] * 22,
         scratch_shapes=[pltpu.VMEM(array.shape, F32) for array in flat]
-        + [pltpu.VMEM((8, 128), F32), pltpu.SemaphoreType.DMA((26,))],
+        + [pltpu.VMEM((8, 128), F32)]
+        + [pltpu.VMEM(array.shape, array.dtype) for array in row_results]
+        + [pltpu.SemaphoreType.DMA((28,))],
         compiler_params=pltpu.CompilerParams(vmem_limit_bytes=56 << 20),
     )(*flat, *row_results)
 

time: 210 us -> 210 us (level)
  no operation moved by 1% of the time
where the time goes in v7:
time: 210 us
  Pallas kernels  209 us (100%)
    pallas_call x1, Pallas kernels, backward_call(): pl.pallas_call(functools.partial(backward_kernel, rep), name='backward',...  108 us
    pallas_call x1, Pallas kernels, forward_call(): pl.pallas_call(functools.partial(forward_kernel, rep), name='forward', in...  94.8 us
    pallas_call x1, Pallas kernels, update_call(): pl.pallas_call(update_kernel, name='update', in_specs=[hbm] * 26, out_sha...  6.16 us

profile of v7, /device:TPU:0, one launch (start us, length us, event | category | flops | bytes accessed | tf_op | source)
XLA Modules:
  0.0 210.0 jit_solution(8845157424773297751)
XLA Ops:
  0.7 94.8 %forward.1 = (bf16[2,12,2,4,4,32,256]{6,5,4,3,2,1,0:T(8,128)(2,1)}, f32[16,512]{1,0:T(8,128)}, f32[8,512]{1,0:T(8,128)}, f32[2,1280,512]{2,1,0:T(8,128)}, f32[2,...) custom-call(s32[10]{0:T(128)} %steps_ref.1, ...), custom_call_target="tpu_custom_call" | custom-call | tf_op jit(solution)/shard_map/forward/pallas_call | solution.py:503
  95.5 108.2 %backward.1 = (bf16[1280,512]{1,0:T(8,128)(2,1)}, f32[2,13,32,256]{3,2,1,0:T(8,128)}, f32[2,16,512]{2,1,0:T(8,128)}, f32[2,16,512]{2,1,0:T(8,128)}) custom-call(f32[10]{0:T(128)} %scale_ref.1, f32[16,512]{1,0:T(8,128)} %get-tuple-element.63.small_ref, f32[8,512]{1,0:T(8,128)} %get-tuple-element.64.feats_ref, bf16[1280,512]{1,0:T(8,128)(2,1)} %cot_ref.1, ...), custom_call_target="tpu_custom_call" | custom-call | tf_op jit(solution)/shard_map/backward/pallas_call | solution.py:919
  203.7 6.2 %update.1 = (bf16[1280,512]{1,0:T(8,128)(2,1)}, bf16[1280,512]{1,0:T(8,128)(2,1)}, f32[2,3,32,256]{3,2,1,0:T(8,128)}, f32[2,3,32,256]{3,2,1,0:T(8,128)}, f32[2,3...) custom-call(f32[2,13,32,256]{3,2,1,0:T(8,128)} %get-tuple-element.73, ...), custom_call_target="tpu_custom_call" | custom-call | tf_op jit(solution)/shard_map/update/pallas_call | solution.py:1045
